TPU v7x, 32 devices: a whole 2x2x4 slice. The times are simulated.
32 devices in a mesh: grp: 2 (over x), blk: 16 (over z, y, core).
Axes of the slice: x: 2, y: 2, z: 4, core: 2. Of those that a mesh axis runs over, the one named last changes fastest.
Arguments:
- activations: bfloat16 [6144, 14336], P(('grp', 'blk')), parts along dimension 0, may hold values from -6 to 6
- errors: bfloat16 [6144, 4096], P(('grp', 'blk')), parts along dimension 0, may hold values from -6 to 6
- err_factors: bfloat16 [16, 13, 4096], P('blk'), may hold values from -0.09375 to 0.09375
- act_factors: bfloat16 [16, 13, 14336], P('blk'), may hold values from -0.046875 to 0.046875
Outputs:
- scores: float32 [16, 6144], P(None, ('grp', 'blk')), parts along dimension 1
There are 2 independent parts, one for each index of `grp`. A program takes and returns all parts, laid end to end along the dimension named above; an argument that names none is the same for every part. Nothing has to cross between parts.
All inputs are finite; a program needn't handle non-finite values.
Results may differ from a plain program's by a relative error of at most 0.0003.
Values may be sent and summed in bfloat16 or wider, within the bound.
No kernel may reach another device: no remote copies, remote signals or barrier semaphores. Data moves between devices by JAX's collectives and lax.ppermute only.
A program may use at most 192 MiB of HBM per device.

v0:
```python
import jax
import jax.numpy as jnp
from jax import lax
from jax.sharding import PartitionSpec as P


def project_rows(err_rows, act_rows, err_piece, act_piece):
    err_proj = jnp.einsum("td,qrd->qrt", err_rows, err_piece, preferred_element_type=jnp.float32)
    act_proj = jnp.einsum("tf,qrf->qrt", act_rows, act_piece, preferred_element_type=jnp.float32)
    return (err_proj, act_proj)


def local(activations, errors, err_factors, act_factors):
    err_width = errors.shape[1]
    joined = jnp.concatenate((err_factors, act_factors), axis=2)
    piece = lax.all_gather(joined, "blk", axis=0, tiled=True)
    err_proj, act_proj = project_rows(
        errors, activations, piece[:, :, :err_width], piece[:, :, err_width:]
    )
    return jnp.sum(err_proj * act_proj, axis=1)


def solution(mesh):
    in_specs = (
        P(("grp", "blk"), None),
        P(("grp", "blk"), None),
        P("blk", None, None),
        P("blk", None, None),
    )
    out_specs = P(None, ("grp", "blk"))
    return jax.shard_map(local, mesh=mesh, in_specs=in_specs, out_specs=out_specs, check_vma=False)
```

profile of v0, /device:TPU:1, one launch (start us, length us, event | category | flops | bytes accessed | tf_op | source)
XLA Modules:
  0.0 113.8 jit_solution(10886809538433093535)
XLA Ops:
  6.5 0.0 copy-start
  6.5 0.0 all-gather.2.cloned.1.call-start
  6.5 2.0 %pad_maximum_fusion = bf16[1,13,18432]{2,1,0:T(8,128)(2,1)} fusion(bf16[1,13,14336]{2,1,0:T(8,128)(2,1)} %param.7, bf16[1,13,4096]{2,1,0:T(8,128)(2,1)} %param.6), kind=kLoop, calls=%fused_computation.8 | loop fusion | flops 958464 | bytes 958464 | tf_op jit(solution)/shard_map/concatenate | solution.py:15
  8.6 0.0 all-gather.2.cloned.1.call-update
  8.6 85.0 %all-gather.2.cloned.1.call-done = bf16[16,13,18432]{2,1,0:T(8,128)(2,1)} async-done(((bf16[1,13,18432]{2,1,0:T(8,128)(2,1)}), bf16[16,13,18432]{2,1,0:T(8,128)(2,1)}) %all-gather.2.cloned.1.call-update) | async-done | bytes 7667728 | tf_op jit(solution)/shard_map/all_gather | solution.py:16
  93.6 0.0 slice-start
  93.6 3.1 %slice-done = bf16[16,13,14336]{2,1,0:T(8,128)(2,1)S(1)} async-done(((bf16[16,13,18432]{2,1,0:T(8,128)(2,1)}), bf16[16,13,14336]{2,1,0:T(8,128)(2,1)S(1)}, s32[]{:S(2)}) %slice-start) | async-done | bytes 5963800 | tf_op jit(solution)/shard_map/slice | solution.py:18
  96.7 6.7 %fusion = f32[16,13,192]{2,0,1:T(8,128)S(1)} fusion(bf16[16,13,14336]{2,1,0:T(8,128)(2,1)S(1)} %slice-done, bf16[192,14336]{1,0:T(8,128)(2,1)} %param.4), kind=kOutput, calls=%fused_computation | convolution fusion | flops 1145044992 | bytes 11628544 | tf_op jit(solution)/shard_map/tf,qrf->qrt/dot_general | solution.py:9
  103.4 0.0 slice-start.1
  103.4 0.0 copy-done
  103.5 1.6 %slice-done.1 = bf16[16,13,4096]{2,1,0:T(8,128)(2,1)S(1)} async-done(((bf16[16,13,18432]{2,1,0:T(8,128)(2,1)}), bf16[16,13,4096]{2,1,0:T(8,128)(2,1)S(1)}, s32[]{:S(2)}) %slice-start.1) | async-done | bytes 1703960 | tf_op jit(solution)/shard_map/slice | solution.py:18
  105.0 1.9 %fusion.11 = f32[16,192]{1,0:T(8,128)} fusion(f32[16,13,192]{2,0,1:T(8,128)S(1)} %fusion, bf16[192,4096]{1,0:T(8,128)(2,1)S(1)} %copy-done, bf16[16,13,4096]{2,1,0:T(8,128)(2,1)S(1)} %slice-done.1), kind=kOutput, calls=%fused_computation.7 | convolution fusion | flops 327232512 | bytes 3448832 | tf_op jit(solution)/shard_map/td,qrd->qrt/dot_general | solution.py:8
Async XLA Ops:
  6.5 96.9 %copy-start = (bf16[192,4096]{1,0:T(8,128)(2,1)S(1)}, bf16[192,4096]{1,0:T(8,128)(2,1)}, u32[]{:S(2)}) copy-start(bf16[192,4096]{1,0:T(8,128)(2,1)} %param.5) | copy-start | bytes 4718596
  6.5 87.1 %all-gather.2.cloned.1.call-start = ((), (), s32[]{:S(2)}) async-start(), calls=%async_computation | async-start | bytes 10027008 | tf_op jit(solution)/shard_map/all_gather | solution.py:16
  93.6 3.1 %slice-start = ((bf16[16,13,18432]{2,1,0:T(8,128)(2,1)}), bf16[16,13,14336]{2,1,0:T(8,128)(2,1)S(1)}, s32[]{:S(2)}) async-start(bf16[16,13,18432]{2,1,0:T(8,128)(2,1)} %all-gather.2.cloned.1.call-done), calls=%async_computation.1 | async-start | bytes 14680064 | tf_op jit(solution)/shard_map/slice | solution.py:18
  103.4 1.6 %slice-start.1 = ((bf16[16,13,18432]{2,1,0:T(8,128)(2,1)}), bf16[16,13,4096]{2,1,0:T(8,128)(2,1)S(1)}, s32[]{:S(2)}) async-start(bf16[16,13,18432]{2,1,0:T(8,128)(2,1)} %all-gather.2.cloned.1.call-done), calls=%async_computation.2 | async-start | bytes 4194304 | tf_op jit(solution)/shard_map/slice | solution.py:18
Sparse Core Ops, SparseCore 0:
  9.6 83.9 all-gather.1
where the time goes:
time: 114 us
  waiting for transfers between devices  85 us (75%)
  between operations  13.4 us (12%)
  matrix products  8.61 us (8%)
  local copies, waits for them, and re-layouts  4.66 us (4%)
  other arithmetic  2.03 us (2%)
    all_gather x1, waiting for transfers between devices, local(): piece = lax.all_gather(joined, 'blk', axis=0, tiled=True)  85 us
    dot_general x1, matrix products, project_rows(): jnp.einsum('tf,qrf->qrt', act_rows, act_piece, preferred_element_type=jnp...  6.72 us
    slice x2, local copies, waits for them, and re-layouts, local(): piece[:, :, err_width:]  3.08 us
  transfers between devices with their start and end apart: 1, of which 1 were waited for; matrix products, arithmetic and copies ran while one was open for 0% of the time, Pallas kernels for 0%

commit v1 on v0

v1 whole, which is shorter than its diff:
```python
import functools

import jax
import jax.numpy as jnp
from jax import lax
from jax.experimental import pallas as pl
from jax.experimental.pallas import tpu as pltpu
from jax.sharding import PartitionSpec as P

AXES = ("grp", "blk")
NT = (((1,), (1,)), ((), ()))
SEGS = 16
ROWS = 16
TILES = 13
STEPS = 8


def project_rows(err_rows, act_rows, err_piece, act_piece):
    err_proj = jnp.einsum("td,qrd->qrt", err_rows, err_piece, preferred_element_type=jnp.float32)
    act_proj = jnp.einsum("tf,qrf->qrt", act_rows, act_piece, preferred_element_type=jnp.float32)
    return (err_proj, act_proj)


def gathered(activations, errors, err_factors, act_factors):
    err_width = errors.shape[1]
    joined = jnp.concatenate((err_factors, act_factors), axis=2)
    piece = lax.all_gather(joined, "blk", axis=0, tiled=True)
    err_proj, act_proj = project_rows(
        errors, activations, piece[:, :, :err_width], piece[:, :, err_width:]
    )
    return jnp.sum(err_proj * act_proj, axis=1)


def place(g):
    tile, row = lax.div(g, ROWS), lax.rem(g, ROWS)
    return jnp.where(row < TILES, g, ROWS * row + tile)


def packed_row(local, half, first):
    return jnp.where(local < half, local + half * first, local - half + half * (1 - first))


def pack_kernel(x_ref, err_ref, act_ref, half_ref, both_ref, runs):
    rank, err_width = err_ref.shape[1], err_ref.shape[2]
    ew, aw = err_width // SEGS, act_ref.shape[2] // SEGS
    runs[...] = jnp.zeros_like(runs)
    for s in range(SEGS):
        runs[s * ROWS : s * ROWS + rank, :ew] = err_ref[0, :, s * ew : (s + 1) * ew]
        runs[s * ROWS : s * ROWS + rank, ew:] = act_ref[0, :, s * aw : (s + 1) * aw]
    rows = both_ref.shape[0]
    shape = (rows, SEGS * ROWS)
    local = lax.broadcasted_iota(jnp.int32, shape, 0)
    source = place(packed_row(local, rows // 2, x_ref[0]))
    pick = (source == lax.broadcasted_iota(jnp.int32, shape, 1)).astype(jnp.bfloat16)
    packed = jnp.dot(pick, runs[...], preferred_element_type=jnp.float32).astype(jnp.bfloat16)
    both_ref[...] = packed
    half_ref[...] = packed[: rows // 2]


def pack(x, err, act):
    rank = err.shape[1]
    width = (err.shape[2] + act.shape[2]) // SEGS
    rows = TILES * ROWS
    vmem = pl.BlockSpec(memory_space=pltpu.VMEM)
    return pl.pallas_call(
        pack_kernel,
        out_shape=(
            jax.ShapeDtypeStruct((rows // 2, width), jnp.bfloat16),
            jax.ShapeDtypeStruct((rows, width), jnp.bfloat16),
        ),
        in_specs=[pl.BlockSpec(memory_space=pltpu.SMEM), vmem, vmem],
        out_specs=(vmem, vmem),
        scratch_shapes=[pltpu.VMEM((SEGS * ROWS, width), jnp.bfloat16)],
        compiler_params=pltpu.CompilerParams(vmem_limit_bytes=16 << 20),
        name="pack",
    )(x, err, act)


def score_kernel(blocks, n_pieces, x_ref, *refs):
    pieces = refs[:n_pieces]
    eo_ref, ao_ref, ep_ref, ap_ref, own_ref, par_ref, we, wa, eo, ao, ep, ap = refs[n_pieces:]
    step = pl.program_id(0)
    ew, aw = we.shape[1] // SEGS, wa.shape[1] // SEGS

    @pl.when(step == 0)
    def _():
        half = TILES * ROWS // 2
        x = x_ref[0]
        for b, parts in enumerate(blocks):
            total = None
            for i, other in parts:
                rows = pieces[i].shape[0]
                shape = (SEGS * ROWS, rows)
                out = lax.broadcasted_iota(jnp.int32, shape, 0)
                local = lax.broadcasted_iota(jnp.int32, shape, 1)
                source = place(packed_row(local, half, 1 - x if other else x))
                pick = (source == out).astype(jnp.bfloat16)
                term = jnp.dot(pick, pieces[i][...], preferred_element_type=jnp.float32)
                total = term if total is None else total + term
            total = total.astype(jnp.bfloat16)
            for s in range(SEGS):
                run = total[s * ROWS : (s + 1) * ROWS]
                we[b * ROWS : (b + 1) * ROWS, s * ew : (s + 1) * ew] = run[:, :ew]
                wa[b * ROWS : (b + 1) * ROWS, s * aw : (s + 1) * aw] = run[:, ew:]
        for acc in (eo, ao, ep, ap):
            acc[...] = jnp.zeros_like(acc)

    ec, ac = eo_ref.shape[1], ao_ref.shape[1]
    wec = we[:, pl.ds(pl.multiple_of(step * ec, ec), ec)]
    wac = wa[:, pl.ds(pl.multiple_of(step * ac, ac), ac)]
    for acc, w, t in ((eo, wec, eo_ref), (ep, wec, ep_ref), (ao, wac, ao_ref), (ap, wac, ap_ref)):
        acc[...] += lax.dot_general(w, t[...], NT, preferred_element_type=jnp.float32)

    @pl.when(step == STEPS - 1)
    def _():
        for e, a, o in ((eo, ao, own_ref), (ep, ap, par_ref)):
            prod = e[...] * a[...]
            for b in range(len(blocks)):
                o[b : b + 1, :] = jnp.sum(
                    prod[b * ROWS : (b + 1) * ROWS], axis=0, keepdims=True
                )


def score(x, pieces, blocks, tokens):
    errs, acts = tokens[0].shape[1], tokens[1].shape[1]
    t, nb = tokens[0].shape[0], len(blocks)
    ew, aw = errs // STEPS, acts // STEPS
    whole = lambda a: pl.BlockSpec(a.shape, lambda i: (0, 0))
    cut = lambda w: pl.BlockSpec((t, w), lambda i: (0, i))
    acc = pltpu.VMEM((nb * ROWS, t), jnp.float32)
    out = jax.ShapeDtypeStruct((nb, t), jnp.float32)
    return pl.pallas_call(
        functools.partial(score_kernel, blocks, len(pieces)),
        grid=(STEPS,),
        out_shape=(out, out),
        in_specs=[pl.BlockSpec(memory_space=pltpu.SMEM)]
        + [whole(p) for p in pieces]
        + [cut(ew), cut(aw), cut(ew), cut(aw)],
        out_specs=(whole(out), whole(out)),
        scratch_shapes=[
            pltpu.VMEM((nb * ROWS, errs), jnp.bfloat16),
            pltpu.VMEM((nb * ROWS, acts), jnp.bfloat16),
            acc, acc, acc, acc,
        ],
        compiler_params=pltpu.CompilerParams(vmem_limit_bytes=40 << 20),
        cost_estimate=pl.CostEstimate(
            flops=2 * nb * ROWS * 2 * t * (errs + acts),
            bytes_accessed=4 * t * (errs + acts),
            transcendentals=0,
        ),
        name="score",
    )(x, *pieces, *tokens)


def place_kernel(me_ref, *refs):
    out_ref = refs[-1]
    me = me_ref[0]
    row = 0
    for own, par in zip(refs[:-1:2], refs[1:-1:2]):
        for b in range(own.shape[0]):
            q = jnp.bitwise_xor(me, 2 * row)
            out_ref[pl.ds(q, 1), :] = own[b : b + 1, :]
            out_ref[pl.ds(jnp.bitwise_xor(q, 1), 1), :] = par[b : b + 1, :]
            row += 1


def finish(me, rows, queries, t):
    vmem = pl.BlockSpec(memory_space=pltpu.VMEM)
    return pl.pallas_call(
        place_kernel,
        out_shape=jax.ShapeDtypeStruct((queries, t), jnp.float32),
        in_specs=[pl.BlockSpec(memory_space=pltpu.SMEM)] + [vmem] * len(rows),
        out_specs=vmem,
        name="place",
    )(me, *rows)


def pairs(n_grp, n_blk, flip_grp, flip_blk):
    return [
        (g * n_blk + b, (g ^ flip_grp) * n_blk + (b ^ flip_blk))
        for g in range(n_grp)
        for b in range(n_blk)
    ]


def permuted(n_grp, n_blk, activations, errors, err_factors, act_factors):
    swap = lambda a, gx, bx: lax.ppermute(a, AXES, pairs(n_grp, n_blk, gx, bx))
    over_x = lambda a: swap(a, 1, 0)
    over_y = lambda a: swap(a, 0, 2)
    over_z = lambda a, k: swap(a, 0, 4 * k)
    mate = lambda a: swap(a, 0, 1)
    x = lax.axis_index("grp").astype(jnp.int32).reshape(1)
    me = lax.axis_index("blk").astype(jnp.int32).reshape(1)

    half, both = pack(x, err_factors, act_factors)
    z2, z3 = over_z(half, 2), over_z(half, 3)
    z1 = over_z(both, 1)
    y0 = over_y(both)
    tokens = (errors, activations, mate(errors), mate(activations))
    y2, xa2 = over_y(z2), over_x(z2)
    xb2 = over_x(y2)
    y3, xa3 = over_y(z3), over_x(z3)
    y1 = over_y(z1)
    xb3 = over_x(y3)

    full = lambda i: ((i, False),)
    split = lambda i: ((i, False), (i + 1, True))
    o0, p0 = score(x, (both, y0, z1, y1), tuple(full(i) for i in range(4)), tokens)
    o2, p2 = score(x, (z2, xa2, y2, xb2), (split(0), split(2)), tokens)
    o3, p3 = score(x, (z3, xa3, y3, xb3), (split(0), split(2)), tokens)
    rows = (o0, mate(p0), o2, mate(p2), o3, mate(p3))
    return finish(me, rows, n_blk, errors.shape[0])


def solution(mesh):
    in_specs = (
        P(("grp", "blk"), None),
        P(("grp", "blk"), None),
        P("blk", None, None),
        P("blk", None, None),
    )
    out_specs = P(None, ("grp", "blk"))
    n_grp, n_blk = mesh.shape["grp"], mesh.shape["blk"]
    body = gathered
    if (n_grp, n_blk) == (2, 16):
        body = functools.partial(permuted, n_grp, n_blk)
    return jax.shard_map(body, mesh=mesh, in_specs=in_specs, out_specs=out_specs, check_vma=False)
```

time: 114 us -> 84.5 us (0.74)
  the two profiles are of different devices: /device:TPU:1 before, /device:TPU:21 now
where the time goes in v1:
time: 84.5 us; the launch traced here: 83.8 us
  Pallas kernels  29 us (34%)
  waiting for transfers between devices  26.1 us (31%)
  starting transfers between devices  20.9 us (25%)
  local copies, waits for them, and re-layouts  7.64 us (9%)
    pallas_call x3, Pallas kernels, score(): pl.pallas_call(functools.partial(score_kernel, blocks, len(pieces)), grid...  27.3 us
    ppermute x16, waiting for transfers between devices, permuted(): swap = lambda a, gx, bx: lax.ppermute(a, AXES, pairs(n_grp, n_blk, gx, bx))  26.1 us
    ppermute x16, starting transfers between devices, permuted(): swap = lambda a, gx, bx: lax.ppermute(a, AXES, pairs(n_grp, n_blk, gx, bx))  20.9 us
    unnamed x24, local copies, waits for them, and re-layouts  7.64 us
  transfers between devices with their start and end apart: 16, of which 6 were waited for; matrix products, arithmetic and copies ran while one was open for 0% of the time, Pallas kernels for 33%

profile of v1, /device:TPU:21, one launch (start us, length us, event | category | flops | bytes accessed | tf_op | source)
XLA Modules:
  0.0 83.8 jit_solution(8511639778751586993)
XLA Ops:
  0.0 0.7 collective-permute-start.4
  0.7 0.0 collective-permute-start.3
  0.7 0.0 copy-start.4
  0.7 1.0 %copy-done.4 = bf16[1,13,14336]{2,1,0:T(8,128)(2,1)S(1)} copy-done((bf16[1,13,14336]{2,1,0:T(8,128)(2,1)S(1)}, bf16[1,13,14336]{2,1,0:T(8,128)(2,1)}, u32[]{:S(2)}) %copy-start.4) | copy-done | bytes 372760
  1.7 0.0 copy-start.5
  1.7 0.9 %copy-done.5 = bf16[1,13,4096]{2,1,0:T(8,128)(2,1)S(1)} copy-done((bf16[1,13,4096]{2,1,0:T(8,128)(2,1)S(1)}, bf16[1,13,4096]{2,1,0:T(8,128)(2,1)}, u32[]{:S(2)}) %copy-start.5) | copy-done | bytes 106520
  2.6 0.4 pack.1
  3.0 0.2 collective-permute-start.11
  3.2 3.2 %collective-permute-start.6 = (bf16[104,1152]{1,0:T(8,128)(2,1)S(1)}, bf16[104,1152]{1,0:T(8,128)(2,1)S(1)}, u32[]{:S(2)}, u32[]{:S(2)}) collective-permute-start(bf16[104,1152]{1,0:T(8,128)(2,1)S(1)} %get-tuple-element.16), channel_id=1, source_target_pairs={{0,8},{1,9},{2,10},{3,11},{4,12},{5,13},{6,14},{7,15},{8,0},{9,1},... | collective-permute-start | bytes 718856 | tf_op jit(solution)/shard_map/ppermute | solution.py:187
  6.4 0.0 collective-permute-start.1
  6.5 13.8 %collective-permute-done.11.refs_0_ = bf16[104,1152]{1,0:T(8,128)(2,1)S(1)} collective-permute-done((bf16[104,1152]{1,0:T(8,128)(2,1)S(1)}, bf16[104,1152]{1,0:T(8,128)(2,1)S(1)}, u32[]{:S(2)}, u32[]{:S(2)}) %collective-permute-start.11) | collective-permute-done | bytes 239648 | tf_op jit(solution)/shard_map/ppermute | solution.py:187
  20.2 0.2 collective-permute-start.13
  20.4 2.9 %collective-permute-done.6.refs_0_ = bf16[104,1152]{1,0:T(8,128)(2,1)S(1)} collective-permute-done((bf16[104,1152]{1,0:T(8,128)(2,1)S(1)}, bf16[104,1152]{1,0:T(8,128)(2,1)S(1)}, u32[]{:S(2)}, u32[]{:S(2)}) %collective-permute-start.6) | collective-permute-done | bytes 239648 | tf_op jit(solution)/shard_map/ppermute | solution.py:187
  23.4 1.2 %collective-permute-start.12 = (bf16[104,1152]{1,0:T(8,128)(2,1)S(1)}, bf16[104,1152]{1,0:T(8,128)(2,1)S(1)}, u32[]{:S(2)}, u32[]{:S(2)}) collective-permute-start(bf16[104,1152]{1,0:T(8,128)(2,1)S(1)} %collective-permute-done.11.refs_0_), channel_id=1, source_target_pairs={{0,16},{1,17},{2,18},{3,19},{4,20},{5,21},{6,22},{7,23},{8,24},{9,... | collective-permute-start | bytes 718856 | tf_op jit(solution)/shard_map/ppermute | solution.py:187
  24.6 0.9 %collective-permute-done.13.refs_2_ = bf16[104,1152]{1,0:T(8,128)(2,1)S(1)} collective-permute-done((bf16[104,1152]{1,0:T(8,128)(2,1)S(1)}, bf16[104,1152]{1,0:T(8,128)(2,1)S(1)}, u32[]{:S(2)}, u32[]{:S(2)}) %collective-permute-start.13) | collective-permute-done | bytes 239648 | tf_op jit(solution)/shard_map/ppermute | solution.py:187
  25.5 0.2 collective-permute-start.8
  25.7 3.6 %collective-permute-done.12.refs_1_ = bf16[104,1152]{1,0:T(8,128)(2,1)S(1)} collective-permute-done((bf16[104,1152]{1,0:T(8,128)(2,1)S(1)}, bf16[104,1152]{1,0:T(8,128)(2,1)S(1)}, u32[]{:S(2)}, u32[]{:S(2)}) %collective-permute-start.12) | collective-permute-done | bytes 239648 | tf_op jit(solution)/shard_map/ppermute | solution.py:187
  29.4 0.2 collective-permute-start
  29.6 0.0 collective-permute-done.1.refs_2_
  29.6 1.2 %collective-permute-start.2 = (bf16[208,1152]{1,0:T(8,128)(2,1)S(1)}, bf16[208,1152]{1,0:T(8,128)(2,1)S(1)}, u32[]{:S(2)}, u32[]{:S(2)}) collective-permute-start(bf16[208,1152]{1,0:T(8,128)(2,1)S(1)} %collective-permute-done.1.refs_2_), channel_id=1, source_target_pairs={{0,2},{1,3},{2,0},{3,1},{4,6},{5,7},{6,4},{7,5},{8,10},{9,11},{10,... | collective-permute-start | bytes 1437704 | tf_op jit(solution)/shard_map/ppermute | solution.py:187
  30.8 0.0 collective-permute-done.8.refs_2_
  30.8 1.2 %collective-permute-start.14 = (bf16[104,1152]{1,0:T(8,128)(2,1)S(1)}, bf16[104,1152]{1,0:T(8,128)(2,1)S(1)}, u32[]{:S(2)}, u32[]{:S(2)}) collective-permute-start(bf16[104,1152]{1,0:T(8,128)(2,1)S(1)} %collective-permute-done.13.refs_2_), channel_id=1, source_target_pairs={{0,16},{1,17},{2,18},{3,19},{4,20},{5,21},{6,22},{7,23},{8,24},{9,... | collective-permute-start | bytes 718856 | tf_op jit(solution)/shard_map/ppermute | solution.py:187
  32.1 4.1 %collective-permute-done.14.refs_3_ = bf16[104,1152]{1,0:T(8,128)(2,1)S(1)} collective-permute-done((bf16[104,1152]{1,0:T(8,128)(2,1)S(1)}, bf16[104,1152]{1,0:T(8,128)(2,1)S(1)}, u32[]{:S(2)}, u32[]{:S(2)}) %collective-permute-start.14) | collective-permute-done | bytes 239648 | tf_op jit(solution)/shard_map/ppermute | solution.py:187
  36.1 1.2 %collective-permute-start.7 = (bf16[104,1152]{1,0:T(8,128)(2,1)S(1)}, bf16[104,1152]{1,0:T(8,128)(2,1)S(1)}, u32[]{:S(2)}, u32[]{:S(2)}) collective-permute-start(bf16[104,1152]{1,0:T(8,128)(2,1)S(1)} %collective-permute-done.6.refs_0_), channel_id=1, source_target_pairs={{0,16},{1,17},{2,18},{3,19},{4,20},{5,21},{6,22},{7,23},{8,24},{9,... | collective-permute-start | bytes 718856 | tf_op jit(solution)/shard_map/ppermute | solution.py:187
  37.3 0.0 collective-permute-done.3.refs_6_
  37.3 0.2 collective-permute-start.9
  37.6 0.0 collective-permute-done.4.refs_7_
  37.6 0.0 copy-start
  37.6 2.6 %copy-done = bf16[192,14336]{1,0:T(8,128)(2,1)S(1)} copy-done((bf16[192,14336]{1,0:T(8,128)(2,1)S(1)}, bf16[192,14336]{1,0:T(8,128)(2,1)}, u32[]{:S(2)}) %copy-start) | copy-done | bytes 5505048
  40.2 0.0 copy-start.2
  40.2 1.4 %copy-done.2 = bf16[192,4096]{1,0:T(8,128)(2,1)S(1)} copy-done((bf16[192,4096]{1,0:T(8,128)(2,1)S(1)}, bf16[192,4096]{1,0:T(8,128)(2,1)}, u32[]{:S(2)}) %copy-start.2) | copy-done | bytes 1572888
  41.6 0.0 copy-start.1
  41.6 0.0 copy-start.3
  41.6 9.1 %score.5 = (f32[2,192]{1,0:T(2,128)S(1)}, f32[2,192]{1,0:T(2,128)S(1)}) custom-call(s32[1]{0:T(128)} %bitcast.1.x_ref, bf16[104,1152]{1,0:T(8,128)(2,1)S(1)} %collective-permute-done.11.refs_0_, bf16[104,1152]{1,0:T(8,128)(2,1)S(1)} %collective-permute-done.12.refs_1_, bf16[104,1152]{1,0:T(8,128)(2,1)S(1)} %collective-permute-done.13.refs_2_, ...), custom_call_target="tpu_custom_call" | custom-call | flops 452984832 | bytes 14155776 | tf_op jit(solution)/shard_map/score/pallas_call | solution.py:132
  50.7 0.0 copy-start.7
  50.7 0.6 copy-done.7
  51.3 10.4 %collective-permute-start.15 = (f32[2,192]{1,0:T(2,128)S(1)}, f32[2,192]{1,0:T(2,128)S(1)}, u32[]{:S(2)}, u32[]{:S(2)}) collective-permute-start(f32[2,192]{1,0:T(2,128)S(1)} %get-tuple-element.20), channel_id=1, source_target_pairs={{0,1},{1,0},{2,3},{3,2},{4,5},{5,4},{6,7},{7,6},{8,9},{9,8},{10,11... | collective-permute-start | bytes 4616 | tf_op jit(solution)/shard_map/ppermute | solution.py:187
  61.6 0.0 collective-permute-done.refs_1_
  61.6 0.0 collective-permute-done.2.refs_3_
  61.6 0.0 copy-done.1
  61.6 0.0 copy-done.3
  61.7 9.3 %score.3 = (f32[4,192]{1,0:T(4,128)S(1)}, f32[4,192]{1,0:T(4,128)S(1)}) custom-call(s32[1]{0:T(128)} %bitcast.1.x_ref, bf16[208,1152]{1,0:T(8,128)(2,1)S(1)} %get-tuple-element.13.refs_0_, bf16[208,1152]{1,0:T(8,128)(2,1)S(1)} %collective-permute-done.refs_1_, bf16[208,1152]{1,0:T(8,128)(2,1)S(1)} %collective-permute-done.1.refs_2_, ...), custom_call_target="tpu_custom_call" | custom-call | flops 905969664 | bytes 14155776 | tf_op jit(solution)/shard_map/score/pallas_call | solution.py:132
  70.9 0.0 copy-start.6
  70.9 0.1 collective-permute-start.5
  71.0 0.0 collective-permute-done.7.refs_1_
  71.0 0.0 collective-permute-done.9.refs_3_
  71.0 9.0 %score.4 = (f32[2,192]{1,0:T(2,128)S(1)}, f32[2,192]{1,0:T(2,128)S(1)}) custom-call(s32[1]{0:T(128)} %bitcast.1.x_ref, bf16[104,1152]{1,0:T(8,128)(2,1)S(1)} %collective-permute-done.6.refs_0_, bf16[104,1152]{1,0:T(8,128)(2,1)S(1)} %collective-permute-done.7.refs_1_, bf16[104,1152]{1,0:T(8,128)(2,1)S(1)} %collective-permute-done.8.refs_2_, ...), custom_call_target="tpu_custom_call" | custom-call | flops 452984832 | bytes 14155776 | tf_op jit(solution)/shard_map/score/pallas_call | solution.py:132
  80.0 0.0 copy-done.6
  80.0 0.0 copy-start.8
  80.0 0.6 copy-done.8
  80.6 0.5 collective-permute-start.10
  81.1 0.0 collective-permute-done.15.refs_5_
  81.1 0.0 copy-start.10
  81.1 0.8 collective-permute-done.10.refs_3_
  81.9 0.0 copy-start.11
  81.9 0.0 collective-permute-done.5.refs_1_
  81.9 0.0 copy-start.9
  81.9 0.0 copy-done.10
  81.9 0.6 copy-done.11
  82.5 0.0 copy-done.9
  82.5 1.3 %place.1 = f32[16,192]{1,0:T(8,128)} custom-call(s32[1]{0:T(128)} %bitcast.me_ref, f32[4,192]{1,0:T(4,128)} %copy-done.6, f32[4,192]{1,0:T(4,128)} %copy-done.9, f32[2,192]{1,0:T(2,128)} %copy-done.8, f32[2,192]{1,0:T(2,128)} %copy-done.11, f32[2,192]{1,0:T(2,128)} %copy-done.7, f32[2,192]{1,0:T(2,128)} %copy-done.10), custom_call_target="tpu_custom_call" | custom-call | tf_op jit(solution)/shard_map/place/pallas_call | solution.py:169
Async XLA Ops:
  0.0 37.6 %collective-permute-start.4 = (bf16[192,14336]{1,0:T(8,128)(2,1)}, bf16[192,14336]{1,0:T(8,128)(2,1)}, u32[]{:S(2)}, u32[]{:S(2)}) collective-permute-start(bf16[192,14336]{1,0:T(8,128)(2,1)} %refs_5_.5), channel_id=1, source_target_pairs={{0,1},{1,0},{2,3},{3,2},{4,5},{5,4},{6,7},{7,6},{8,9},{9,8},{10,11... | collective-permute-start | bytes 16515080 | tf_op jit(solution)/shard_map/ppermute | solution.py:187
  0.7 36.7 %collective-permute-start.3 = (bf16[192,4096]{1,0:T(8,128)(2,1)}, bf16[192,4096]{1,0:T(8,128)(2,1)S(1)}, u32[]{:S(2)}, u32[]{:S(2)}) collective-permute-start(bf16[192,4096]{1,0:T(8,128)(2,1)} %refs_4_.5), channel_id=1, source_target_pairs={{0,1},{1,0},{2,3},{3,2},{4,5},{5,4},{6,7},{7,6},{8,9},{9,8},{10,11... | collective-permute-start | bytes 4718600 | tf_op jit(solution)/shard_map/ppermute | solution.py:187
  0.7 1.0 %copy-start.4 = (bf16[1,13,14336]{2,1,0:T(8,128)(2,1)S(1)}, bf16[1,13,14336]{2,1,0:T(8,128)(2,1)}, u32[]{:S(2)}) copy-start(bf16[1,13,14336]{2,1,0:T(8,128)(2,1)} %act_ref.1) | copy-start | bytes 1118212
  1.7 0.9 %copy-start.5 = (bf16[1,13,4096]{2,1,0:T(8,128)(2,1)S(1)}, bf16[1,13,4096]{2,1,0:T(8,128)(2,1)}, u32[]{:S(2)}) copy-start(bf16[1,13,4096]{2,1,0:T(8,128)(2,1)} %err_ref.1) | copy-start | bytes 319492
  3.0 17.2 %collective-permute-start.11 = (bf16[104,1152]{1,0:T(8,128)(2,1)S(1)}, bf16[104,1152]{1,0:T(8,128)(2,1)S(1)}, u32[]{:S(2)}, u32[]{:S(2)}) collective-permute-start(bf16[104,1152]{1,0:T(8,128)(2,1)S(1)} %get-tuple-element.16), channel_id=1, source_target_pairs={{0,12},{1,13},{2,14},{3,15},{4,8},{5,9},{6,10},{7,11},{8,4},{9,5},... | collective-permute-start | bytes 718856 | tf_op jit(solution)/shard_map/ppermute | solution.py:187
  3.2 20.1 %collective-permute-start.6 = (bf16[104,1152]{1,0:T(8,128)(2,1)S(1)}, bf16[104,1152]{1,0:T(8,128)(2,1)S(1)}, u32[]{:S(2)}, u32[]{:S(2)}) collective-permute-start(bf16[104,1152]{1,0:T(8,128)(2,1)S(1)} %get-tuple-element.16), channel_id=1, source_target_pairs={{0,8},{1,9},{2,10},{3,11},{4,12},{5,13},{6,14},{7,15},{8,0},{9,1},... | collective-permute-start | bytes 718856 | tf_op jit(solution)/shard_map/ppermute | solution.py:187
  6.4 23.2 %collective-permute-start.1 = (bf16[208,1152]{1,0:T(8,128)(2,1)S(1)}, bf16[208,1152]{1,0:T(8,128)(2,1)S(1)}, u32[]{:S(2)}, u32[]{:S(2)}) collective-permute-start(bf16[208,1152]{1,0:T(8,128)(2,1)S(1)} %get-tuple-element.13.refs_0_), channel_id=1, source_target_pairs={{0,4},{1,5},{2,6},{3,7},{4,0},{5,1},{6,2},{7,3},{8,12},{9,13},{10,... | collective-permute-start | bytes 1437704 | tf_op jit(solution)/shard_map/ppermute | solution.py:187
  20.2 5.3 %collective-permute-start.13 = (bf16[104,1152]{1,0:T(8,128)(2,1)S(1)}, bf16[104,1152]{1,0:T(8,128)(2,1)S(1)}, u32[]{:S(2)}, u32[]{:S(2)}) collective-permute-start(bf16[104,1152]{1,0:T(8,128)(2,1)S(1)} %collective-permute-done.11.refs_0_), channel_id=1, source_target_pairs={{0,2},{1,3},{2,0},{3,1},{4,6},{5,7},{6,4},{7,5},{8,10},{9,11},{10,... | collective-permute-start | bytes 718856 | tf_op jit(solution)/shard_map/ppermute | solution.py:187
  23.4 6.0 %collective-permute-start.12 = (bf16[104,1152]{1,0:T(8,128)(2,1)S(1)}, bf16[104,1152]{1,0:T(8,128)(2,1)S(1)}, u32[]{:S(2)}, u32[]{:S(2)}) collective-permute-start(bf16[104,1152]{1,0:T(8,128)(2,1)S(1)} %collective-permute-done.11.refs_0_), channel_id=1, source_target_pairs={{0,16},{1,17},{2,18},{3,19},{4,20},{5,21},{6,22},{7,23},{8,24},{9,... | collective-permute-start | bytes 718856 | tf_op jit(solution)/shard_map/ppermute | solution.py:187
  25.5 5.4 %collective-permute-start.8 = (bf16[104,1152]{1,0:T(8,128)(2,1)S(1)}, bf16[104,1152]{1,0:T(8,128)(2,1)S(1)}, u32[]{:S(2)}, u32[]{:S(2)}) collective-permute-start(bf16[104,1152]{1,0:T(8,128)(2,1)S(1)} %collective-permute-done.6.refs_0_), channel_id=1, source_target_pairs={{0,2},{1,3},{2,0},{3,1},{4,6},{5,7},{6,4},{7,5},{8,10},{9,11},{10,... | collective-permute-start | bytes 718856 | tf_op jit(solution)/shard_map/ppermute | solution.py:187
  29.4 32.3 %collective-permute-start = (bf16[208,1152]{1,0:T(8,128)(2,1)S(1)}, bf16[208,1152]{1,0:T(8,128)(2,1)S(1)}, u32[]{:S(2)}, u32[]{:S(2)}) collective-permute-start(bf16[208,1152]{1,0:T(8,128)(2,1)S(1)} %get-tuple-element.13.refs_0_), channel_id=1, source_target_pairs={{0,2},{1,3},{2,0},{3,1},{4,6},{5,7},{6,4},{7,5},{8,10},{9,11},{10,... | collective-permute-start | bytes 1437704 | tf_op jit(solution)/shard_map/ppermute | solution.py:187
  29.6 32.0 %collective-permute-start.2 = (bf16[208,1152]{1,0:T(8,128)(2,1)S(1)}, bf16[208,1152]{1,0:T(8,128)(2,1)S(1)}, u32[]{:S(2)}, u32[]{:S(2)}) collective-permute-start(bf16[208,1152]{1,0:T(8,128)(2,1)S(1)} %collective-permute-done.1.refs_2_), channel_id=1, source_target_pairs={{0,2},{1,3},{2,0},{3,1},{4,6},{5,7},{6,4},{7,5},{8,10},{9,11},{10,... | collective-permute-start | bytes 1437704 | tf_op jit(solution)/shard_map/ppermute | solution.py:187
  30.8 5.3 %collective-permute-start.14 = (bf16[104,1152]{1,0:T(8,128)(2,1)S(1)}, bf16[104,1152]{1,0:T(8,128)(2,1)S(1)}, u32[]{:S(2)}, u32[]{:S(2)}) collective-permute-start(bf16[104,1152]{1,0:T(8,128)(2,1)S(1)} %collective-permute-done.13.refs_2_), channel_id=1, source_target_pairs={{0,16},{1,17},{2,18},{3,19},{4,20},{5,21},{6,22},{7,23},{8,24},{9,... | collective-permute-start | bytes 718856 | tf_op jit(solution)/shard_map/ppermute | solution.py:187
  36.1 34.9 %collective-permute-start.7 = (bf16[104,1152]{1,0:T(8,128)(2,1)S(1)}, bf16[104,1152]{1,0:T(8,128)(2,1)S(1)}, u32[]{:S(2)}, u32[]{:S(2)}) collective-permute-start(bf16[104,1152]{1,0:T(8,128)(2,1)S(1)} %collective-permute-done.6.refs_0_), channel_id=1, source_target_pairs={{0,16},{1,17},{2,18},{3,19},{4,20},{5,21},{6,22},{7,23},{8,24},{9,... | collective-permute-start | bytes 718856 | tf_op jit(solution)/shard_map/ppermute | solution.py:187
  37.3 33.7 %collective-permute-start.9 = (bf16[104,1152]{1,0:T(8,128)(2,1)S(1)}, bf16[104,1152]{1,0:T(8,128)(2,1)S(1)}, u32[]{:S(2)}, u32[]{:S(2)}) collective-permute-start(bf16[104,1152]{1,0:T(8,128)(2,1)S(1)} %collective-permute-done.8.refs_2_), channel_id=1, source_target_pairs={{0,16},{1,17},{2,18},{3,19},{4,20},{5,21},{6,22},{7,23},{8,24},{9,... | collective-permute-start | bytes 718856 | tf_op jit(solution)/shard_map/ppermute | solution.py:187
  37.6 2.6 %copy-start = (bf16[192,14336]{1,0:T(8,128)(2,1)S(1)}, bf16[192,14336]{1,0:T(8,128)(2,1)}, u32[]{:S(2)}) copy-start(bf16[192,14336]{1,0:T(8,128)(2,1)} %refs_5_.5) | copy-start | bytes 16515076
  40.2 1.4 %copy-start.2 = (bf16[192,4096]{1,0:T(8,128)(2,1)S(1)}, bf16[192,4096]{1,0:T(8,128)(2,1)}, u32[]{:S(2)}) copy-start(bf16[192,4096]{1,0:T(8,128)(2,1)} %refs_4_.5) | copy-start | bytes 4718596
  41.6 20.1 %copy-start.1 = (bf16[192,14336]{1,0:T(8,128)(2,1)S(1)}, bf16[192,14336]{1,0:T(8,128)(2,1)}, u32[]{:S(2)}) copy-start(bf16[192,14336]{1,0:T(8,128)(2,1)} %refs_5_.5) | copy-start | bytes 16515076
  41.6 20.1 %copy-start.3 = (bf16[192,4096]{1,0:T(8,128)(2,1)S(1)}, bf16[192,4096]{1,0:T(8,128)(2,1)}, u32[]{:S(2)}) copy-start(bf16[192,4096]{1,0:T(8,128)(2,1)} %refs_4_.5) | copy-start | bytes 4718596
  50.7 0.6 copy-start.7
  51.3 29.8 %collective-permute-start.15 = (f32[2,192]{1,0:T(2,128)S(1)}, f32[2,192]{1,0:T(2,128)S(1)}, u32[]{:S(2)}, u32[]{:S(2)}) collective-permute-start(f32[2,192]{1,0:T(2,128)S(1)} %get-tuple-element.20), channel_id=1, source_target_pairs={{0,1},{1,0},{2,3},{3,2},{4,5},{5,4},{6,7},{7,6},{8,9},{9,8},{10,11... | collective-permute-start | bytes 4616 | tf_op jit(solution)/shard_map/ppermute | solution.py:187
  70.9 9.1 %copy-start.6 = (f32[4,192]{1,0:T(4,128)}, f32[4,192]{1,0:T(4,128)S(1)}, u32[]{:S(2)}) copy-start(f32[4,192]{1,0:T(4,128)S(1)} %get-tuple-element.14.refs_0_) | copy-start | bytes 9220
  70.9 11.0 %collective-permute-start.5 = (f32[4,192]{1,0:T(4,128)S(1)}, f32[4,192]{1,0:T(4,128)S(1)}, u32[]{:S(2)}, u32[]{:S(2)}) collective-permute-start(f32[4,192]{1,0:T(4,128)S(1)} %get-tuple-element.15), channel_id=1, source_target_pairs={{0,1},{1,0},{2,3},{3,2},{4,5},{5,4},{6,7},{7,6},{8,9},{9,8},{10,11... | collective-permute-start | bytes 9224 | tf_op jit(solution)/shard_map/ppermute | solution.py:187
  80.0 0.6 copy-start.8
  80.6 1.3 %collective-permute-start.10 = (f32[2,192]{1,0:T(2,128)S(1)}, f32[2,192]{1,0:T(2,128)S(1)}, u32[]{:S(2)}, u32[]{:S(2)}) collective-permute-start(f32[2,192]{1,0:T(2,128)S(1)} %get-tuple-element.18), channel_id=1, source_target_pairs={{0,1},{1,0},{2,3},{3,2},{4,5},{5,4},{6,7},{7,6},{8,9},{9,8},{10,11... | collective-permute-start | bytes 4616 | tf_op jit(solution)/shard_map/ppermute | solution.py:187
  81.1 0.8 copy-start.10
  81.9 0.6 copy-start.11
  81.9 0.6 copy-start.9

commit v2 on v0

v2 whole, which is shorter than its diff:
```python
import functools

import jax
import jax.numpy as jnp
from jax import lax
from jax.experimental import pallas as pl
from jax.experimental.pallas import tpu as pltpu
from jax.sharding import PartitionSpec as P

AXES = ("grp", "blk")
NT = (((1,), (1,)), ((), ()))
RANK = 13
SEGS = 16
ROWS = 16
CUTS = 4


def project_rows(err_rows, act_rows, err_piece, act_piece):
    err_proj = jnp.einsum("td,qrd->qrt", err_rows, err_piece, preferred_element_type=jnp.float32)
    act_proj = jnp.einsum("tf,qrf->qrt", act_rows, act_piece, preferred_element_type=jnp.float32)
    return (err_proj, act_proj)


def gathered(activations, errors, err_factors, act_factors):
    err_width = errors.shape[1]
    joined = jnp.concatenate((err_factors, act_factors), axis=2)
    piece = lax.all_gather(joined, "blk", axis=0, tiled=True)
    err_proj, act_proj = project_rows(
        errors, activations, piece[:, :, :err_width], piece[:, :, err_width:]
    )
    return jnp.sum(err_proj * act_proj, axis=1)


def picks(shape, stacked_dim, offset):
    stacked = lax.broadcasted_iota(jnp.int32, shape, stacked_dim)
    packed = lax.broadcasted_iota(jnp.int32, shape, 1 - stacked_dim) - offset
    m, r = stacked >> 4, stacked & 15
    return ((r < RANK) & (packed == RANK * m + r)).astype(jnp.bfloat16)


def pack_kernel(first, x_ref, err_ref, act_ref, out_ref, runs):
    ew, aw = err_ref.shape[2] // SEGS, act_ref.shape[2] // SEGS
    n = SEGS // 2
    rows = n * RANK
    runs[...] = jnp.zeros_like(runs)
    for s in range(SEGS):
        runs[s // n, s % n * ROWS : s % n * ROWS + RANK, :ew] = err_ref[0, :, s * ew : (s + 1) * ew]
        runs[s // n, s % n * ROWS : s % n * ROWS + RANK, ew:] = act_ref[0, :, s * aw : (s + 1) * aw]
    x = x_ref[0]
    total = None
    for i, h in enumerate((x,) if first else (x, 1 - x)):
        pick = picks((out_ref.shape[0], n * ROWS), 1, i * rows)
        term = jnp.dot(pick, runs[h], preferred_element_type=jnp.float32)
        total = term if total is None else total + term
    out_ref[...] = total.astype(jnp.bfloat16)


def pack(x, err, act, first):
    width = (err.shape[2] + act.shape[2]) // SEGS
    n = SEGS // 2
    vmem = pl.BlockSpec(memory_space=pltpu.VMEM)
    return pl.pallas_call(
        functools.partial(pack_kernel, first),
        out_shape=jax.ShapeDtypeStruct(((1 if first else 2) * n * RANK, width), jnp.bfloat16),
        in_specs=[pl.BlockSpec(memory_space=pltpu.SMEM), vmem, vmem],
        out_specs=vmem,
        scratch_shapes=[pltpu.VMEM((2, n * ROWS, width), jnp.bfloat16)],
        compiler_params=pltpu.CompilerParams(vmem_limit_bytes=16 << 20),
        cost_estimate=None if first else weight(20),
        name="pack",
    )(x, err, act)


def weight(us):
    return pl.CostEstimate(flops=int(us * 1e9), bytes_accessed=int(us * 3e6), transcendentals=0)


def score_kernel(jobs, n_pieces, n_in, last, x_ref, *refs):
    pieces, refs = refs[:n_pieces], refs[n_pieces:]
    (eo_ref, ao_ref, ep_ref, ap_ref), refs = refs[:4], refs[4:]
    accs_in, refs = refs[:n_in], refs[n_in:]
    outs, (we, wa) = refs[:-2], refs[-2:]
    n = SEGS // 2
    ew, aw = we.shape[1] // n, wa.shape[1] // n
    x = x_ref[0]
    sums = [a[...] for a in accs_in] if n_in else [None] * 4
    for other, parts in jobs:
        for b, (i, offset) in enumerate(parts):
            pick = picks((n * ROWS, pieces[i].shape[0]), 0, offset)
            run = jnp.dot(pick, pieces[i][...], preferred_element_type=jnp.float32)
            run = run.astype(jnp.bfloat16)
            for s in range(n):
                own = run[s * ROWS : (s + 1) * ROWS]
                we[b * ROWS : (b + 1) * ROWS, s * ew : (s + 1) * ew] = own[:, :ew]
                wa[b * ROWS : (b + 1) * ROWS, s * aw : (s + 1) * aw] = own[:, ew:]
        half = 1 - x if other else x
        for j, (w, t_ref) in enumerate(((we, eo_ref), (wa, ao_ref), (we, ep_ref), (wa, ap_ref))):
            width = w.shape[1]
            cut = width // CUTS
            for i in range(CUTS):
                at = pl.ds(pl.multiple_of(half * width + i * cut, cut), cut)
                term = lax.dot_general(
                    w[:, i * cut : (i + 1) * cut], t_ref[:, at], NT,
                    preferred_element_type=jnp.float32,
                )
                sums[j] = term if sums[j] is None else sums[j] + term
    if not last:
        for o, v in zip(outs, sums):
            o[...] = v
        return
    for o, e, a in zip(outs, sums[::2], sums[1::2]):
        prod = e * a
        for b in range(o.shape[0]):
            o[b : b + 1, :] = jnp.sum(prod[b * ROWS : (b + 1) * ROWS], axis=0, keepdims=True)


def score(x, pieces, jobs, tokens, accs=(), last=True):
    errs, acts = tokens[0].shape[1], tokens[1].shape[1]
    t, nb = tokens[0].shape[0], len(jobs[0][1])
    vmem = pl.BlockSpec(memory_space=pltpu.VMEM)
    if last:
        outs = (jax.ShapeDtypeStruct((nb, t), jnp.float32),) * 2
    else:
        outs = (jax.ShapeDtypeStruct((nb * ROWS, t), jnp.float32),) * 4
    return pl.pallas_call(
        functools.partial(score_kernel, jobs, len(pieces), len(accs), last),
        out_shape=outs,
        in_specs=[pl.BlockSpec(memory_space=pltpu.SMEM)]
        + [vmem] * (len(pieces) + 4 + len(accs)),
        out_specs=(vmem,) * len(outs),
        scratch_shapes=[
            pltpu.VMEM((nb * ROWS, errs // 2), jnp.bfloat16),
            pltpu.VMEM((nb * ROWS, acts // 2), jnp.bfloat16),
        ],
        compiler_params=pltpu.CompilerParams(vmem_limit_bytes=32 << 20),
        cost_estimate=weight(30),
        name="score",
    )(x, *pieces, *tokens, *accs)


def place_kernel(me_ref, *refs):
    out_ref = refs[-1]
    me = me_ref[0]
    row = 0
    for own, par in zip(refs[:-1:2], refs[1:-1:2]):
        for b in range(own.shape[0]):
            q = jnp.bitwise_xor(me, 2 * row)
            out_ref[pl.ds(q, 1), :] = own[b : b + 1, :]
            out_ref[pl.ds(jnp.bitwise_xor(q, 1), 1), :] = par[b : b + 1, :]
            row += 1


def finish(me, rows, queries, t):
    vmem = pl.BlockSpec(memory_space=pltpu.VMEM)
    return pl.pallas_call(
        place_kernel,
        out_shape=jax.ShapeDtypeStruct((queries, t), jnp.float32),
        in_specs=[pl.BlockSpec(memory_space=pltpu.SMEM)] + [vmem] * len(rows),
        out_specs=vmem,
        name="place",
    )(me, *rows)


def pairs(n_grp, n_blk, flip_grp, flip_blk):
    return [
        (g * n_blk + b, (g ^ flip_grp) * n_blk + (b ^ flip_blk))
        for g in range(n_grp)
        for b in range(n_blk)
    ]


def after(*arrays):
    return lax.optimization_barrier(arrays)


def permuted(n_grp, n_blk, activations, errors, err_factors, act_factors):
    swap = lambda a, gx, bx: lax.ppermute(a, AXES, pairs(n_grp, n_blk, gx, bx))
    over_x = lambda a: swap(a, 1, 0)
    over_y = lambda a: swap(a, 0, 2)
    over_z = lambda a, k: swap(a, 0, 4 * k)
    mate = lambda a: swap(a, 0, 1)
    x = lax.axis_index("grp").astype(jnp.int32).reshape(1)
    me = lax.axis_index("blk").astype(jnp.int32).reshape(1)

    half = pack(x, err_factors, act_factors, True)
    mate_acts = mate(activations)
    mate_errs = mate(errors)
    z3 = over_z(half, 3)
    x_late, half = after(x, half)
    both = pack(x_late, err_factors, act_factors, False)
    y0, z1 = over_y(both), over_z(both, 1)
    y3, xa3 = over_y(z3), over_x(z3)
    z2 = over_z(z3, 1)
    n = half.shape[0]
    y1m = over_y(z1[:n])

    tokens = (errors, activations, mate_errs, mate_acts)
    y0, z3 = after(y0, z3)
    o0, p0 = score(
        x, (both, y0), ((False, ((0, 0), (1, 0))), (True, ((0, n), (1, n)))), tokens
    )
    z2, y3, z1, o0 = after(z2, y3, z1, o0)
    xb3 = over_x(y3)
    y2, xa2 = over_y(z2), over_x(z2)
    y1o = over_y(z1[n:])
    xb2 = over_x(y2)

    z2, xa3, xa2, xb3 = after(z2, xa3, xa2, xb3)
    five = tuple((i, 0) for i in range(1, 6))
    accs = score(x, (z1, y1m, z2, y2, z3, y3), ((False, ((0, 0),) + five),), tokens, last=False)
    o1, p1 = score(
        x, (z1, y1o, xa2, xb2, xa3, xb3), ((True, ((0, n),) + five),), tokens, accs
    )
    rows = (o0, mate(p0), o1, mate(p1))
    return finish(me, rows, n_blk, errors.shape[0])


def solution(mesh):
    in_specs = (
        P(("grp", "blk"), None),
        P(("grp", "blk"), None),
        P("blk", None, None),
        P("blk", None, None),
    )
    out_specs = P(None, ("grp", "blk"))
    n_grp, n_blk = mesh.shape["grp"], mesh.shape["blk"]
    body = gathered
    if (n_grp, n_blk) == (2, 16):
        body = functools.partial(permuted, n_grp, n_blk)
    return jax.shard_map(body, mesh=mesh, in_specs=in_specs, out_specs=out_specs, check_vma=False)
```

time: 114 us -> 61.6 us (0.54)
  waiting for transfers between devices: 85 us -> 17.4 us
  starting transfers between devices: 0.01 us -> 20 us
  Pallas kernels: 0 us -> 19.9 us
  between operations: 13.4 us -> 0.14 us
  matrix products: 8.61 us -> 0 us
  other arithmetic: 2.03 us -> 0.01 us
    all_gather x1 -> x0, waiting for transfers between devices: 85 us -> none  [local(): piece = lax.all_gather(joined, 'blk', axis=0, tiled=True)]
    ppermute x0 -> x16, starting transfers between devices: none -> 20 us  [permuted(): swap = lambda a, gx, bx: lax.ppermute(a, AXES, pairs(n_grp, n_blk, gx, bx))]
    pallas_call x0 -> x6, Pallas kernels: none -> 19.9 us  [the longest x3 17.7 us: score(): pl.pallas_call(functools.partial(score_kernel, jobs, len(pieces), len(acc...]
    ppermute x0 -> x16, waiting for transfers between devices: none -> 17.4 us  [permuted(): swap = lambda a, gx, bx: lax.ppermute(a, AXES, pairs(n_grp, n_blk, gx, bx))]
    dot_general x2 -> x0, matrix products: 8.61 us -> none  [the longest x1 6.72 us: project_rows(): jnp.einsum('tf,qrf->qrt', act_rows, act_piece, preferred_element_type=jnp...]
    slice x4 -> x2, local copies, waits for them, and re-layouts: 4.66 us -> 0.04 us  [the longest x1 0.02 us: permuted(): y1m = over_y(z1[:n])]
    unnamed x2 -> x18, local copies, waits for them, and re-layouts: 0.01 us -> 3.69 us
    concatenate x1 -> x0, other arithmetic: 2.03 us -> none  [local(): joined = jnp.concatenate((err_factors, act_factors), axis=2)]
  transfers between devices with their start and end apart: 1 -> 16, of which waited for: 1 -> 5; matrix products, arithmetic and copies ran while one was open for 0% -> 0% of each run, Pallas kernels for 0% -> 22%
where the time goes in v2:
time: 61.6 us; the launch traced here: 61.2 us
  starting transfers between devices  20 us (32%)
  Pallas kernels  19.9 us (32%)
  waiting for transfers between devices  17.4 us (28%)
  local copies, waits for them, and re-layouts  3.73 us (6%)
    ppermute x16, starting transfers between devices, permuted(): swap = lambda a, gx, bx: lax.ppermute(a, AXES, pairs(n_grp, n_blk, gx, bx))  20 us
    pallas_call x3, Pallas kernels, score(): pl.pallas_call(functools.partial(score_kernel, jobs, len(pieces), len(acc...  17.7 us
    ppermute x16, waiting for transfers between devices, permuted(): swap = lambda a, gx, bx: lax.ppermute(a, AXES, pairs(n_grp, n_blk, gx, bx))  17.4 us
    unnamed x18, local copies, waits for them, and re-layouts  3.69 us
    pallas_call x1, Pallas kernels, finish(): pl.pallas_call(place_kernel, out_shape=jax.ShapeDtypeStruct((queries, t),...  1.35 us
  transfers between devices with their start and end apart: 16, of which 5 were waited for; matrix products, arithmetic and copies ran while one was open for 0% of the time, Pallas kernels for 22%

profile of v2, /device:TPU:1, one launch (start us, length us, event | category | flops | bytes accessed | tf_op | source)
XLA Modules:
  0.0 61.2 jit_solution(14606474376127029043)
XLA Ops:
  0.0 0.1 collective-permute-start.6
  0.1 0.5 collective-permute-start.5
  0.5 0.0 copy-start
  0.5 1.0 %copy-done = bf16[1,13,14336]{2,1,0:T(8,128)(2,1)S(1)} copy-done((bf16[1,13,14336]{2,1,0:T(8,128)(2,1)S(1)}, bf16[1,13,14336]{2,1,0:T(8,128)(2,1)}, u32[]{:S(2)}) %copy-start) | copy-done | bytes 372760
  1.5 0.0 copy-start.1
  1.5 0.9 %copy-done.1 = bf16[1,13,4096]{2,1,0:T(8,128)(2,1)S(1)} copy-done((bf16[1,13,4096]{2,1,0:T(8,128)(2,1)S(1)}, bf16[1,13,4096]{2,1,0:T(8,128)(2,1)}, u32[]{:S(2)}) %copy-start.1) | copy-done | bytes 106520
  2.4 0.0 slice-start
  2.4 0.3 pack.2
  2.8 0.0 slice-start.1
  2.8 0.0 copy-start.4
  2.8 0.5 pack.3.refs_0_
  3.3 2.3 %collective-permute-start.4 = (bf16[208,1152]{1,0:T(8,128)(2,1)S(1)}, bf16[208,1152]{1,0:T(8,128)(2,1)S(1)}, u32[]{:S(2)}, u32[]{:S(2)}) collective-permute-start(bf16[208,1152]{1,0:T(8,128)(2,1)S(1)} %pack.3.refs_0_), channel_id=1, source_target_pairs={{0,2},{1,3},{2,0},{3,1},{4,6},{5,7},{6,4},{7,5},{8,10},{9,11},{10,... | collective-permute-start | bytes 1437704 | tf_op jit(solution)/shard_map/ppermute | solution.py:177
  5.6 3.3 %collective-permute-start = (bf16[104,1152]{1,0:T(8,128)(2,1)S(1)}, bf16[104,1152]{1,0:T(8,128)(2,1)S(1)}, u32[]{:S(2)}, u32[]{:S(2)}) collective-permute-start(bf16[104,1152]{1,0:T(8,128)(2,1)S(1)} %pack.2), channel_id=1, source_target_pairs={{0,12},{1,13},{2,14},{3,15},{4,8},{5,9},{6,10},{7,11},{8,4},{9,5},... | collective-permute-start | bytes 718856 | tf_op jit(solution)/shard_map/ppermute | solution.py:177
  8.9 0.0 collective-permute-start.3
  8.9 5.3 %collective-permute-done.refs_4_ = bf16[104,1152]{1,0:T(8,128)(2,1)S(1)} collective-permute-done((bf16[104,1152]{1,0:T(8,128)(2,1)S(1)}, bf16[104,1152]{1,0:T(8,128)(2,1)S(1)}, u32[]{:S(2)}, u32[]{:S(2)}) %collective-permute-start) | collective-permute-done | bytes 239648 | tf_op jit(solution)/shard_map/ppermute | solution.py:177
  14.2 4.7 %collective-permute-start.1 = (bf16[104,1152]{1,0:T(8,128)(2,1)S(1)}, bf16[104,1152]{1,0:T(8,128)(2,1)S(1)}, u32[]{:S(2)}, u32[]{:S(2)}) collective-permute-start(bf16[104,1152]{1,0:T(8,128)(2,1)S(1)} %collective-permute-done.refs_4_), channel_id=1, source_target_pairs={{0,4},{1,5},{2,6},{3,7},{4,0},{5,1},{6,2},{7,3},{8,12},{9,13},{10,... | collective-permute-start | bytes 718856 | tf_op jit(solution)/shard_map/ppermute | solution.py:177
  18.9 0.0 collective-permute-done.4.refs_1_
  18.9 0.2 collective-permute-start.2
  19.1 0.0 collective-permute-done.5.refs_4_.refs_8_
  19.1 1.2 %collective-permute-start.9 = (bf16[104,1152]{1,0:T(8,128)(2,1)S(1)}, bf16[104,1152]{1,0:T(8,128)(2,1)S(1)}, u32[]{:S(2)}, u32[]{:S(2)}) collective-permute-start(bf16[104,1152]{1,0:T(8,128)(2,1)S(1)} %collective-permute-done.refs_4_), channel_id=1, source_target_pairs={{0,16},{1,17},{2,18},{3,19},{4,20},{5,21},{6,22},{7,23},{8,24},{9,... | collective-permute-start | bytes 718856 | tf_op jit(solution)/shard_map/ppermute | solution.py:177
  20.3 0.0 collective-permute-done.6.refs_5_.refs_9_
  20.3 0.0 slice-done
  20.3 0.0 slice-done.1
  20.3 0.0 copy-done.4
  20.4 7.4 %score.3 = (f32[2,192]{1,0:T(2,128)S(1)}, f32[2,192]{1,0:T(2,128)S(1)}) custom-call(s32[1]{0:T(128)} %bitcast.1.x_ref, bf16[208,1152]{1,0:T(8,128)(2,1)S(1)} %pack.3.refs_0_, bf16[208,1152]{1,0:T(8,128)(2,1)S(1)} %collective-permute-done.4.refs_1_, bf16[192,4096]{1,0:T(8,128)(2,1)S(1)} %copy-done.4, bf16[192,14336]{1,0:T(8,128)(2,1)S(1)} %bitcast.3, ...), custom_call_target="tpu_custom_call" | custom-call | flops 30000001024 | bytes 90000000 | tf_op jit(solution)/shard_map/score/pallas_call | solution.py:125
  27.8 0.0 copy-start.3
  27.8 0.6 copy-done.3
  28.4 0.0 collective-permute-done.3.refs_0_
  28.4 2.3 %collective-permute-done.1.refs_2_ = bf16[104,1152]{1,0:T(8,128)(2,1)S(1)} collective-permute-done((bf16[104,1152]{1,0:T(8,128)(2,1)S(1)}, bf16[104,1152]{1,0:T(8,128)(2,1)S(1)}, u32[]{:S(2)}, u32[]{:S(2)}) %collective-permute-start.1) | collective-permute-done | bytes 239648 | tf_op jit(solution)/shard_map/ppermute | solution.py:177
  30.7 0.0 collective-permute-done.2.refs_5_
  30.7 1.2 %collective-permute-start.10 = (bf16[104,1152]{1,0:T(8,128)(2,1)S(1)}, bf16[104,1152]{1,0:T(8,128)(2,1)S(1)}, u32[]{:S(2)}, u32[]{:S(2)}) collective-permute-start(bf16[104,1152]{1,0:T(8,128)(2,1)S(1)} %collective-permute-done.1.refs_2_), channel_id=1, source_target_pairs={{0,16},{1,17},{2,18},{3,19},{4,20},{5,21},{6,22},{7,23},{8,24},{9,... | collective-permute-start | bytes 718856 | tf_op jit(solution)/shard_map/ppermute | solution.py:177
  31.9 0.3 collective-permute-start.11
  32.2 0.2 collective-permute-start.12
  32.4 1.3 %collective-permute-start.14 = (bf16[104,1152]{1,0:T(8,128)(2,1)S(1)}, bf16[104,1152]{1,0:T(8,128)(2,1)S(1)}, u32[]{:S(2)}, u32[]{:S(2)}) collective-permute-start(bf16[104,1152]{1,0:T(8,128)(2,1)S(1)} %slice.8), channel_id=1, source_target_pairs={{0,2},{1,3},{2,0},{3,1},{4,6},{5,7},{6,4},{7,5},{8,10},{9,11},{10,... | collective-permute-start | bytes 718856 | tf_op jit(solution)/shard_map/ppermute | solution.py:177
  33.7 0.0 collective-permute-done.9.refs_4_
  33.8 0.3 collective-permute-start.8
  34.0 3.6 %collective-permute-done.10.refs_2_ = bf16[104,1152]{1,0:T(8,128)(2,1)S(1)} collective-permute-done((bf16[104,1152]{1,0:T(8,128)(2,1)S(1)}, bf16[104,1152]{1,0:T(8,128)(2,1)S(1)}, u32[]{:S(2)}, u32[]{:S(2)}) %collective-permute-start.10) | collective-permute-done | bytes 239648 | tf_op jit(solution)/shard_map/ppermute | solution.py:177
  37.6 5.1 %collective-permute-done.11.refs_5_ = bf16[104,1152]{1,0:T(8,128)(2,1)S(1)} collective-permute-done((bf16[104,1152]{1,0:T(8,128)(2,1)S(1)}, bf16[104,1152]{1,0:T(8,128)(2,1)S(1)}, u32[]{:S(2)}, u32[]{:S(2)}) %collective-permute-start.11) | collective-permute-done | bytes 239648 | tf_op jit(solution)/shard_map/ppermute | solution.py:177
  42.7 0.0 collective-permute-done.12.refs_3_
  42.7 1.2 %collective-permute-start.13 = (bf16[104,1152]{1,0:T(8,128)(2,1)S(1)}, bf16[104,1152]{1,0:T(8,128)(2,1)S(1)}, u32[]{:S(2)}, u32[]{:S(2)}) collective-permute-start(bf16[104,1152]{1,0:T(8,128)(2,1)S(1)} %collective-permute-done.12.refs_3_), channel_id=1, source_target_pairs={{0,16},{1,17},{2,18},{3,19},{4,20},{5,21},{6,22},{7,23},{8,24},{9,... | collective-permute-start | bytes 718856 | tf_op jit(solution)/shard_map/ppermute | solution.py:177
  44.0 0.0 collective-permute-done.14.refs_1_
  44.0 5.1 %score.4 = (f32[96,192]{1,0:T(8,128)S(1)}, f32[96,192]{1,0:T(8,128)S(1)}, f32[96,192]{1,0:T(8,128)S(1)}, f32[96,192]{1,0:T(8,128)S(1)}) custom-call(s32[1]{0:T(128)} %bitcast.1.x_ref, bf16[208,1152]{1,0:T(8,128)(2,1)S(1)} %collective-permute-done.3.refs_0_, bf16[104,1152]{1,0:T(8,128)(2,1)S(1)} %collective-permute-done.14.refs_1_, ...), custom_call_target="tpu_custom_call" | custom-call | flops 30000001024 | bytes 90000000 | tf_op jit(solution)/shard_map/score/pallas_call | solution.py:125
  49.1 0.0 collective-permute-done.8.refs_1_
  49.1 0.0 collective-permute-done.13.refs_3_
  49.1 5.2 %score.5 = (f32[6,192]{1,0:T(8,128)S(1)}, f32[6,192]{1,0:T(8,128)S(1)}) custom-call(s32[1]{0:T(128)} %bitcast.1.x_ref, bf16[208,1152]{1,0:T(8,128)(2,1)S(1)} %collective-permute-done.3.refs_0_, bf16[104,1152]{1,0:T(8,128)(2,1)S(1)} %collective-permute-done.8.refs_1_, bf16[104,1152]{1,0:T(8,128)(2,1)S(1)} %collective-permute-done.10.refs_2_, ...), custom_call_target="tpu_custom_call" | custom-call | flops 30000001024 | bytes 90000000 | tf_op jit(solution)/shard_map/score/pallas_call | solution.py:125
  54.3 0.0 copy-start.2
  54.3 0.6 copy-done.2
  54.9 3.2 %collective-permute-start.15 = (f32[6,192]{1,0:T(8,128)S(1)}, f32[6,192]{1,0:T(8,128)S(1)}, u32[]{:S(2)}, u32[]{:S(2)}) collective-permute-start(f32[6,192]{1,0:T(8,128)S(1)} %get-tuple-element.42), channel_id=1, source_target_pairs={{0,1},{1,0},{2,3},{3,2},{4,5},{5,4},{6,7},{7,6},{8,9},{9,8},{10,11... | collective-permute-start | bytes 13832 | tf_op jit(solution)/shard_map/ppermute | solution.py:177
  58.0 0.0 collective-permute-start.7
  58.1 1.2 %collective-permute-done.7.refs_1_ = f32[2,192]{1,0:T(2,128)S(1)} collective-permute-done((f32[2,192]{1,0:T(2,128)S(1)}, f32[2,192]{1,0:T(2,128)S(1)}, u32[]{:S(2)}, u32[]{:S(2)}) %collective-permute-start.7) | collective-permute-done | bytes 1568 | tf_op jit(solution)/shard_map/ppermute | solution.py:177
  59.2 0.0 copy-start.6
  59.2 0.0 collective-permute-done.15.refs_3_
  59.2 0.0 copy-start.5
  59.2 0.6 copy-done.6
  59.8 0.0 copy-done.5
  59.8 1.3 %place.1 = f32[16,192]{1,0:T(8,128)} custom-call(s32[1]{0:T(128)} %bitcast.me_ref, f32[2,192]{1,0:T(2,128)} %copy-done.3, f32[2,192]{1,0:T(2,128)} %copy-done.6, f32[6,192]{1,0:T(8,128)} %copy-done.2, f32[6,192]{1,0:T(8,128)} %copy-done.5), custom_call_target="tpu_custom_call" | custom-call | tf_op jit(solution)/shard_map/place/pallas_call | solution.py:155
  (3 shorter events, 0.0 us)
Async XLA Ops:
  0.0 20.3 %collective-permute-start.6 = (bf16[192,14336]{1,0:T(8,128)(2,1)}, bf16[192,14336]{1,0:T(8,128)(2,1)}, u32[]{:S(2)}, u32[]{:S(2)}) collective-permute-start(bf16[192,14336]{1,0:T(8,128)(2,1)} %refs_7_.3), channel_id=1, source_target_pairs={{0,1},{1,0},{2,3},{3,2},{4,5},{5,4},{6,7},{7,6},{8,9},{9,8},{10,11... | collective-permute-start | bytes 16515080 | tf_op jit(solution)/shard_map/ppermute | solution.py:177
  0.1 19.1 %collective-permute-start.5 = (bf16[192,4096]{1,0:T(8,128)(2,1)}, bf16[192,4096]{1,0:T(8,128)(2,1)S(1)}, u32[]{:S(2)}, u32[]{:S(2)}) collective-permute-start(bf16[192,4096]{1,0:T(8,128)(2,1)} %refs_6_.3), channel_id=1, source_target_pairs={{0,1},{1,0},{2,3},{3,2},{4,5},{5,4},{6,7},{7,6},{8,9},{9,8},{10,11... | collective-permute-start | bytes 4718600 | tf_op jit(solution)/shard_map/ppermute | solution.py:177
  0.5 1.0 %copy-start = (bf16[1,13,14336]{2,1,0:T(8,128)(2,1)S(1)}, bf16[1,13,14336]{2,1,0:T(8,128)(2,1)}, u32[]{:S(2)}) copy-start(bf16[1,13,14336]{2,1,0:T(8,128)(2,1)} %act_ref.3) | copy-start | bytes 1118212
  1.5 0.9 %copy-start.1 = (bf16[1,13,4096]{2,1,0:T(8,128)(2,1)S(1)}, bf16[1,13,4096]{2,1,0:T(8,128)(2,1)}, u32[]{:S(2)}) copy-start(bf16[1,13,4096]{2,1,0:T(8,128)(2,1)} %err_ref.3) | copy-start | bytes 319492
  2.4 17.9 %slice-start = ((s8[5505024]{0:T(1024)(128)(4,1)}), s8[4194304]{0:T(1024)(128)(4,1)S(1)}, s32[]{:S(2)}) async-start(s8[5505024]{0:T(1024)(128)(4,1)} %bitcast.2), calls=%async_computation | async-start | bytes 8388608
  2.8 17.6 %slice-start.1 = ((s8[5505024]{0:T(1024)(128)(4,1)}), s8[1310720]{0:T(1024)(128)(4,1)S(1)}, s32[]{:S(2)}) async-start(s8[5505024]{0:T(1024)(128)(4,1)} %bitcast.2), calls=%async_computation.1 | async-start | bytes 2621440
  2.8 17.6 %copy-start.4 = (bf16[192,4096]{1,0:T(8,128)(2,1)S(1)}, bf16[192,4096]{1,0:T(8,128)(2,1)}, u32[]{:S(2)}) copy-start(bf16[192,4096]{1,0:T(8,128)(2,1)} %refs_6_.3) | copy-start | bytes 4718596
  3.3 15.6 %collective-permute-start.4 = (bf16[208,1152]{1,0:T(8,128)(2,1)S(1)}, bf16[208,1152]{1,0:T(8,128)(2,1)S(1)}, u32[]{:S(2)}, u32[]{:S(2)}) collective-permute-start(bf16[208,1152]{1,0:T(8,128)(2,1)S(1)} %pack.3.refs_0_), channel_id=1, source_target_pairs={{0,2},{1,3},{2,0},{3,1},{4,6},{5,7},{6,4},{7,5},{8,10},{9,11},{10,... | collective-permute-start | bytes 1437704 | tf_op jit(solution)/shard_map/ppermute | solution.py:177
  5.6 8.6 %collective-permute-start = (bf16[104,1152]{1,0:T(8,128)(2,1)S(1)}, bf16[104,1152]{1,0:T(8,128)(2,1)S(1)}, u32[]{:S(2)}, u32[]{:S(2)}) collective-permute-start(bf16[104,1152]{1,0:T(8,128)(2,1)S(1)} %pack.2), channel_id=1, source_target_pairs={{0,12},{1,13},{2,14},{3,15},{4,8},{5,9},{6,10},{7,11},{8,4},{9,5},... | collective-permute-start | bytes 718856 | tf_op jit(solution)/shard_map/ppermute | solution.py:177
  8.9 19.5 %collective-permute-start.3 = (bf16[208,1152]{1,0:T(8,128)(2,1)S(1)}, bf16[208,1152]{1,0:T(8,128)(2,1)S(1)}, u32[]{:S(2)}, u32[]{:S(2)}) collective-permute-start(bf16[208,1152]{1,0:T(8,128)(2,1)S(1)} %pack.3.refs_0_), channel_id=1, source_target_pairs={{0,4},{1,5},{2,6},{3,7},{4,0},{5,1},{6,2},{7,3},{8,12},{9,13},{10,... | collective-permute-start | bytes 1437704 | tf_op jit(solution)/shard_map/ppermute | solution.py:177
  14.2 16.5 %collective-permute-start.1 = (bf16[104,1152]{1,0:T(8,128)(2,1)S(1)}, bf16[104,1152]{1,0:T(8,128)(2,1)S(1)}, u32[]{:S(2)}, u32[]{:S(2)}) collective-permute-start(bf16[104,1152]{1,0:T(8,128)(2,1)S(1)} %collective-permute-done.refs_4_), channel_id=1, source_target_pairs={{0,4},{1,5},{2,6},{3,7},{4,0},{5,1},{6,2},{7,3},{8,12},{9,13},{10,... | collective-permute-start | bytes 718856 | tf_op jit(solution)/shard_map/ppermute | solution.py:177
  18.9 11.8 %collective-permute-start.2 = (bf16[104,1152]{1,0:T(8,128)(2,1)S(1)}, bf16[104,1152]{1,0:T(8,128)(2,1)S(1)}, u32[]{:S(2)}, u32[]{:S(2)}) collective-permute-start(bf16[104,1152]{1,0:T(8,128)(2,1)S(1)} %collective-permute-done.refs_4_), channel_id=1, source_target_pairs={{0,2},{1,3},{2,0},{3,1},{4,6},{5,7},{6,4},{7,5},{8,10},{9,11},{10,... | collective-permute-start | bytes 718856 | tf_op jit(solution)/shard_map/ppermute | solution.py:177
  19.1 14.6 %collective-permute-start.9 = (bf16[104,1152]{1,0:T(8,128)(2,1)S(1)}, bf16[104,1152]{1,0:T(8,128)(2,1)S(1)}, u32[]{:S(2)}, u32[]{:S(2)}) collective-permute-start(bf16[104,1152]{1,0:T(8,128)(2,1)S(1)} %collective-permute-done.refs_4_), channel_id=1, source_target_pairs={{0,16},{1,17},{2,18},{3,19},{4,20},{5,21},{6,22},{7,23},{8,24},{9,... | collective-permute-start | bytes 718856 | tf_op jit(solution)/shard_map/ppermute | solution.py:177
  27.8 0.6 copy-start.3
  30.7 6.9 %collective-permute-start.10 = (bf16[104,1152]{1,0:T(8,128)(2,1)S(1)}, bf16[104,1152]{1,0:T(8,128)(2,1)S(1)}, u32[]{:S(2)}, u32[]{:S(2)}) collective-permute-start(bf16[104,1152]{1,0:T(8,128)(2,1)S(1)} %collective-permute-done.1.refs_2_), channel_id=1, source_target_pairs={{0,16},{1,17},{2,18},{3,19},{4,20},{5,21},{6,22},{7,23},{8,24},{9,... | collective-permute-start | bytes 718856 | tf_op jit(solution)/shard_map/ppermute | solution.py:177
  31.9 10.8 %collective-permute-start.11 = (bf16[104,1152]{1,0:T(8,128)(2,1)S(1)}, bf16[104,1152]{1,0:T(8,128)(2,1)S(1)}, u32[]{:S(2)}, u32[]{:S(2)}) collective-permute-start(bf16[104,1152]{1,0:T(8,128)(2,1)S(1)} %collective-permute-done.2.refs_5_), channel_id=1, source_target_pairs={{0,16},{1,17},{2,18},{3,19},{4,20},{5,21},{6,22},{7,23},{8,24},{9,... | collective-permute-start | bytes 718856 | tf_op jit(solution)/shard_map/ppermute | solution.py:177
  32.2 10.6 %collective-permute-start.12 = (bf16[104,1152]{1,0:T(8,128)(2,1)S(1)}, bf16[104,1152]{1,0:T(8,128)(2,1)S(1)}, u32[]{:S(2)}, u32[]{:S(2)}) collective-permute-start(bf16[104,1152]{1,0:T(8,128)(2,1)S(1)} %collective-permute-done.1.refs_2_), channel_id=1, source_target_pairs={{0,2},{1,3},{2,0},{3,1},{4,6},{5,7},{6,4},{7,5},{8,10},{9,11},{10,... | collective-permute-start | bytes 718856 | tf_op jit(solution)/shard_map/ppermute | solution.py:177
  32.4 11.5 %collective-permute-start.14 = (bf16[104,1152]{1,0:T(8,128)(2,1)S(1)}, bf16[104,1152]{1,0:T(8,128)(2,1)S(1)}, u32[]{:S(2)}, u32[]{:S(2)}) collective-permute-start(bf16[104,1152]{1,0:T(8,128)(2,1)S(1)} %slice.8), channel_id=1, source_target_pairs={{0,2},{1,3},{2,0},{3,1},{4,6},{5,7},{6,4},{7,5},{8,10},{9,11},{10,... | collective-permute-start | bytes 718856 | tf_op jit(solution)/shard_map/ppermute | solution.py:177
  33.8 15.3 %collective-permute-start.8 = (bf16[104,1152]{1,0:T(8,128)(2,1)S(1)}, bf16[104,1152]{1,0:T(8,128)(2,1)S(1)}, u32[]{:S(2)}, u32[]{:S(2)}) collective-permute-start(bf16[104,1152]{1,0:T(8,128)(2,1)S(1)} %slice.6), channel_id=1, source_target_pairs={{0,2},{1,3},{2,0},{3,1},{4,6},{5,7},{6,4},{7,5},{8,10},{9,11},{10,... | collective-permute-start | bytes 718856 | tf_op jit(solution)/shard_map/ppermute | solution.py:177
  42.7 6.3 %collective-permute-start.13 = (bf16[104,1152]{1,0:T(8,128)(2,1)S(1)}, bf16[104,1152]{1,0:T(8,128)(2,1)S(1)}, u32[]{:S(2)}, u32[]{:S(2)}) collective-permute-start(bf16[104,1152]{1,0:T(8,128)(2,1)S(1)} %collective-permute-done.12.refs_3_), channel_id=1, source_target_pairs={{0,16},{1,17},{2,18},{3,19},{4,20},{5,21},{6,22},{7,23},{8,24},{9,... | collective-permute-start | bytes 718856 | tf_op jit(solution)/shard_map/ppermute | solution.py:177
  54.3 0.6 copy-start.2
  54.9 4.4 %collective-permute-start.15 = (f32[6,192]{1,0:T(8,128)S(1)}, f32[6,192]{1,0:T(8,128)S(1)}, u32[]{:S(2)}, u32[]{:S(2)}) collective-permute-start(f32[6,192]{1,0:T(8,128)S(1)} %get-tuple-element.42), channel_id=1, source_target_pairs={{0,1},{1,0},{2,3},{3,2},{4,5},{5,4},{6,7},{7,6},{8,9},{9,8},{10,11... | collective-permute-start | bytes 13832 | tf_op jit(solution)/shard_map/ppermute | solution.py:177
  58.0 1.2 %collective-permute-start.7 = (f32[2,192]{1,0:T(2,128)S(1)}, f32[2,192]{1,0:T(2,128)S(1)}, u32[]{:S(2)}, u32[]{:S(2)}) collective-permute-start(f32[2,192]{1,0:T(2,128)S(1)} %get-tuple-element.28), channel_id=1, source_target_pairs={{0,1},{1,0},{2,3},{3,2},{4,5},{5,4},{6,7},{7,6},{8,9},{9,8},{10,11... | collective-permute-start | bytes 4616 | tf_op jit(solution)/shard_map/ppermute | solution.py:177
  59.2 0.6 copy-start.6
  59.2 0.6 copy-start.5

commit v3 on v0

v3 whole, which is shorter than its diff:
```python
import functools

import jax
import jax.numpy as jnp
from jax import lax
from jax.experimental import pallas as pl
from jax.experimental.pallas import tpu as pltpu
from jax.sharding import PartitionSpec as P

AXES = ("grp", "blk")
NT = (((1,), (1,)), ((), ()))
RANK = 13
SEGS = 16
ROWS = 16
CUTS = (1, 4)
AHEAD = 10
LIMIT = 16 << 20
TICK = 8
PACK = 30


def project_rows(err_rows, act_rows, err_piece, act_piece):
    err_proj = jnp.einsum("td,qrd->qrt", err_rows, err_piece, preferred_element_type=jnp.float32)
    act_proj = jnp.einsum("tf,qrf->qrt", act_rows, act_piece, preferred_element_type=jnp.float32)
    return (err_proj, act_proj)


def gathered(activations, errors, err_factors, act_factors):
    err_width = errors.shape[1]
    joined = jnp.concatenate((err_factors, act_factors), axis=2)
    piece = lax.all_gather(joined, "blk", axis=0, tiled=True)
    err_proj, act_proj = project_rows(
        errors, activations, piece[:, :, :err_width], piece[:, :, err_width:]
    )
    return jnp.sum(err_proj * act_proj, axis=1)


def picks(shape, stacked_dim):
    stacked = lax.broadcasted_iota(jnp.int32, shape, stacked_dim)
    packed = lax.broadcasted_iota(jnp.int32, shape, 1 - stacked_dim)
    m, r = stacked >> 4, stacked & 15
    return ((r < RANK) & (packed == RANK * m + r)).astype(jnp.bfloat16)


def pack_kernel(x_ref, err_hbm, act_hbm, half_ref, runs, err_ref, act_ref, sems):
    ew, aw = err_ref.shape[2] // SEGS, act_ref.shape[2] // SEGS
    n = SEGS // 2
    copies = [
        pltpu.make_async_copy(err_hbm, err_ref, sems.at[0]),
        pltpu.make_async_copy(act_hbm, act_ref, sems.at[1]),
    ]
    for copy in copies:
        copy.start()
    runs[...] = jnp.zeros_like(runs)
    for copy in copies:
        copy.wait()
    for s in range(SEGS):
        runs[s // n, s % n * ROWS : s % n * ROWS + RANK, :ew] = err_ref[0, :, s * ew : (s + 1) * ew]
        runs[s // n, s % n * ROWS : s % n * ROWS + RANK, ew:] = act_ref[0, :, s * aw : (s + 1) * aw]
    pick = picks((half_ref.shape[0], n * ROWS), 1)
    half = jnp.dot(pick, runs[x_ref[0]], preferred_element_type=jnp.float32)
    half_ref[...] = half.astype(jnp.bfloat16)


def pack(x, err, act):
    width = (err.shape[2] + act.shape[2]) // SEGS
    n = SEGS // 2
    vmem, hbm = pl.BlockSpec(memory_space=pltpu.VMEM), pl.BlockSpec(memory_space=pltpu.HBM)
    return pl.pallas_call(
        pack_kernel,
        out_shape=(
            jax.ShapeDtypeStruct((n * RANK, width), jnp.bfloat16),
            jax.ShapeDtypeStruct((2, n * ROWS, width), jnp.bfloat16),
        ),
        in_specs=[pl.BlockSpec(memory_space=pltpu.SMEM), hbm, hbm],
        out_specs=(vmem, vmem),
        scratch_shapes=[
            pltpu.VMEM(err.shape, err.dtype),
            pltpu.VMEM(act.shape, act.dtype),
            pltpu.SemaphoreType.DMA((2,)),
        ],
        compiler_params=pltpu.CompilerParams(vmem_limit_bytes=LIMIT),
        name="pack",
    )(x, err, act)


def again_kernel(x_ref, runs, half_ref, rest_ref):
    n = SEGS // 2
    pick = picks((half_ref.shape[0], n * ROWS), 1)
    for h, out_ref in ((x_ref[0], half_ref), (1 - x_ref[0], rest_ref)):
        half = jnp.dot(pick, runs[h], preferred_element_type=jnp.float32)
        out_ref[...] = half.astype(jnp.bfloat16)


def pack_again(x, runs):
    vmem = pl.BlockSpec(memory_space=pltpu.VMEM)
    out = jax.ShapeDtypeStruct((SEGS // 2 * RANK, runs.shape[2]), jnp.bfloat16)
    return pl.pallas_call(
        again_kernel,
        out_shape=(out, out),
        in_specs=[pl.BlockSpec(memory_space=pltpu.SMEM), vmem],
        out_specs=(vmem, vmem),
        compiler_params=pltpu.CompilerParams(vmem_limit_bytes=LIMIT),
        cost_estimate=weight(PACK),
        name="pack_again",
    )(x, runs)


def weight(us):
    return pl.CostEstimate(flops=int(us * 1e9), bytes_accessed=int(us * 3e6), transcendentals=0)


def unpack(piece, out_ref, at, ew):
    n = SEGS // 2
    aw = piece.shape[1] - ew
    pick = picks((n * ROWS, piece.shape[0]), 0)
    runs = jnp.dot(pick, piece[...], preferred_element_type=jnp.float32).astype(jnp.bfloat16)
    for s in range(n):
        run = runs[s * ROWS : (s + 1) * ROWS]
        out_ref[at : at + ROWS, s * ew : (s + 1) * ew] = run[:, :ew]
        out_ref[at : at + ROWS, n * ew + s * aw : n * ew + (s + 1) * aw] = run[:, ew:]


def gate_kernel(*refs):
    pass


def gate(*arrays):
    hbm = pl.BlockSpec(memory_space=pl.ANY)
    return pl.pallas_call(
        gate_kernel,
        out_shape=tuple(jax.ShapeDtypeStruct(a.shape, a.dtype) for a in arrays),
        in_specs=[hbm] * len(arrays),
        out_specs=(hbm,) * len(arrays),
        input_output_aliases={i: i for i in range(len(arrays))},
        compiler_params=pltpu.CompilerParams(vmem_limit_bytes=1 << 20),
        cost_estimate=weight(TICK),
        name="gate",
    )(*arrays)


def fetch(half, tokens, buffers, sems):
    jobs = []
    for j in range(4):
        width, side = buffers[j].shape[1], j % 2
        start = side * buffers[0].shape[1]
        cut = width // CUTS[side]
        for i in range(CUTS[side]):
            at = pl.ds(pl.multiple_of(half * width + i * cut, cut), cut)
            copy = pltpu.make_async_copy(
                tokens[j].at[:, at], buffers[j].at[:, pl.ds(i * cut, cut)], sems.at[len(jobs)]
            )
            jobs.append((copy, j, i * cut, start + i * cut, cut))
    for job in jobs[:AHEAD]:
        job[0].start()
    return jobs


def project(rows, jobs, buffers):
    sums = [None] * 4
    for i, (copy, j, first, start, cut) in enumerate(jobs):
        copy.wait()
        if i + AHEAD < len(jobs):
            jobs[i + AHEAD][0].start()
        term = lax.dot_general(
            rows[:, start : start + cut], buffers[j][:, first : first + cut], NT,
            preferred_element_type=jnp.float32,
        )
        sums[j] = term if sums[j] is None else sums[j] + term
    return sums


def half_scratch(tokens):
    return [pltpu.VMEM((a.shape[0], a.shape[1] // 2), a.dtype) for a in tokens] + [
        pltpu.SemaphoreType.DMA((2 * sum(CUTS),))
    ]


def unpack_kernel(now, later, ew, *refs):
    pieces, (now_ref, later_ref) = refs[:-2], refs[-2:]
    for out_ref, parts in ((now_ref, now), (later_ref, later)):
        for i, p in enumerate(parts):
            unpack(pieces[p], out_ref, i * ROWS, ew)


def unpacked(pieces, now, later, ew):
    vmem = pl.BlockSpec(memory_space=pltpu.VMEM)
    width = SEGS // 2 * pieces[0].shape[1]
    return pl.pallas_call(
        functools.partial(unpack_kernel, now, later, ew),
        out_shape=tuple(
            jax.ShapeDtypeStruct((len(p) * ROWS, width), jnp.bfloat16) for p in (now, later)
        ),
        in_specs=[vmem] * len(pieces),
        out_specs=(vmem, vmem),
        compiler_params=pltpu.CompilerParams(vmem_limit_bytes=LIMIT),
        cost_estimate=weight(TICK),
        name="unpacked",
    )(*pieces)


def first_kernel(now, later, n_pieces, x_ref, rows_ref, *refs):
    pieces, refs = refs[:n_pieces], refs[n_pieces:]
    tokens, accs, (later_ref, rows, *buffers, sems) = refs[:4], refs[4:8], refs[8:]
    jobs = fetch(x_ref[0], tokens, buffers, sems)
    ew, n = tokens[0].shape[1] // SEGS, rows_ref.shape[0]
    rows[:n] = rows_ref[...]
    for i, p in enumerate(now):
        unpack(pieces[p], rows, n + i * ROWS, ew)
    for acc, v in zip(accs, project(rows, jobs, buffers)):
        acc[...] = v
    for i, p in enumerate(later):
        unpack(pieces[p], later_ref, i * ROWS, ew)


def first_half(x, rows, pieces, now, later, tokens):
    vmem, hbm = pl.BlockSpec(memory_space=pltpu.VMEM), pl.BlockSpec(memory_space=pltpu.HBM)
    n, width = rows.shape[0] + len(now) * ROWS, rows.shape[1]
    acc = jax.ShapeDtypeStruct((n, tokens[0].shape[0]), jnp.float32)
    return pl.pallas_call(
        functools.partial(first_kernel, now, later, len(pieces)),
        out_shape=(acc,) * 4
        + (jax.ShapeDtypeStruct((len(later) * ROWS, width), jnp.bfloat16),),
        in_specs=[pl.BlockSpec(memory_space=pltpu.SMEM)] + [vmem] * (len(pieces) + 1) + [hbm] * 4,
        out_specs=(vmem,) * 5,
        scratch_shapes=[pltpu.VMEM((n, width), jnp.bfloat16)] + half_scratch(tokens),
        compiler_params=pltpu.CompilerParams(vmem_limit_bytes=LIMIT),
        cost_estimate=weight(12),
        name="first_half",
    )(x, rows, *pieces, *tokens)


def second_kernel(order, n_pieces, x_ref, me_ref, rows_a, rows_b, *refs):
    pieces, refs = refs[:n_pieces], refs[n_pieces:]
    tokens, accs = refs[:4], refs[4:8]
    own_ref, mate_ref, rows, *buffers, sems = refs[8:]
    jobs = fetch(1 - x_ref[0], tokens, buffers, sems)
    n, m = rows_a.shape[0], rows_a.shape[0] + rows_b.shape[0]
    rows[:n], rows[n:m] = rows_a[...], rows_b[...]
    for i, piece in enumerate(pieces):
        unpack(piece, rows, m + i * ROWS, tokens[0].shape[1] // SEGS)
    me = me_ref[0]
    sums = [v + acc[...] for v, acc in zip(project(rows, jobs, buffers), accs)]
    for j, out_ref in enumerate((own_ref, mate_ref)):
        prod = sums[2 * j] * sums[2 * j + 1]
        out_ref[...] = jnp.zeros_like(out_ref)
        for b, flip in enumerate(order):
            row = jnp.sum(prod[b * ROWS : (b + 1) * ROWS], axis=0, keepdims=True)
            out_ref[pl.ds(jnp.bitwise_xor(me, flip), 1), :] = row


def second_half(x, me, order, rows_a, rows_b, pieces, tokens, accs):
    vmem, smem = pl.BlockSpec(memory_space=pltpu.VMEM), pl.BlockSpec(memory_space=pltpu.SMEM)
    hbm = pl.BlockSpec(memory_space=pltpu.HBM)
    out = jax.ShapeDtypeStruct((2 * len(order), tokens[0].shape[0]), jnp.float32)
    return pl.pallas_call(
        functools.partial(second_kernel, order, len(pieces)),
        out_shape=(out, out),
        in_specs=[smem, smem] + [vmem] * (2 + len(pieces)) + [hbm] * 4 + [vmem] * 4,
        out_specs=(vmem, vmem),
        scratch_shapes=[pltpu.VMEM((len(order) * ROWS, rows_a.shape[1]), jnp.bfloat16)]
        + half_scratch(tokens),
        compiler_params=pltpu.CompilerParams(vmem_limit_bytes=LIMIT),
        cost_estimate=weight(10),
        name="second_half",
    )(x, me, rows_a, rows_b, *pieces, *tokens, *accs)


def pairs(n_grp, n_blk, flip_grp, flip_blk):
    return [
        (g * n_blk + b, (g ^ flip_grp) * n_blk + (b ^ flip_blk))
        for g in range(n_grp)
        for b in range(n_blk)
    ]


def in_hbm(a):
    return pltpu.with_memory_space_constraint(a, pltpu.HBM)


def permuted(n_grp, n_blk, activations, errors, err_factors, act_factors):
    swap = lambda a, gx, bx: lax.ppermute(a, AXES, pairs(n_grp, n_blk, gx, bx))
    over_x = lambda a: swap(a, 1, 0)
    over_y = lambda a: swap(a, 0, 2)
    over_z = lambda a, k: swap(a, 0, 4 * k)
    mate = lambda a: swap(a, 0, 1)
    x = lax.axis_index("grp").astype(jnp.int32).reshape(1)
    me = lax.axis_index("blk").astype(jnp.int32).reshape(1)

    mate_acts, mate_errs = mate(activations), mate(errors)
    half, runs = pack(x, in_hbm(err_factors), in_hbm(act_factors))
    z3 = over_z(half, 3)
    half, rest = pack_again(x, runs)
    y0, z1, y0r = over_y(half), over_z(half, 1), over_y(rest)
    z3, z1, y0, y0r, rest, mate_acts = gate(z3, z1, y0, y0r, rest, mate_acts)
    z2, y3, xa3 = over_z(z3, 1), over_y(z3), over_x(z3)
    y1, y1r = over_y(z1), over_z(y0r, 1)
    z2, y3, xa3, rest = gate(z2, y3, xa3, rest)
    y2, xa2, xb3 = over_y(z2), over_x(z2), over_x(y3)
    z1r = over_z(rest, 1)
    mine, others = unpacked(
        (half, y0, z3, z1, y1, z2, y3, rest, y0r, xa3), tuple(range(7)), (7, 8, 9),
        errors.shape[1] // SEGS,
    )
    xb2 = over_x(y2)

    tokens = tuple(in_hbm(a) for a in (errors, activations, mate_errs, mate_acts))
    *accs, late = first_half(x, mine, (y2, z1r, y1r), (0,), (1, 2), tokens)
    order = (0, 2, 12, 4, 6, 8, 14, 10)
    own, mates = second_half(x, me, order, others, late, (xa2, xb3, xb2), tokens, accs)
    return own + mate(mates)


def solution(mesh):
    in_specs = (
        P(("grp", "blk"), None),
        P(("grp", "blk"), None),
        P("blk", None, None),
        P("blk", None, None),
    )
    out_specs = P(None, ("grp", "blk"))
    n_grp, n_blk = mesh.shape["grp"], mesh.shape["blk"]
    body = gathered
    if (n_grp, n_blk) == (2, 16):
        body = functools.partial(permuted, n_grp, n_blk)
    return jax.shard_map(body, mesh=mesh, in_specs=in_specs, out_specs=out_specs, check_vma=False)
```

time: 114 us -> 54.9 us (0.48)
  waiting for transfers between devices: 85 us -> 21.5 us
  starting transfers between devices: 0.01 us -> 17.9 us
  Pallas kernels: 0 us -> 14.3 us
  between operations: 13.4 us -> 0.08 us
  matrix products: 8.61 us -> 0 us
  local copies, waits for them, and re-layouts: 4.66 us -> 0 us
  other arithmetic: 2.03 us -> 0.61 us
    all_gather x1 -> x0, waiting for transfers between devices: 85 us -> none  [local(): piece = lax.all_gather(joined, 'blk', axis=0, tiled=True)]
    ppermute x0 -> x17, waiting for transfers between devices: none -> 21.5 us  [permuted(): swap = lambda a, gx, bx: lax.ppermute(a, AXES, pairs(n_grp, n_blk, gx, bx))]
    ppermute x0 -> x17, starting transfers between devices: none -> 17.9 us  [permuted(): swap = lambda a, gx, bx: lax.ppermute(a, AXES, pairs(n_grp, n_blk, gx, bx))]
    pallas_call x0 -> x7, Pallas kernels: none -> 14.3 us  [the longest x1 5.92 us: second_half(): pl.pallas_call(functools.partial(second_kernel, order, len(pieces)), out_...]
    dot_general x2 -> x0, matrix products: 8.61 us -> none  [the longest x1 6.72 us: project_rows(): jnp.einsum('tf,qrf->qrt', act_rows, act_piece, preferred_element_type=jnp...]
    slice x4 -> x0, local copies, waits for them, and re-layouts: 4.66 us -> none  [the longest x2 3.08 us: local(): piece[:, :, err_width:]]
    concatenate x1 -> x0, other arithmetic: 2.03 us -> none  [local(): joined = jnp.concatenate((err_factors, act_factors), axis=2)]
  transfers between devices with their start and end apart: 1 -> 17, of which waited for: 1 -> 11; matrix products, arithmetic and copies ran while one was open for 0% -> 0% of each run, Pallas kernels for 0% -> 15%
where the time goes in v3:
time: 54.9 us; the launch traced here: 54.4 us
  waiting for transfers between devices  21.5 us (39%)
  starting transfers between devices  17.9 us (33%)
  Pallas kernels  14.3 us (26%)
  other arithmetic  0.61 us (1%)
    ppermute x17, waiting for transfers between devices, permuted(): swap = lambda a, gx, bx: lax.ppermute(a, AXES, pairs(n_grp, n_blk, gx, bx))  21.5 us
    ppermute x17, starting transfers between devices, permuted(): swap = lambda a, gx, bx: lax.ppermute(a, AXES, pairs(n_grp, n_blk, gx, bx))  17.9 us
    pallas_call x1, Pallas kernels, second_half(): pl.pallas_call(functools.partial(second_kernel, order, len(pieces)), out_...  5.92 us
    pallas_call x1, Pallas kernels, first_half(): pl.pallas_call(functools.partial(first_kernel, now, later, len(pieces)),...  5.81 us
    pallas_call x1, Pallas kernels, pack(): pl.pallas_call(pack_kernel, out_shape=(jax.ShapeDtypeStruct((n * RANK, wi...  1.39 us
  transfers between devices with their start and end apart: 17, of which 11 were waited for; matrix products, arithmetic and copies ran while one was open for 0% of the time, Pallas kernels for 15%

profile of v3, /device:TPU:1, one launch (start us, length us, event | category | flops | bytes accessed | tf_op | source)
XLA Modules:
  0.0 54.4 jit_solution(5449823096732450577)
XLA Ops:
  0.0 0.1 collective-permute-start.4
  0.1 1.4 %pack.1 = (bf16[104,1152]{1,0:T(8,128)(2,1)S(1)}, bf16[2,128,1152]{2,1,0:T(8,128)(2,1)S(1)}) custom-call(s32[1]{0:T(128)} %bitcast.x_ref, bf16[1,13,4096]{2,1,0:T(8,128)(2,1)} %err_hbm.1, bf16[1,13,14336]{2,1,0:T(8,128)(2,1)} %act_hbm.1), custom_call_target="tpu_custom_call" | custom-call | tf_op jit(solution)/shard_map/pack/pallas_call | solution.py:69
  1.5 0.3 pack_again.1
  1.8 2.8 %collective-permute-start.1 = (bf16[104,1152]{1,0:T(8,128)(2,1)S(1)}, bf16[104,1152]{1,0:T(8,128)(2,1)S(1)}, u32[]{:S(2)}, u32[]{:S(2)}) collective-permute-start(bf16[104,1152]{1,0:T(8,128)(2,1)S(1)} %get-tuple-element.29.refs_0_), channel_id=1, source_target_pairs={{0,4},{1,5},{2,6},{3,7},{4,0},{5,1},{6,2},{7,3},{8,12},{9,13},{10,... | collective-permute-start | bytes 718856 | tf_op jit(solution)/shard_map/ppermute | solution.py:282
  4.6 1.2 %collective-permute-start.2 = (bf16[104,1152]{1,0:T(8,128)(2,1)S(1)}, bf16[104,1152]{1,0:T(8,128)(2,1)S(1)}, u32[]{:S(2)}, u32[]{:S(2)}) collective-permute-start(bf16[104,1152]{1,0:T(8,128)(2,1)S(1)} %get-tuple-element.29.refs_0_), channel_id=1, source_target_pairs={{0,2},{1,3},{2,0},{3,1},{4,6},{5,7},{6,4},{7,5},{8,10},{9,11},{10,... | collective-permute-start | bytes 718856 | tf_op jit(solution)/shard_map/ppermute | solution.py:282
  5.8 0.2 collective-permute-start.3
  6.0 2.2 %collective-permute-start = (bf16[104,1152]{1,0:T(8,128)(2,1)S(1)}, bf16[104,1152]{1,0:T(8,128)(2,1)S(1)}, u32[]{:S(2)}, u32[]{:S(2)}) collective-permute-start(bf16[104,1152]{1,0:T(8,128)(2,1)S(1)} %get-tuple-element.30), channel_id=1, source_target_pairs={{0,12},{1,13},{2,14},{3,15},{4,8},{5,9},{6,10},{7,11},{8,4},{9,5},... | collective-permute-start | bytes 718856 | tf_op jit(solution)/shard_map/ppermute | solution.py:282
  8.2 2.5 %collective-permute-done.1.refs_1_ = bf16[104,1152]{1,0:T(8,128)(2,1)S(1)} collective-permute-done((bf16[104,1152]{1,0:T(8,128)(2,1)S(1)}, bf16[104,1152]{1,0:T(8,128)(2,1)S(1)}, u32[]{:S(2)}, u32[]{:S(2)}) %collective-permute-start.1) | collective-permute-done | bytes 239648 | tf_op jit(solution)/shard_map/ppermute | solution.py:282
  10.8 0.9 %collective-permute-done.2.refs_2_ = bf16[104,1152]{1,0:T(8,128)(2,1)S(1)} collective-permute-done((bf16[104,1152]{1,0:T(8,128)(2,1)S(1)}, bf16[104,1152]{1,0:T(8,128)(2,1)S(1)}, u32[]{:S(2)}, u32[]{:S(2)}) %collective-permute-start.2) | collective-permute-done | bytes 239648 | tf_op jit(solution)/shard_map/ppermute | solution.py:282
  11.7 5.1 %collective-permute-done.3.refs_3_ = bf16[104,1152]{1,0:T(8,128)(2,1)S(1)} collective-permute-done((bf16[104,1152]{1,0:T(8,128)(2,1)S(1)}, bf16[104,1152]{1,0:T(8,128)(2,1)S(1)}, u32[]{:S(2)}, u32[]{:S(2)}) %collective-permute-start.3) | collective-permute-done | bytes 239648 | tf_op jit(solution)/shard_map/ppermute | solution.py:282
  16.8 1.1 %collective-permute-done.refs_0_ = bf16[104,1152]{1,0:T(8,128)(2,1)S(1)} collective-permute-done((bf16[104,1152]{1,0:T(8,128)(2,1)S(1)}, bf16[104,1152]{1,0:T(8,128)(2,1)S(1)}, u32[]{:S(2)}, u32[]{:S(2)}) %collective-permute-start) | collective-permute-done | bytes 239648 | tf_op jit(solution)/shard_map/ppermute | solution.py:282
  17.9 0.0 collective-permute-done.4.refs_5_
  18.0 1.2 %collective-permute-start.6 = (bf16[104,1152]{1,0:T(8,128)(2,1)S(1)}, bf16[104,1152]{1,0:T(8,128)(2,1)S(1)}, u32[]{:S(2)}, u32[]{:S(2)}) collective-permute-start(bf16[104,1152]{1,0:T(8,128)(2,1)S(1)} %get-tuple-element.33.refs_2_), channel_id=1, source_target_pairs={{0,4},{1,5},{2,6},{3,7},{4,0},{5,1},{6,2},{7,3},{8,12},{9,13},{10,... | collective-permute-start | bytes 718856 | tf_op jit(solution)/shard_map/ppermute | solution.py:282
  19.1 1.2 %collective-permute-start.7 = (bf16[104,1152]{1,0:T(8,128)(2,1)S(1)}, bf16[104,1152]{1,0:T(8,128)(2,1)S(1)}, u32[]{:S(2)}, u32[]{:S(2)}) collective-permute-start(bf16[104,1152]{1,0:T(8,128)(2,1)S(1)} %get-tuple-element.33.refs_2_), channel_id=1, source_target_pairs={{0,2},{1,3},{2,0},{3,1},{4,6},{5,7},{6,4},{7,5},{8,10},{9,11},{10,... | collective-permute-start | bytes 718856 | tf_op jit(solution)/shard_map/ppermute | solution.py:282
  20.4 1.2 %collective-permute-start.8 = (bf16[104,1152]{1,0:T(8,128)(2,1)S(1)}, bf16[104,1152]{1,0:T(8,128)(2,1)S(1)}, u32[]{:S(2)}, u32[]{:S(2)}) collective-permute-start(bf16[104,1152]{1,0:T(8,128)(2,1)S(1)} %get-tuple-element.33.refs_2_), channel_id=1, source_target_pairs={{0,16},{1,17},{2,18},{3,19},{4,20},{5,21},{6,22},{7,23},{8,24},{9,... | collective-permute-start | bytes 718856 | tf_op jit(solution)/shard_map/ppermute | solution.py:282
  21.6 2.3 %collective-permute-start.12 = (bf16[192,4096]{1,0:T(8,128)(2,1)}, bf16[192,4096]{1,0:T(8,128)(2,1)}, u32[]{:S(2)}, u32[]{:S(2)}) collective-permute-start(bf16[192,4096]{1,0:T(8,128)(2,1)} %refs_3_.3), channel_id=1, source_target_pairs={{0,1},{1,0},{2,3},{3,2},{4,5},{5,4},{6,7},{7,6},{8,9},{9,8},{10,11... | collective-permute-start | bytes 4718600 | tf_op jit(solution)/shard_map/ppermute | solution.py:282
  23.8 0.2 collective-permute-start.5
  24.1 0.4 collective-permute-done.6.refs_0_
  24.4 0.6 %collective-permute-start.11 = (bf16[104,1152]{1,0:T(8,128)(2,1)S(1)}, bf16[104,1152]{1,0:T(8,128)(2,1)S(1)}, u32[]{:S(2)}, u32[]{:S(2)}) collective-permute-start(bf16[104,1152]{1,0:T(8,128)(2,1)S(1)} %get-tuple-element.39.refs_8_), channel_id=1, source_target_pairs={{0,4},{1,5},{2,6},{3,7},{4,0},{5,1},{6,2},{7,3},{8,12},{9,13},{10,... | collective-permute-start | bytes 718856 | tf_op jit(solution)/shard_map/ppermute | solution.py:282
  25.0 0.0 collective-permute-done.7.refs_1_
  25.0 0.7 %collective-permute-done.8.refs_2_ = bf16[104,1152]{1,0:T(8,128)(2,1)S(1)} collective-permute-done((bf16[104,1152]{1,0:T(8,128)(2,1)S(1)}, bf16[104,1152]{1,0:T(8,128)(2,1)S(1)}, u32[]{:S(2)}, u32[]{:S(2)}) %collective-permute-start.8) | collective-permute-done | bytes 239648 | tf_op jit(solution)/shard_map/ppermute | solution.py:282
  25.7 0.6 %collective-permute-start.9 = (bf16[104,1152]{1,0:T(8,128)(2,1)S(1)}, bf16[104,1152]{1,0:T(8,128)(2,1)S(1)}, u32[]{:S(2)}, u32[]{:S(2)}) collective-permute-start(bf16[104,1152]{1,0:T(8,128)(2,1)S(1)} %get-tuple-element.36.refs_5_), channel_id=1, source_target_pairs={{0,2},{1,3},{2,0},{3,1},{4,6},{5,7},{6,4},{7,5},{8,10},{9,11},{10,... | collective-permute-start | bytes 718856 | tf_op jit(solution)/shard_map/ppermute | solution.py:282
  26.3 1.2 %collective-permute-start.13 = (bf16[104,1152]{1,0:T(8,128)(2,1)S(1)}, bf16[104,1152]{1,0:T(8,128)(2,1)S(1)}, u32[]{:S(2)}, u32[]{:S(2)}) collective-permute-start(bf16[104,1152]{1,0:T(8,128)(2,1)S(1)} %get-tuple-element.36.refs_5_), channel_id=1, source_target_pairs={{0,16},{1,17},{2,18},{3,19},{4,20},{5,21},{6,22},{7,23},{8,24},{9,... | collective-permute-start | bytes 718856 | tf_op jit(solution)/shard_map/ppermute | solution.py:282
  27.5 4.3 %collective-permute-done.5.refs_4_ = bf16[104,1152]{1,0:T(8,128)(2,1)S(1)} collective-permute-done((bf16[104,1152]{1,0:T(8,128)(2,1)S(1)}, bf16[104,1152]{1,0:T(8,128)(2,1)S(1)}, u32[]{:S(2)}, u32[]{:S(2)}) %collective-permute-start.5) | collective-permute-done | bytes 239648 | tf_op jit(solution)/shard_map/ppermute | solution.py:282
  31.8 0.0 collective-permute-start.10
  31.8 0.9 %unpacked.1 = (bf16[112,9216]{1,0:T(8,128)(2,1)S(1)}, bf16[48,9216]{1,0:T(8,128)(2,1)S(1)}) custom-call(bf16[104,1152]{1,0:T(8,128)(2,1)S(1)} %get-tuple-element.29.refs_0_, bf16[104,1152]{1,0:T(8,128)(2,1)S(1)} %get-tuple-element.32.refs_1_, bf16[104,1152]{1,0:T(8,128)(2,1)S(1)} %get-tuple-element.33.refs_2_, ...), custom_call_target="tpu_custom_call" | custom-call | flops 8000000000 | bytes 24000000 | tf_op jit(solution)/shard_map/unpacked/pallas_call | solution.py:189
  32.7 0.0 collective-permute-done.12.refs_5_
  32.7 0.3 collective-permute-start.14
  33.0 3.9 %collective-permute-done.9.refs_0_ = bf16[104,1152]{1,0:T(8,128)(2,1)S(1)} collective-permute-done((bf16[104,1152]{1,0:T(8,128)(2,1)S(1)}, bf16[104,1152]{1,0:T(8,128)(2,1)S(1)}, u32[]{:S(2)}, u32[]{:S(2)}) %collective-permute-start.9) | collective-permute-done | bytes 239648 | tf_op jit(solution)/shard_map/ppermute | solution.py:282
  36.9 0.3 collective-permute-start.15
  37.1 0.0 collective-permute-done.11.refs_2_
  37.1 0.8 %collective-permute-done.10.refs_1_ = bf16[104,1152]{1,0:T(8,128)(2,1)S(1)} collective-permute-done((bf16[104,1152]{1,0:T(8,128)(2,1)S(1)}, bf16[104,1152]{1,0:T(8,128)(2,1)S(1)}, u32[]{:S(2)}, u32[]{:S(2)}) %collective-permute-start.10) | collective-permute-done | bytes 239648 | tf_op jit(solution)/shard_map/ppermute | solution.py:282
  37.9 5.8 %first_half.1 = (f32[128,192]{1,0:T(8,128)S(1)}, f32[128,192]{1,0:T(8,128)S(1)}, f32[128,192]{1,0:T(8,128)S(1)}, f32[128,192]{1,0:T(8,128)S(1)}, bf16[32,9216]{1,0:T(8,128)(2,1)S(1)}) custom-call(s32[1]{0:T(128)} %bitcast.x_ref, bf16[112,9216]{1,0:T(8,128)(2,1)S(1)} %get-tuple-element.42.rows_ref, bf16[104,1152]{1,0:T(8,128)(2,1)S(1)} %collective-permute-done.9.refs_0_, ...), custom_call_target="tpu_custom_call" | custom-call | flops 12000000000 | bytes 36000000 | tf_op jit(solution)/shard_map/first_half/pallas_call | solution.py:220
  43.7 0.0 collective-permute-done.13.refs_0_
  43.7 0.0 collective-permute-done.14.refs_1_
  43.7 1.0 %collective-permute-done.15.refs_2_ = bf16[104,1152]{1,0:T(8,128)(2,1)S(1)} collective-permute-done((bf16[104,1152]{1,0:T(8,128)(2,1)S(1)}, bf16[104,1152]{1,0:T(8,128)(2,1)S(1)}, u32[]{:S(2)}, u32[]{:S(2)}) %collective-permute-start.15) | collective-permute-done | bytes 239648 | tf_op jit(solution)/shard_map/ppermute | solution.py:282
  44.8 5.9 %second_half.1 = (f32[16,192]{1,0:T(8,128)S(1)}, f32[16,192]{1,0:T(8,128)S(1)}) custom-call(s32[1]{0:T(128)} %bitcast.x_ref, s32[1]{0:T(128)} %bitcast.1.me_ref, bf16[48,9216]{1,0:T(8,128)(2,1)S(1)} %get-tuple-element.41.rows_a, bf16[32,9216]{1,0:T(8,128)(2,1)S(1)} %get-tuple-element.44.rows_b, bf16[104,1152]{1,0:T(8,128)(2,1)S(1)} %collective-permute-done.13.refs_0_, ...), custom_call_target="tpu_custom_call" | custom-call | flops 10000000000 | bytes 30000000 | tf_op jit(solution)/shard_map/second_half/pallas_call | solution.py:256
  50.7 2.3 %collective-permute-start.16 = (f32[16,192]{1,0:T(8,128)S(1)}, f32[16,192]{1,0:T(8,128)S(1)}, u32[]{:S(2)}, u32[]{:S(2)}) collective-permute-start(f32[16,192]{1,0:T(8,128)S(1)} %get-tuple-element.50), channel_id=1, source_target_pairs={{0,1},{1,0},{2,3},{3,2},{4,5},{5,4},{6,7},{7,6},{8,9},{9,8},{10,11... | collective-permute-start | bytes 36872 | tf_op jit(solution)/shard_map/ppermute | solution.py:282
  53.0 0.8 %collective-permute-done.16 = f32[16,192]{1,0:T(8,128)S(1)} collective-permute-done((f32[16,192]{1,0:T(8,128)S(1)}, f32[16,192]{1,0:T(8,128)S(1)}, u32[]{:S(2)}, u32[]{:S(2)}) %collective-permute-start.16) | collective-permute-done | bytes 12320 | tf_op jit(solution)/shard_map/ppermute | solution.py:282
  53.8 0.6 %add.3 = f32[16,192]{1,0:T(8,128)} add(f32[16,192]{1,0:T(8,128)S(1)} %get-tuple-element.49, f32[16,192]{1,0:T(8,128)S(1)} %collective-permute-done.16) | non-fusion elementwise | flops 3072 | bytes 36864 | tf_op jit(solution)/shard_map/add | solution.py:311
  (2 shorter events, 0.0 us)
Async XLA Ops:
  0.0 17.9 %collective-permute-start.4 = (bf16[192,14336]{1,0:T(8,128)(2,1)}, bf16[192,14336]{1,0:T(8,128)(2,1)}, u32[]{:S(2)}, u32[]{:S(2)}) collective-permute-start(bf16[192,14336]{1,0:T(8,128)(2,1)} %refs_4_.3), channel_id=1, source_target_pairs={{0,1},{1,0},{2,3},{3,2},{4,5},{5,4},{6,7},{7,6},{8,9},{9,8},{10,11... | collective-permute-start | bytes 16515080 | tf_op jit(solution)/shard_map/ppermute | solution.py:282
  1.8 9.0 %collective-permute-start.1 = (bf16[104,1152]{1,0:T(8,128)(2,1)S(1)}, bf16[104,1152]{1,0:T(8,128)(2,1)S(1)}, u32[]{:S(2)}, u32[]{:S(2)}) collective-permute-start(bf16[104,1152]{1,0:T(8,128)(2,1)S(1)} %get-tuple-element.29.refs_0_), channel_id=1, source_target_pairs={{0,4},{1,5},{2,6},{3,7},{4,0},{5,1},{6,2},{7,3},{8,12},{9,13},{10,... | collective-permute-start | bytes 718856 | tf_op jit(solution)/shard_map/ppermute | solution.py:282
  4.6 7.1 %collective-permute-start.2 = (bf16[104,1152]{1,0:T(8,128)(2,1)S(1)}, bf16[104,1152]{1,0:T(8,128)(2,1)S(1)}, u32[]{:S(2)}, u32[]{:S(2)}) collective-permute-start(bf16[104,1152]{1,0:T(8,128)(2,1)S(1)} %get-tuple-element.29.refs_0_), channel_id=1, source_target_pairs={{0,2},{1,3},{2,0},{3,1},{4,6},{5,7},{6,4},{7,5},{8,10},{9,11},{10,... | collective-permute-start | bytes 718856 | tf_op jit(solution)/shard_map/ppermute | solution.py:282
  5.8 11.0 %collective-permute-start.3 = (bf16[104,1152]{1,0:T(8,128)(2,1)S(1)}, bf16[104,1152]{1,0:T(8,128)(2,1)S(1)}, u32[]{:S(2)}, u32[]{:S(2)}) collective-permute-start(bf16[104,1152]{1,0:T(8,128)(2,1)S(1)} %get-tuple-element.31.refs_4_), channel_id=1, source_target_pairs={{0,2},{1,3},{2,0},{3,1},{4,6},{5,7},{6,4},{7,5},{8,10},{9,11},{10,... | collective-permute-start | bytes 718856 | tf_op jit(solution)/shard_map/ppermute | solution.py:282
  6.0 11.9 %collective-permute-start = (bf16[104,1152]{1,0:T(8,128)(2,1)S(1)}, bf16[104,1152]{1,0:T(8,128)(2,1)S(1)}, u32[]{:S(2)}, u32[]{:S(2)}) collective-permute-start(bf16[104,1152]{1,0:T(8,128)(2,1)S(1)} %get-tuple-element.30), channel_id=1, source_target_pairs={{0,12},{1,13},{2,14},{3,15},{4,8},{5,9},{6,10},{7,11},{8,4},{9,5},... | collective-permute-start | bytes 718856 | tf_op jit(solution)/shard_map/ppermute | solution.py:282
  18.0 6.5 %collective-permute-start.6 = (bf16[104,1152]{1,0:T(8,128)(2,1)S(1)}, bf16[104,1152]{1,0:T(8,128)(2,1)S(1)}, u32[]{:S(2)}, u32[]{:S(2)}) collective-permute-start(bf16[104,1152]{1,0:T(8,128)(2,1)S(1)} %get-tuple-element.33.refs_2_), channel_id=1, source_target_pairs={{0,4},{1,5},{2,6},{3,7},{4,0},{5,1},{6,2},{7,3},{8,12},{9,13},{10,... | collective-permute-start | bytes 718856 | tf_op jit(solution)/shard_map/ppermute | solution.py:282
  19.1 5.9 %collective-permute-start.7 = (bf16[104,1152]{1,0:T(8,128)(2,1)S(1)}, bf16[104,1152]{1,0:T(8,128)(2,1)S(1)}, u32[]{:S(2)}, u32[]{:S(2)}) collective-permute-start(bf16[104,1152]{1,0:T(8,128)(2,1)S(1)} %get-tuple-element.33.refs_2_), channel_id=1, source_target_pairs={{0,2},{1,3},{2,0},{3,1},{4,6},{5,7},{6,4},{7,5},{8,10},{9,11},{10,... | collective-permute-start | bytes 718856 | tf_op jit(solution)/shard_map/ppermute | solution.py:282
  20.4 5.3 %collective-permute-start.8 = (bf16[104,1152]{1,0:T(8,128)(2,1)S(1)}, bf16[104,1152]{1,0:T(8,128)(2,1)S(1)}, u32[]{:S(2)}, u32[]{:S(2)}) collective-permute-start(bf16[104,1152]{1,0:T(8,128)(2,1)S(1)} %get-tuple-element.33.refs_2_), channel_id=1, source_target_pairs={{0,16},{1,17},{2,18},{3,19},{4,20},{5,21},{6,22},{7,23},{8,24},{9,... | collective-permute-start | bytes 718856 | tf_op jit(solution)/shard_map/ppermute | solution.py:282
  21.6 11.1 %collective-permute-start.12 = (bf16[192,4096]{1,0:T(8,128)(2,1)}, bf16[192,4096]{1,0:T(8,128)(2,1)}, u32[]{:S(2)}, u32[]{:S(2)}) collective-permute-start(bf16[192,4096]{1,0:T(8,128)(2,1)} %refs_3_.3), channel_id=1, source_target_pairs={{0,1},{1,0},{2,3},{3,2},{4,5},{5,4},{6,7},{7,6},{8,9},{9,8},{10,11... | collective-permute-start | bytes 4718600 | tf_op jit(solution)/shard_map/ppermute | solution.py:282
  23.8 7.9 %collective-permute-start.5 = (bf16[104,1152]{1,0:T(8,128)(2,1)S(1)}, bf16[104,1152]{1,0:T(8,128)(2,1)S(1)}, u32[]{:S(2)}, u32[]{:S(2)}) collective-permute-start(bf16[104,1152]{1,0:T(8,128)(2,1)S(1)} %get-tuple-element.34.refs_3_), channel_id=1, source_target_pairs={{0,2},{1,3},{2,0},{3,1},{4,6},{5,7},{6,4},{7,5},{8,10},{9,11},{10,... | collective-permute-start | bytes 718856 | tf_op jit(solution)/shard_map/ppermute | solution.py:282
  24.4 12.7 %collective-permute-start.11 = (bf16[104,1152]{1,0:T(8,128)(2,1)S(1)}, bf16[104,1152]{1,0:T(8,128)(2,1)S(1)}, u32[]{:S(2)}, u32[]{:S(2)}) collective-permute-start(bf16[104,1152]{1,0:T(8,128)(2,1)S(1)} %get-tuple-element.39.refs_8_), channel_id=1, source_target_pairs={{0,4},{1,5},{2,6},{3,7},{4,0},{5,1},{6,2},{7,3},{8,12},{9,13},{10,... | collective-permute-start | bytes 718856 | tf_op jit(solution)/shard_map/ppermute | solution.py:282
  25.7 11.2 %collective-permute-start.9 = (bf16[104,1152]{1,0:T(8,128)(2,1)S(1)}, bf16[104,1152]{1,0:T(8,128)(2,1)S(1)}, u32[]{:S(2)}, u32[]{:S(2)}) collective-permute-start(bf16[104,1152]{1,0:T(8,128)(2,1)S(1)} %get-tuple-element.36.refs_5_), channel_id=1, source_target_pairs={{0,2},{1,3},{2,0},{3,1},{4,6},{5,7},{6,4},{7,5},{8,10},{9,11},{10,... | collective-permute-start | bytes 718856 | tf_op jit(solution)/shard_map/ppermute | solution.py:282
  26.3 17.4 %collective-permute-start.13 = (bf16[104,1152]{1,0:T(8,128)(2,1)S(1)}, bf16[104,1152]{1,0:T(8,128)(2,1)S(1)}, u32[]{:S(2)}, u32[]{:S(2)}) collective-permute-start(bf16[104,1152]{1,0:T(8,128)(2,1)S(1)} %get-tuple-element.36.refs_5_), channel_id=1, source_target_pairs={{0,16},{1,17},{2,18},{3,19},{4,20},{5,21},{6,22},{7,23},{8,24},{9,... | collective-permute-start | bytes 718856 | tf_op jit(solution)/shard_map/ppermute | solution.py:282
  31.8 6.1 %collective-permute-start.10 = (bf16[104,1152]{1,0:T(8,128)(2,1)S(1)}, bf16[104,1152]{1,0:T(8,128)(2,1)S(1)}, u32[]{:S(2)}, u32[]{:S(2)}) collective-permute-start(bf16[104,1152]{1,0:T(8,128)(2,1)S(1)} %get-tuple-element.38.refs_7_), channel_id=1, source_target_pairs={{0,4},{1,5},{2,6},{3,7},{4,0},{5,1},{6,2},{7,3},{8,12},{9,13},{10,... | collective-permute-start | bytes 718856 | tf_op jit(solution)/shard_map/ppermute | solution.py:282
  32.7 11.0 %collective-permute-start.14 = (bf16[104,1152]{1,0:T(8,128)(2,1)S(1)}, bf16[104,1152]{1,0:T(8,128)(2,1)S(1)}, u32[]{:S(2)}, u32[]{:S(2)}) collective-permute-start(bf16[104,1152]{1,0:T(8,128)(2,1)S(1)} %get-tuple-element.37.refs_6_), channel_id=1, source_target_pairs={{0,16},{1,17},{2,18},{3,19},{4,20},{5,21},{6,22},{7,23},{8,24},{9,... | collective-permute-start | bytes 718856 | tf_op jit(solution)/shard_map/ppermute | solution.py:282
  36.9 7.9 %collective-permute-start.15 = (bf16[104,1152]{1,0:T(8,128)(2,1)S(1)}, bf16[104,1152]{1,0:T(8,128)(2,1)S(1)}, u32[]{:S(2)}, u32[]{:S(2)}) collective-permute-start(bf16[104,1152]{1,0:T(8,128)(2,1)S(1)} %collective-permute-done.9.refs_0_), channel_id=1, source_target_pairs={{0,16},{1,17},{2,18},{3,19},{4,20},{5,21},{6,22},{7,23},{8,24},{9,... | collective-permute-start | bytes 718856 | tf_op jit(solution)/shard_map/ppermute | solution.py:282
  50.7 3.1 %collective-permute-start.16 = (f32[16,192]{1,0:T(8,128)S(1)}, f32[16,192]{1,0:T(8,128)S(1)}, u32[]{:S(2)}, u32[]{:S(2)}) collective-permute-start(f32[16,192]{1,0:T(8,128)S(1)} %get-tuple-element.50), channel_id=1, source_target_pairs={{0,1},{1,0},{2,3},{3,2},{4,5},{5,4},{6,7},{7,6},{8,9},{9,8},{10,11... | collective-permute-start | bytes 36872 | tf_op jit(solution)/shard_map/ppermute | solution.py:282

commit v4 on v3

--- a/solution.py
+++ b/solution.py
@@ -13,7 +13,6 @@
 SEGS = 16
 ROWS = 16
 CUTS = (1, 4)
-AHEAD = 10
 LIMIT = 16 << 20
 TICK = 8
 PACK = 30
@@ -141,27 +140,24 @@
 
 def fetch(half, tokens, buffers, sems):
     jobs = []
-    for j in range(4):
-        width, side = buffers[j].shape[1], j % 2
+    for j, buf in enumerate(buffers):
+        width, side = buf.shape[1], j % 2
         start = side * buffers[0].shape[1]
         cut = width // CUTS[side]
         for i in range(CUTS[side]):
             at = pl.ds(pl.multiple_of(half * width + i * cut, cut), cut)
             copy = pltpu.make_async_copy(
-                tokens[j].at[:, at], buffers[j].at[:, pl.ds(i * cut, cut)], sems.at[len(jobs)]
+                tokens[j].at[:, at], buf.at[:, pl.ds(i * cut, cut)], sems.at[len(jobs)]
             )
+            copy.start()
             jobs.append((copy, j, i * cut, start + i * cut, cut))
-    for job in jobs[:AHEAD]:
-        job[0].start()
     return jobs
 
 
 def project(rows, jobs, buffers):
     sums = [None] * 4
-    for i, (copy, j, first, start, cut) in enumerate(jobs):
+    for copy, j, first, start, cut in jobs:
         copy.wait()
-        if i + AHEAD < len(jobs):
-            jobs[i + AHEAD][0].start()
         term = lax.dot_general(
             rows[:, start : start + cut], buffers[j][:, first : first + cut], NT,
             preferred_element_type=jnp.float32,
@@ -172,7 +168,7 @@
 
 def half_scratch(tokens):
     return [pltpu.VMEM((a.shape[0], a.shape[1] // 2), a.dtype) for a in tokens] + [
-        pltpu.SemaphoreType.DMA((2 * sum(CUTS),))
+        pltpu.SemaphoreType.DMA((len(tokens) // 2 * sum(CUTS),))
     ]
 
 
@@ -201,8 +197,15 @@
 
 def first_kernel(now, later, n_pieces, x_ref, rows_ref, *refs):
     pieces, refs = refs[:n_pieces], refs[n_pieces:]
-    tokens, accs, (later_ref, rows, *buffers, sems) = refs[:4], refs[4:8], refs[8:]
+    tokens, accs, later_ref, staged = refs[:4], refs[4:8], refs[8], refs[9:13]
+    rows, *buffers, sems, staged_sems = refs[13:]
     jobs = fetch(x_ref[0], tokens, buffers, sems)
+    copies = []
+    for j, (src, dst) in enumerate(zip(tokens, staged)):
+        width = dst.shape[1]
+        at = pl.ds(pl.multiple_of((1 - x_ref[0]) * width, width), width)
+        copies.append(pltpu.make_async_copy(src.at[:, at], dst, staged_sems.at[j]))
+        copies[j].start()
     ew, n = tokens[0].shape[1] // SEGS, rows_ref.shape[0]
     rows[:n] = rows_ref[...]
     for i, p in enumerate(now):
@@ -211,6 +214,8 @@
         acc[...] = v
     for i, p in enumerate(later):
         unpack(pieces[p], later_ref, i * ROWS, ew)
+    for copy in copies:
+        copy.wait()
 
 
 def first_half(x, rows, pieces, now, later, tokens):
@@ -220,50 +225,84 @@
     return pl.pallas_call(
         functools.partial(first_kernel, now, later, len(pieces)),
         out_shape=(acc,) * 4
-        + (jax.ShapeDtypeStruct((len(later) * ROWS, width), jnp.bfloat16),),
+        + (jax.ShapeDtypeStruct((len(later) * ROWS, width), jnp.bfloat16),)
+        + tuple(jax.ShapeDtypeStruct((a.shape[0], a.shape[1] // 2), a.dtype) for a in tokens),
         in_specs=[pl.BlockSpec(memory_space=pltpu.SMEM)] + [vmem] * (len(pieces) + 1) + [hbm] * 4,
-        out_specs=(vmem,) * 5,
-        scratch_shapes=[pltpu.VMEM((n, width), jnp.bfloat16)] + half_scratch(tokens),
+        out_specs=(vmem,) * 9,
+        scratch_shapes=[pltpu.VMEM((n, width), jnp.bfloat16)]
+        + half_scratch(tokens)
+        + [pltpu.SemaphoreType.DMA((4,))],
         compiler_params=pltpu.CompilerParams(vmem_limit_bytes=LIMIT),
         cost_estimate=weight(12),
         name="first_half",
     )(x, rows, *pieces, *tokens)
 
 
-def second_kernel(order, n_pieces, x_ref, me_ref, rows_a, rows_b, *refs):
+def side_sums(rows, tokens):
+    sums, start = [], 0
+    for t_ref, cuts in zip(tokens, CUTS):
+        cut, total = t_ref.shape[1] // cuts, None
+        for i in range(cuts):
+            term = lax.dot_general(
+                rows[:, start : start + cut], t_ref[:, i * cut : (i + 1) * cut], NT,
+                preferred_element_type=jnp.float32,
+            )
+            total = term if total is None else total + term
+            start += cut
+        sums.append(total)
+    return sums
+
+
+def scores(order, me, sums, accs, out_ref):
+    prod = (sums[0] + accs[0][...]) * (sums[1] + accs[1][...])
+    out_ref[...] = jnp.zeros_like(out_ref)
+    for b, flip in enumerate(order):
+        row = jnp.sum(prod[b * ROWS : (b + 1) * ROWS], axis=0, keepdims=True)
+        out_ref[pl.ds(jnp.bitwise_xor(me, flip), 1), :] = row
+
+
+def mate_kernel(order, n_pieces, me_ref, rows_a, rows_b, *refs):
     pieces, refs = refs[:n_pieces], refs[n_pieces:]
-    tokens, accs = refs[:4], refs[4:8]
-    own_ref, mate_ref, rows, *buffers, sems = refs[8:]
-    jobs = fetch(1 - x_ref[0], tokens, buffers, sems)
+    tokens, accs, (out_ref, rows) = refs[:2], refs[2:4], refs[4:]
     n, m = rows_a.shape[0], rows_a.shape[0] + rows_b.shape[0]
     rows[:n], rows[n:m] = rows_a[...], rows_b[...]
     for i, piece in enumerate(pieces):
-        unpack(piece, rows, m + i * ROWS, tokens[0].shape[1] // SEGS)
-    me = me_ref[0]
-    sums = [v + acc[...] for v, acc in zip(project(rows, jobs, buffers), accs)]
-    for j, out_ref in enumerate((own_ref, mate_ref)):
-        prod = sums[2 * j] * sums[2 * j + 1]
-        out_ref[...] = jnp.zeros_like(out_ref)
-        for b, flip in enumerate(order):
-            row = jnp.sum(prod[b * ROWS : (b + 1) * ROWS], axis=0, keepdims=True)
-            out_ref[pl.ds(jnp.bitwise_xor(me, flip), 1), :] = row
-
-
-def second_half(x, me, order, rows_a, rows_b, pieces, tokens, accs):
+        unpack(piece, rows, m + i * ROWS, 2 * tokens[0].shape[1] // SEGS)
+    scores(order, me_ref[0], side_sums(rows, tokens), accs, out_ref)
+
+
+def own_kernel(order, me_ref, rows, *refs):
+    tokens, accs, out_ref = refs[:2], refs[2:4], refs[4]
+    scores(order, me_ref[0], side_sums(rows, tokens), accs, out_ref)
+
+
+def mate_scores(me, order, rows_a, rows_b, pieces, tokens, accs):
     vmem, smem = pl.BlockSpec(memory_space=pltpu.VMEM), pl.BlockSpec(memory_space=pltpu.SMEM)
-    hbm = pl.BlockSpec(memory_space=pltpu.HBM)
-    out = jax.ShapeDtypeStruct((2 * len(order), tokens[0].shape[0]), jnp.float32)
-    return pl.pallas_call(
-        functools.partial(second_kernel, order, len(pieces)),
-        out_shape=(out, out),
-        in_specs=[smem, smem] + [vmem] * (2 + len(pieces)) + [hbm] * 4 + [vmem] * 4,
+    return pl.pallas_call(
+        functools.partial(mate_kernel, order, len(pieces)),
+        out_shape=(
+            jax.ShapeDtypeStruct((2 * len(order), tokens[0].shape[0]), jnp.float32),
+            jax.ShapeDtypeStruct((len(order) * ROWS, rows_a.shape[1]), jnp.bfloat16),
+        ),
+        in_specs=[smem] + [vmem] * (6 + len(pieces)),
         out_specs=(vmem, vmem),
-        scratch_shapes=[pltpu.VMEM((len(order) * ROWS, rows_a.shape[1]), jnp.bfloat16)]
-        + half_scratch(tokens),
-        compiler_params=pltpu.CompilerParams(vmem_limit_bytes=LIMIT),
-        cost_estimate=weight(10),
-        name="second_half",
-    )(x, me, rows_a, rows_b, *pieces, *tokens, *accs)
+        compiler_params=pltpu.CompilerParams(vmem_limit_bytes=LIMIT),
+        cost_estimate=weight(5),
+        name="mate_scores",
+    )(me, rows_a, rows_b, *pieces, *tokens, *accs)
+
+
+def own_scores(me, order, rows, tokens, accs):
+    vmem, smem = pl.BlockSpec(memory_space=pltpu.VMEM), pl.BlockSpec(memory_space=pltpu.SMEM)
+    return pl.pallas_call(
+        functools.partial(own_kernel, order),
+        out_shape=jax.ShapeDtypeStruct((2 * len(order), tokens[0].shape[0]), jnp.float32),
+        in_specs=[smem] + [vmem] * 5,
+        out_specs=vmem,
+        compiler_params=pltpu.CompilerParams(vmem_limit_bytes=LIMIT),
+        cost_estimate=weight(30),
+        name="own_scores",
+    )(me, rows, *tokens, *accs)
 
 
 def pairs(n_grp, n_blk, flip_grp, flip_blk):
@@ -283,6 +322,7 @@
     over_x = lambda a: swap(a, 1, 0)
     over_y = lambda a: swap(a, 0, 2)
     over_z = lambda a, k: swap(a, 0, 4 * k)
+    over_xy = lambda a: swap(a, 1, 2)
     mate = lambda a: swap(a, 0, 1)
     x = lax.axis_index("grp").astype(jnp.int32).reshape(1)
     me = lax.axis_index("blk").astype(jnp.int32).reshape(1)
@@ -292,7 +332,7 @@
     z3 = over_z(half, 3)
     half, rest = pack_again(x, runs)
     y0, z1, y0r = over_y(half), over_z(half, 1), over_y(rest)
-    z3, z1, y0, y0r, rest, mate_acts = gate(z3, z1, y0, y0r, rest, mate_acts)
+    z1, y0, y0r, rest, mate_acts = gate(z1, y0, y0r, rest, mate_acts)
     z2, y3, xa3 = over_z(z3, 1), over_y(z3), over_x(z3)
     y1, y1r = over_y(z1), over_z(y0r, 1)
     z2, y3, xa3, rest = gate(z2, y3, xa3, rest)
@@ -302,13 +342,15 @@
         (half, y0, z3, z1, y1, z2, y3, rest, y0r, xa3), tuple(range(7)), (7, 8, 9),
         errors.shape[1] // SEGS,
     )
-    xb2 = over_x(y2)
+    xb2 = over_xy(z2)
 
     tokens = tuple(in_hbm(a) for a in (errors, activations, mate_errs, mate_acts))
-    *accs, late = first_half(x, mine, (y2, z1r, y1r), (0,), (1, 2), tokens)
+    *accs, late, e0, a0, e1, a1 = first_half(x, mine, (y2, z1r, y1r), (0,), (1, 2), tokens)
     order = (0, 2, 12, 4, 6, 8, 14, 10)
-    own, mates = second_half(x, me, order, others, late, (xa2, xb3, xb2), tokens, accs)
-    return own + mate(mates)
+    mates, rows = mate_scores(
+        me, order, others, late, (xa2, xb3, xb2), (e1, a1), accs[2:]
+    )
+    return mate(mates) + own_scores(me, order, rows, (e0, a0), accs[:2])
 
 
 def solution(mesh):

time: 54.9 us -> 50 us (0.911)
  waiting for transfers between devices: 21.5 us -> 14.9 us
  starting transfers between devices: 17.9 us -> 23 us
  Pallas kernels: 14.3 us -> 11.3 us
    ppermute x17, waiting for transfers between devices: 21.5 us -> 14.9 us  [permuted(): swap = lambda a, gx, bx: lax.ppermute(a, AXES, pairs(n_grp, n_blk, gx, bx))]
    ppermute x17, starting transfers between devices: 17.9 us -> 23 us  [permuted(): swap = lambda a, gx, bx: lax.ppermute(a, AXES, pairs(n_grp, n_blk, gx, bx))]
    pallas_call x1 -> x2, Pallas kernels: 5.92 us -> 2.79 us  [the longest x1 1.43 us: mate_scores(): pl.pallas_call(functools.partial(mate_kernel, order, len(pieces)), out_sh...]
  transfers between devices with their start and end apart: 17 -> 17, of which waited for: 11 -> 6; matrix products, arithmetic and copies ran while one was open for 0% -> 0% of each run, Pallas kernels for 15% -> 20%
where the time goes in v4:
time: 50 us; the launch traced here: 49.8 us
  starting transfers between devices  23 us (46%)
  waiting for transfers between devices  14.9 us (30%)
  Pallas kernels  11.3 us (23%)
  other arithmetic  0.61 us (1%)
    ppermute x17, starting transfers between devices, permuted(): swap = lambda a, gx, bx: lax.ppermute(a, AXES, pairs(n_grp, n_blk, gx, bx))  23 us
    ppermute x17, waiting for transfers between devices, permuted(): swap = lambda a, gx, bx: lax.ppermute(a, AXES, pairs(n_grp, n_blk, gx, bx))  14.9 us
    pallas_call x1, Pallas kernels, first_half(): pl.pallas_call(functools.partial(first_kernel, now, later, len(pieces)),...  5.86 us
    pallas_call x1, Pallas kernels, mate_scores(): pl.pallas_call(functools.partial(mate_kernel, order, len(pieces)), out_sh...  1.43 us
    pallas_call x1, Pallas kernels, pack(): pl.pallas_call(pack_kernel, out_shape=(jax.ShapeDtypeStruct((n * RANK, wi...  1.39 us
    pallas_call x1, Pallas kernels, own_scores(): pl.pallas_call(functools.partial(own_kernel, order), out_shape=jax.ShapeD...  1.35 us
  transfers between devices with their start and end apart: 17, of which 6 were waited for; matrix products, arithmetic and copies ran while one was open for 0% of the time, Pallas kernels for 20%

profile of v4, /device:TPU:1, one launch (start us, length us, event | category | flops | bytes accessed | tf_op | source)
XLA Modules:
  0.0 49.8 jit_solution(11463648079111927930)
XLA Ops:
  0.0 0.1 collective-permute-start.3
  0.1 1.4 %pack.1 = (bf16[104,1152]{1,0:T(8,128)(2,1)S(1)}, bf16[2,128,1152]{2,1,0:T(8,128)(2,1)S(1)}) custom-call(s32[1]{0:T(128)} %bitcast.1.x_ref, bf16[1,13,4096]{2,1,0:T(8,128)(2,1)} %err_hbm.1, bf16[1,13,14336]{2,1,0:T(8,128)(2,1)} %act_hbm.1), custom_call_target="tpu_custom_call" | custom-call | tf_op jit(solution)/shard_map/pack/pallas_call | solution.py:68
  1.5 0.0 copy-start
  1.5 0.3 pack_again.1
  1.8 2.8 %collective-permute-start = (bf16[104,1152]{1,0:T(8,128)(2,1)S(1)}, bf16[104,1152]{1,0:T(8,128)(2,1)S(1)}, u32[]{:S(2)}, u32[]{:S(2)}) collective-permute-start(bf16[104,1152]{1,0:T(8,128)(2,1)S(1)} %get-tuple-element.32.refs_0_), channel_id=1, source_target_pairs={{0,4},{1,5},{2,6},{3,7},{4,0},{5,1},{6,2},{7,3},{8,12},{9,13},{10,... | collective-permute-start | bytes 718856 | tf_op jit(solution)/shard_map/ppermute | solution.py:321
  4.6 2.2 %collective-permute-start.4 = (bf16[104,1152]{1,0:T(8,128)(2,1)S(1)}, bf16[104,1152]{1,0:T(8,128)(2,1)S(1)}, u32[]{:S(2)}, u32[]{:S(2)}) collective-permute-start(bf16[104,1152]{1,0:T(8,128)(2,1)S(1)} %get-tuple-element.35), channel_id=1, source_target_pairs={{0,12},{1,13},{2,14},{3,15},{4,8},{5,9},{6,10},{7,11},{8,4},{9,5},... | collective-permute-start | bytes 718856 | tf_op jit(solution)/shard_map/ppermute | solution.py:321
  6.8 1.2 %collective-permute-start.1 = (bf16[104,1152]{1,0:T(8,128)(2,1)S(1)}, bf16[104,1152]{1,0:T(8,128)(2,1)S(1)}, u32[]{:S(2)}, u32[]{:S(2)}) collective-permute-start(bf16[104,1152]{1,0:T(8,128)(2,1)S(1)} %get-tuple-element.32.refs_0_), channel_id=1, source_target_pairs={{0,2},{1,3},{2,0},{3,1},{4,6},{5,7},{6,4},{7,5},{8,10},{9,11},{10,... | collective-permute-start | bytes 718856 | tf_op jit(solution)/shard_map/ppermute | solution.py:321
  8.0 0.2 collective-permute-start.2
  8.3 2.5 %collective-permute-done.refs_0_ = bf16[104,1152]{1,0:T(8,128)(2,1)S(1)} collective-permute-done((bf16[104,1152]{1,0:T(8,128)(2,1)S(1)}, bf16[104,1152]{1,0:T(8,128)(2,1)S(1)}, u32[]{:S(2)}, u32[]{:S(2)}) %collective-permute-start) | collective-permute-done | bytes 239648 | tf_op jit(solution)/shard_map/ppermute | solution.py:321
  10.8 0.0 copy-done
  10.8 0.6 %collective-permute-start.12 = (bf16[192,4096]{1,0:T(8,128)(2,1)S(1)}, bf16[192,4096]{1,0:T(8,128)(2,1)S(1)}, u32[]{:S(2)}, u32[]{:S(2)}) collective-permute-start(bf16[192,4096]{1,0:T(8,128)(2,1)S(1)} %copy-done), channel_id=1, source_target_pairs={{0,1},{1,0},{2,3},{3,2},{4,5},{5,4},{6,7},{7,6},{8,9},{9,8},{10,11... | collective-permute-start | bytes 4718600 | tf_op jit(solution)/shard_map/ppermute | solution.py:321
  11.4 6.6 %collective-permute-done.4.refs_2_ = bf16[104,1152]{1,0:T(8,128)(2,1)S(1)} collective-permute-done((bf16[104,1152]{1,0:T(8,128)(2,1)S(1)}, bf16[104,1152]{1,0:T(8,128)(2,1)S(1)}, u32[]{:S(2)}, u32[]{:S(2)}) %collective-permute-start.4) | collective-permute-done | bytes 239648 | tf_op jit(solution)/shard_map/ppermute | solution.py:321
  18.0 0.0 collective-permute-start.6
  18.0 0.0 collective-permute-done.1.refs_1_
  18.0 1.2 %collective-permute-start.7 = (bf16[104,1152]{1,0:T(8,128)(2,1)S(1)}, bf16[104,1152]{1,0:T(8,128)(2,1)S(1)}, u32[]{:S(2)}, u32[]{:S(2)}) collective-permute-start(bf16[104,1152]{1,0:T(8,128)(2,1)S(1)} %collective-permute-done.4.refs_2_), channel_id=1, source_target_pairs={{0,2},{1,3},{2,0},{3,1},{4,6},{5,7},{6,4},{7,5},{8,10},{9,11},{10,... | collective-permute-start | bytes 718856 | tf_op jit(solution)/shard_map/ppermute | solution.py:321
  19.2 0.0 collective-permute-done.2.refs_2_
  19.2 1.2 %collective-permute-start.8 = (bf16[104,1152]{1,0:T(8,128)(2,1)S(1)}, bf16[104,1152]{1,0:T(8,128)(2,1)S(1)}, u32[]{:S(2)}, u32[]{:S(2)}) collective-permute-start(bf16[104,1152]{1,0:T(8,128)(2,1)S(1)} %collective-permute-done.4.refs_2_), channel_id=1, source_target_pairs={{0,16},{1,17},{2,18},{3,19},{4,20},{5,21},{6,22},{7,23},{8,24},{9,... | collective-permute-start | bytes 718856 | tf_op jit(solution)/shard_map/ppermute | solution.py:321
  20.4 0.0 collective-permute-done.3.refs_4_
  20.4 0.8 %collective-permute-start.5 = (bf16[104,1152]{1,0:T(8,128)(2,1)S(1)}, bf16[104,1152]{1,0:T(8,128)(2,1)S(1)}, u32[]{:S(2)}, u32[]{:S(2)}) collective-permute-start(bf16[104,1152]{1,0:T(8,128)(2,1)S(1)} %get-tuple-element.36.refs_3_), channel_id=1, source_target_pairs={{0,2},{1,3},{2,0},{3,1},{4,6},{5,7},{6,4},{7,5},{8,10},{9,11},{10,... | collective-permute-start | bytes 718856 | tf_op jit(solution)/shard_map/ppermute | solution.py:321
  21.2 3.3 %collective-permute-done.6.refs_0_ = bf16[104,1152]{1,0:T(8,128)(2,1)S(1)} collective-permute-done((bf16[104,1152]{1,0:T(8,128)(2,1)S(1)}, bf16[104,1152]{1,0:T(8,128)(2,1)S(1)}, u32[]{:S(2)}, u32[]{:S(2)}) %collective-permute-start.6) | collective-permute-done | bytes 239648 | tf_op jit(solution)/shard_map/ppermute | solution.py:321
  24.5 0.0 collective-permute-done.7.refs_1_
  24.5 0.4 collective-permute-done.8.refs_2_
  24.8 1.0 %collective-permute-start.9 = (bf16[104,1152]{1,0:T(8,128)(2,1)S(1)}, bf16[104,1152]{1,0:T(8,128)(2,1)S(1)}, u32[]{:S(2)}, u32[]{:S(2)}) collective-permute-start(bf16[104,1152]{1,0:T(8,128)(2,1)S(1)} %get-tuple-element.38.refs_5_), channel_id=1, source_target_pairs={{0,2},{1,3},{2,0},{3,1},{4,6},{5,7},{6,4},{7,5},{8,10},{9,11},{10,... | collective-permute-start | bytes 718856 | tf_op jit(solution)/shard_map/ppermute | solution.py:321
  25.9 1.2 %collective-permute-start.13 = (bf16[104,1152]{1,0:T(8,128)(2,1)S(1)}, bf16[104,1152]{1,0:T(8,128)(2,1)S(1)}, u32[]{:S(2)}, u32[]{:S(2)}) collective-permute-start(bf16[104,1152]{1,0:T(8,128)(2,1)S(1)} %get-tuple-element.38.refs_5_), channel_id=1, source_target_pairs={{0,16},{1,17},{2,18},{3,19},{4,20},{5,21},{6,22},{7,23},{8,24},{9,... | collective-permute-start | bytes 718856 | tf_op jit(solution)/shard_map/ppermute | solution.py:321
  27.1 1.0 %collective-permute-start.10 = (bf16[104,1152]{1,0:T(8,128)(2,1)S(1)}, bf16[104,1152]{1,0:T(8,128)(2,1)S(1)}, u32[]{:S(2)}, u32[]{:S(2)}) collective-permute-start(bf16[104,1152]{1,0:T(8,128)(2,1)S(1)} %get-tuple-element.40.refs_7_), channel_id=1, source_target_pairs={{0,4},{1,5},{2,6},{3,7},{4,0},{5,1},{6,2},{7,3},{8,12},{9,13},{10,... | collective-permute-start | bytes 718856 | tf_op jit(solution)/shard_map/ppermute | solution.py:321
  28.1 0.9 %collective-permute-done.5.refs_4_ = bf16[104,1152]{1,0:T(8,128)(2,1)S(1)} collective-permute-done((bf16[104,1152]{1,0:T(8,128)(2,1)S(1)}, bf16[104,1152]{1,0:T(8,128)(2,1)S(1)}, u32[]{:S(2)}, u32[]{:S(2)}) %collective-permute-start.5) | collective-permute-done | bytes 239648 | tf_op jit(solution)/shard_map/ppermute | solution.py:321
  29.0 1.8 %collective-permute-start.11 = (bf16[104,1152]{1,0:T(8,128)(2,1)S(1)}, bf16[104,1152]{1,0:T(8,128)(2,1)S(1)}, u32[]{:S(2)}, u32[]{:S(2)}) collective-permute-start(bf16[104,1152]{1,0:T(8,128)(2,1)S(1)} %get-tuple-element.41.refs_8_), channel_id=1, source_target_pairs={{0,4},{1,5},{2,6},{3,7},{4,0},{5,1},{6,2},{7,3},{8,12},{9,13},{10,... | collective-permute-start | bytes 718856 | tf_op jit(solution)/shard_map/ppermute | solution.py:321
  30.8 0.9 %unpacked.1 = (bf16[112,9216]{1,0:T(8,128)(2,1)S(1)}, bf16[48,9216]{1,0:T(8,128)(2,1)S(1)}) custom-call(bf16[104,1152]{1,0:T(8,128)(2,1)S(1)} %get-tuple-element.32.refs_0_, bf16[104,1152]{1,0:T(8,128)(2,1)S(1)} %get-tuple-element.34.refs_1_, bf16[104,1152]{1,0:T(8,128)(2,1)S(1)} %collective-permute-done.4.refs_2_, ...), custom_call_target="tpu_custom_call" | custom-call | flops 8000000000 | bytes 24000000 | tf_op jit(solution)/shard_map/unpacked/pallas_call | solution.py:185
  31.7 0.0 collective-permute-done.12.refs_5_
  31.7 0.0 copy-start.1
  31.7 1.3 %collective-permute-start.14 = (bf16[104,1152]{1,0:T(8,128)(2,1)S(1)}, bf16[104,1152]{1,0:T(8,128)(2,1)S(1)}, u32[]{:S(2)}, u32[]{:S(2)}) collective-permute-start(bf16[104,1152]{1,0:T(8,128)(2,1)S(1)} %get-tuple-element.39.refs_6_), channel_id=1, source_target_pairs={{0,16},{1,17},{2,18},{3,19},{4,20},{5,21},{6,22},{7,23},{8,24},{9,... | collective-permute-start | bytes 718856 | tf_op jit(solution)/shard_map/ppermute | solution.py:321
  33.0 1.2 %collective-permute-done.9.refs_0_ = bf16[104,1152]{1,0:T(8,128)(2,1)S(1)} collective-permute-done((bf16[104,1152]{1,0:T(8,128)(2,1)S(1)}, bf16[104,1152]{1,0:T(8,128)(2,1)S(1)}, u32[]{:S(2)}, u32[]{:S(2)}) %collective-permute-start.9) | collective-permute-done | bytes 239648 | tf_op jit(solution)/shard_map/ppermute | solution.py:321
  34.1 2.2 %collective-permute-start.15 = (bf16[104,1152]{1,0:T(8,128)(2,1)S(1)}, bf16[104,1152]{1,0:T(8,128)(2,1)S(1)}, u32[]{:S(2)}, u32[]{:S(2)}) collective-permute-start(bf16[104,1152]{1,0:T(8,128)(2,1)S(1)} %get-tuple-element.38.refs_5_), channel_id=1, source_target_pairs={{0,18},{1,19},{2,16},{3,17},{4,22},{5,23},{6,20},{7,21},{8,26},{9,... | collective-permute-start | bytes 718856 | tf_op jit(solution)/shard_map/ppermute | solution.py:321
  36.3 0.0 collective-permute-done.10.refs_1_
  36.3 0.0 collective-permute-done.11.refs_2_
  36.3 0.0 copy-done.1
  36.3 5.9 %first_half.1 = (f32[128,192]{1,0:T(8,128)S(1)}, f32[128,192]{1,0:T(8,128)S(1)}, f32[128,192]{1,0:T(8,128)S(1)}, f32[128,192]{1,0:T(8,128)S(1)}, bf16[32,9216]{1...) custom-call(s32[1]{0:T(128)} %bitcast.1.x_ref, ...), custom_call_target="tpu_custom_call" | custom-call | flops 12000000000 | bytes 36000000 | tf_op jit(solution)/shard_map/first_half/pallas_call | solution.py:225
  42.2 0.0 collective-permute-done.13.refs_0_
  42.2 0.0 collective-permute-done.14.refs_1_
  42.2 0.0 collective-permute-done.15.refs_2_
  42.2 1.4 %mate_scores.1 = (f32[16,192]{1,0:T(8,128)S(1)}, bf16[128,9216]{1,0:T(8,128)(2,1)S(1)}) custom-call(s32[1]{0:T(128)} %bitcast.me_ref, bf16[48,9216]{1,0:T(8,128)(2,1)S(1)} %get-tuple-element.43.rows_a, bf16[32,9216]{1,0:T(8,128)(2,1)S(1)} %get-tuple-element.46.rows_b, bf16[104,1152]{1,0:T(8,128)(2,1)S(1)} %collective-permute-done.13.refs_0_, ...), custom_call_target="tpu_custom_call" | custom-call | flops 5000000000 | bytes 15000000 | tf_op jit(solution)/shard_map/mate_scores/pallas_call | solution.py:281
  43.6 4.2 %collective-permute-start.16 = (f32[16,192]{1,0:T(8,128)S(1)}, f32[16,192]{1,0:T(8,128)S(1)}, u32[]{:S(2)}, u32[]{:S(2)}) collective-permute-start(f32[16,192]{1,0:T(8,128)S(1)} %get-tuple-element.51), channel_id=1, source_target_pairs={{0,1},{1,0},{2,3},{3,2},{4,5},{5,4},{6,7},{7,6},{8,9},{9,8},{10,11... | collective-permute-start | bytes 36872 | tf_op jit(solution)/shard_map/ppermute | solution.py:321
  47.9 1.4 %own_scores.1 = f32[16,192]{1,0:T(8,128)S(1)} custom-call(s32[1]{0:T(128)} %bitcast.me_ref, bf16[128,9216]{1,0:T(8,128)(2,1)S(1)} %get-tuple-element.52.rows, bf16[192,2048]{1,0:T(8,128)(2,1)S(1)} %get-tuple-element.53.refs_0_, bf16[192,7168]{1,0:T(8,128)(2,1)S(1)} %get-tuple-element.54.refs_1_, f32[128,192]{1,0:T(8,128)S(1)} %get-tuple-element.55.refs_2_, ...), custom_call_target="tpu_custom_call" | custom-call | flops 30000001024 | bytes 90000000 | tf_op jit(solution)/shard_map/own_scores/pallas_call | solution.py:297
  49.2 0.0 collective-permute-done.16
  49.2 0.6 %add.3 = f32[16,192]{1,0:T(8,128)} add(f32[16,192]{1,0:T(8,128)S(1)} %collective-permute-done.16, f32[16,192]{1,0:T(8,128)S(1)} %own_scores.1) | non-fusion elementwise | flops 3072 | bytes 36864 | tf_op jit(solution)/shard_map/add | solution.py:353
  (2 shorter events, 0.0 us)
Async XLA Ops:
  0.0 20.4 %collective-permute-start.3 = (bf16[192,14336]{1,0:T(8,128)(2,1)}, bf16[192,14336]{1,0:T(8,128)(2,1)}, u32[]{:S(2)}, u32[]{:S(2)}) collective-permute-start(bf16[192,14336]{1,0:T(8,128)(2,1)} %refs_4_.1), channel_id=1, source_target_pairs={{0,1},{1,0},{2,3},{3,2},{4,5},{5,4},{6,7},{7,6},{8,9},{9,8},{10,11... | collective-permute-start | bytes 16515080 | tf_op jit(solution)/shard_map/ppermute | solution.py:321
  1.5 9.3 %copy-start = (bf16[192,4096]{1,0:T(8,128)(2,1)S(1)}, bf16[192,4096]{1,0:T(8,128)(2,1)}, u32[]{:S(2)}) copy-start(bf16[192,4096]{1,0:T(8,128)(2,1)} %refs_3_.1) | copy-start | bytes 4718596
  1.8 9.0 %collective-permute-start = (bf16[104,1152]{1,0:T(8,128)(2,1)S(1)}, bf16[104,1152]{1,0:T(8,128)(2,1)S(1)}, u32[]{:S(2)}, u32[]{:S(2)}) collective-permute-start(bf16[104,1152]{1,0:T(8,128)(2,1)S(1)} %get-tuple-element.32.refs_0_), channel_id=1, source_target_pairs={{0,4},{1,5},{2,6},{3,7},{4,0},{5,1},{6,2},{7,3},{8,12},{9,13},{10,... | collective-permute-start | bytes 718856 | tf_op jit(solution)/shard_map/ppermute | solution.py:321
  4.6 13.4 %collective-permute-start.4 = (bf16[104,1152]{1,0:T(8,128)(2,1)S(1)}, bf16[104,1152]{1,0:T(8,128)(2,1)S(1)}, u32[]{:S(2)}, u32[]{:S(2)}) collective-permute-start(bf16[104,1152]{1,0:T(8,128)(2,1)S(1)} %get-tuple-element.35), channel_id=1, source_target_pairs={{0,12},{1,13},{2,14},{3,15},{4,8},{5,9},{6,10},{7,11},{8,4},{9,5},... | collective-permute-start | bytes 718856 | tf_op jit(solution)/shard_map/ppermute | solution.py:321
  6.8 11.2 %collective-permute-start.1 = (bf16[104,1152]{1,0:T(8,128)(2,1)S(1)}, bf16[104,1152]{1,0:T(8,128)(2,1)S(1)}, u32[]{:S(2)}, u32[]{:S(2)}) collective-permute-start(bf16[104,1152]{1,0:T(8,128)(2,1)S(1)} %get-tuple-element.32.refs_0_), channel_id=1, source_target_pairs={{0,2},{1,3},{2,0},{3,1},{4,6},{5,7},{6,4},{7,5},{8,10},{9,11},{10,... | collective-permute-start | bytes 718856 | tf_op jit(solution)/shard_map/ppermute | solution.py:321
  8.0 11.2 %collective-permute-start.2 = (bf16[104,1152]{1,0:T(8,128)(2,1)S(1)}, bf16[104,1152]{1,0:T(8,128)(2,1)S(1)}, u32[]{:S(2)}, u32[]{:S(2)}) collective-permute-start(bf16[104,1152]{1,0:T(8,128)(2,1)S(1)} %get-tuple-element.33.refs_3_), channel_id=1, source_target_pairs={{0,2},{1,3},{2,0},{3,1},{4,6},{5,7},{6,4},{7,5},{8,10},{9,11},{10,... | collective-permute-start | bytes 718856 | tf_op jit(solution)/shard_map/ppermute | solution.py:321
  10.8 20.9 %collective-permute-start.12 = (bf16[192,4096]{1,0:T(8,128)(2,1)S(1)}, bf16[192,4096]{1,0:T(8,128)(2,1)S(1)}, u32[]{:S(2)}, u32[]{:S(2)}) collective-permute-start(bf16[192,4096]{1,0:T(8,128)(2,1)S(1)} %copy-done), channel_id=1, source_target_pairs={{0,1},{1,0},{2,3},{3,2},{4,5},{5,4},{6,7},{7,6},{8,9},{9,8},{10,11... | collective-permute-start | bytes 4718600 | tf_op jit(solution)/shard_map/ppermute | solution.py:321
  18.0 6.5 %collective-permute-start.6 = (bf16[104,1152]{1,0:T(8,128)(2,1)S(1)}, bf16[104,1152]{1,0:T(8,128)(2,1)S(1)}, u32[]{:S(2)}, u32[]{:S(2)}) collective-permute-start(bf16[104,1152]{1,0:T(8,128)(2,1)S(1)} %collective-permute-done.4.refs_2_), channel_id=1, source_target_pairs={{0,4},{1,5},{2,6},{3,7},{4,0},{5,1},{6,2},{7,3},{8,12},{9,13},{10,... | collective-permute-start | bytes 718856 | tf_op jit(solution)/shard_map/ppermute | solution.py:321
  18.0 6.5 %collective-permute-start.7 = (bf16[104,1152]{1,0:T(8,128)(2,1)S(1)}, bf16[104,1152]{1,0:T(8,128)(2,1)S(1)}, u32[]{:S(2)}, u32[]{:S(2)}) collective-permute-start(bf16[104,1152]{1,0:T(8,128)(2,1)S(1)} %collective-permute-done.4.refs_2_), channel_id=1, source_target_pairs={{0,2},{1,3},{2,0},{3,1},{4,6},{5,7},{6,4},{7,5},{8,10},{9,11},{10,... | collective-permute-start | bytes 718856 | tf_op jit(solution)/shard_map/ppermute | solution.py:321
  19.2 5.6 %collective-permute-start.8 = (bf16[104,1152]{1,0:T(8,128)(2,1)S(1)}, bf16[104,1152]{1,0:T(8,128)(2,1)S(1)}, u32[]{:S(2)}, u32[]{:S(2)}) collective-permute-start(bf16[104,1152]{1,0:T(8,128)(2,1)S(1)} %collective-permute-done.4.refs_2_), channel_id=1, source_target_pairs={{0,16},{1,17},{2,18},{3,19},{4,20},{5,21},{6,22},{7,23},{8,24},{9,... | collective-permute-start | bytes 718856 | tf_op jit(solution)/shard_map/ppermute | solution.py:321
  20.4 8.6 %collective-permute-start.5 = (bf16[104,1152]{1,0:T(8,128)(2,1)S(1)}, bf16[104,1152]{1,0:T(8,128)(2,1)S(1)}, u32[]{:S(2)}, u32[]{:S(2)}) collective-permute-start(bf16[104,1152]{1,0:T(8,128)(2,1)S(1)} %get-tuple-element.36.refs_3_), channel_id=1, source_target_pairs={{0,2},{1,3},{2,0},{3,1},{4,6},{5,7},{6,4},{7,5},{8,10},{9,11},{10,... | collective-permute-start | bytes 718856 | tf_op jit(solution)/shard_map/ppermute | solution.py:321
  24.8 9.3 %collective-permute-start.9 = (bf16[104,1152]{1,0:T(8,128)(2,1)S(1)}, bf16[104,1152]{1,0:T(8,128)(2,1)S(1)}, u32[]{:S(2)}, u32[]{:S(2)}) collective-permute-start(bf16[104,1152]{1,0:T(8,128)(2,1)S(1)} %get-tuple-element.38.refs_5_), channel_id=1, source_target_pairs={{0,2},{1,3},{2,0},{3,1},{4,6},{5,7},{6,4},{7,5},{8,10},{9,11},{10,... | collective-permute-start | bytes 718856 | tf_op jit(solution)/shard_map/ppermute | solution.py:321
  25.9 16.3 %collective-permute-start.13 = (bf16[104,1152]{1,0:T(8,128)(2,1)S(1)}, bf16[104,1152]{1,0:T(8,128)(2,1)S(1)}, u32[]{:S(2)}, u32[]{:S(2)}) collective-permute-start(bf16[104,1152]{1,0:T(8,128)(2,1)S(1)} %get-tuple-element.38.refs_5_), channel_id=1, source_target_pairs={{0,16},{1,17},{2,18},{3,19},{4,20},{5,21},{6,22},{7,23},{8,24},{9,... | collective-permute-start | bytes 718856 | tf_op jit(solution)/shard_map/ppermute | solution.py:321
  27.1 9.2 %collective-permute-start.10 = (bf16[104,1152]{1,0:T(8,128)(2,1)S(1)}, bf16[104,1152]{1,0:T(8,128)(2,1)S(1)}, u32[]{:S(2)}, u32[]{:S(2)}) collective-permute-start(bf16[104,1152]{1,0:T(8,128)(2,1)S(1)} %get-tuple-element.40.refs_7_), channel_id=1, source_target_pairs={{0,4},{1,5},{2,6},{3,7},{4,0},{5,1},{6,2},{7,3},{8,12},{9,13},{10,... | collective-permute-start | bytes 718856 | tf_op jit(solution)/shard_map/ppermute | solution.py:321
  29.0 7.3 %collective-permute-start.11 = (bf16[104,1152]{1,0:T(8,128)(2,1)S(1)}, bf16[104,1152]{1,0:T(8,128)(2,1)S(1)}, u32[]{:S(2)}, u32[]{:S(2)}) collective-permute-start(bf16[104,1152]{1,0:T(8,128)(2,1)S(1)} %get-tuple-element.41.refs_8_), channel_id=1, source_target_pairs={{0,4},{1,5},{2,6},{3,7},{4,0},{5,1},{6,2},{7,3},{8,12},{9,13},{10,... | collective-permute-start | bytes 718856 | tf_op jit(solution)/shard_map/ppermute | solution.py:321
  31.7 4.6 %copy-start.1 = (bf16[192,4096]{1,0:T(8,128)(2,1)}, bf16[192,4096]{1,0:T(8,128)(2,1)S(1)}, u32[]{:S(2)}) copy-start(bf16[192,4096]{1,0:T(8,128)(2,1)S(1)} %collective-permute-done.12.refs_5_) | copy-start | bytes 4718596
  31.7 10.5 %collective-permute-start.14 = (bf16[104,1152]{1,0:T(8,128)(2,1)S(1)}, bf16[104,1152]{1,0:T(8,128)(2,1)S(1)}, u32[]{:S(2)}, u32[]{:S(2)}) collective-permute-start(bf16[104,1152]{1,0:T(8,128)(2,1)S(1)} %get-tuple-element.39.refs_6_), channel_id=1, source_target_pairs={{0,16},{1,17},{2,18},{3,19},{4,20},{5,21},{6,22},{7,23},{8,24},{9,... | collective-permute-start | bytes 718856 | tf_op jit(solution)/shard_map/ppermute | solution.py:321
  34.1 8.1 %collective-permute-start.15 = (bf16[104,1152]{1,0:T(8,128)(2,1)S(1)}, bf16[104,1152]{1,0:T(8,128)(2,1)S(1)}, u32[]{:S(2)}, u32[]{:S(2)}) collective-permute-start(bf16[104,1152]{1,0:T(8,128)(2,1)S(1)} %get-tuple-element.38.refs_5_), channel_id=1, source_target_pairs={{0,18},{1,19},{2,16},{3,17},{4,22},{5,23},{6,20},{7,21},{8,26},{9,... | collective-permute-start | bytes 718856 | tf_op jit(solution)/shard_map/ppermute | solution.py:321
  43.6 5.6 %collective-permute-start.16 = (f32[16,192]{1,0:T(8,128)S(1)}, f32[16,192]{1,0:T(8,128)S(1)}, u32[]{:S(2)}, u32[]{:S(2)}) collective-permute-start(f32[16,192]{1,0:T(8,128)S(1)} %get-tuple-element.51), channel_id=1, source_target_pairs={{0,1},{1,0},{2,3},{3,2},{4,5},{5,4},{6,7},{7,6},{8,9},{9,8},{10,11... | collective-permute-start | bytes 36872 | tf_op jit(solution)/shard_map/ppermute | solution.py:321

commit v5 on v4

--- a/solution.py
+++ b/solution.py
@@ -195,10 +195,10 @@
     )(*pieces)
 
 
-def first_kernel(now, later, n_pieces, x_ref, rows_ref, *refs):
+def first_kernel(now, n_pieces, x_ref, rows_ref, *refs):
     pieces, refs = refs[:n_pieces], refs[n_pieces:]
-    tokens, accs, later_ref, staged = refs[:4], refs[4:8], refs[8], refs[9:13]
-    rows, *buffers, sems, staged_sems = refs[13:]
+    tokens, accs, staged = refs[:4], refs[4:8], refs[8:12]
+    rows, *buffers, sems, staged_sems = refs[12:]
     jobs = fetch(x_ref[0], tokens, buffers, sems)
     copies = []
     for j, (src, dst) in enumerate(zip(tokens, staged)):
@@ -212,23 +212,20 @@
         unpack(pieces[p], rows, n + i * ROWS, ew)
     for acc, v in zip(accs, project(rows, jobs, buffers)):
         acc[...] = v
-    for i, p in enumerate(later):
-        unpack(pieces[p], later_ref, i * ROWS, ew)
     for copy in copies:
         copy.wait()
 
 
-def first_half(x, rows, pieces, now, later, tokens):
+def first_half(x, rows, pieces, now, tokens):
     vmem, hbm = pl.BlockSpec(memory_space=pltpu.VMEM), pl.BlockSpec(memory_space=pltpu.HBM)
     n, width = rows.shape[0] + len(now) * ROWS, rows.shape[1]
     acc = jax.ShapeDtypeStruct((n, tokens[0].shape[0]), jnp.float32)
     return pl.pallas_call(
-        functools.partial(first_kernel, now, later, len(pieces)),
+        functools.partial(first_kernel, now, len(pieces)),
         out_shape=(acc,) * 4
-        + (jax.ShapeDtypeStruct((len(later) * ROWS, width), jnp.bfloat16),)
         + tuple(jax.ShapeDtypeStruct((a.shape[0], a.shape[1] // 2), a.dtype) for a in tokens),
         in_specs=[pl.BlockSpec(memory_space=pltpu.SMEM)] + [vmem] * (len(pieces) + 1) + [hbm] * 4,
-        out_specs=(vmem,) * 9,
+        out_specs=(vmem,) * 8,
         scratch_shapes=[pltpu.VMEM((n, width), jnp.bfloat16)]
         + half_scratch(tokens)
         + [pltpu.SemaphoreType.DMA((4,))],
@@ -261,13 +258,13 @@
         out_ref[pl.ds(jnp.bitwise_xor(me, flip), 1), :] = row
 
 
-def mate_kernel(order, n_pieces, me_ref, rows_a, rows_b, *refs):
+def mate_kernel(order, n_pieces, me_ref, rows_ref, *refs):
     pieces, refs = refs[:n_pieces], refs[n_pieces:]
     tokens, accs, (out_ref, rows) = refs[:2], refs[2:4], refs[4:]
-    n, m = rows_a.shape[0], rows_a.shape[0] + rows_b.shape[0]
-    rows[:n], rows[n:m] = rows_a[...], rows_b[...]
+    n = rows_ref.shape[0]
+    rows[:n] = rows_ref[...]
     for i, piece in enumerate(pieces):
-        unpack(piece, rows, m + i * ROWS, 2 * tokens[0].shape[1] // SEGS)
+        unpack(piece, rows, n + i * ROWS, 2 * tokens[0].shape[1] // SEGS)
     scores(order, me_ref[0], side_sums(rows, tokens), accs, out_ref)
 
 
@@ -276,20 +273,20 @@
     scores(order, me_ref[0], side_sums(rows, tokens), accs, out_ref)
 
 
-def mate_scores(me, order, rows_a, rows_b, pieces, tokens, accs):
+def mate_scores(me, order, rows, pieces, tokens, accs):
     vmem, smem = pl.BlockSpec(memory_space=pltpu.VMEM), pl.BlockSpec(memory_space=pltpu.SMEM)
     return pl.pallas_call(
         functools.partial(mate_kernel, order, len(pieces)),
         out_shape=(
             jax.ShapeDtypeStruct((2 * len(order), tokens[0].shape[0]), jnp.float32),
-            jax.ShapeDtypeStruct((len(order) * ROWS, rows_a.shape[1]), jnp.bfloat16),
+            jax.ShapeDtypeStruct((len(order) * ROWS, rows.shape[1]), jnp.bfloat16),
         ),
-        in_specs=[smem] + [vmem] * (6 + len(pieces)),
+        in_specs=[smem] + [vmem] * (5 + len(pieces)),
         out_specs=(vmem, vmem),
         compiler_params=pltpu.CompilerParams(vmem_limit_bytes=LIMIT),
         cost_estimate=weight(5),
         name="mate_scores",
-    )(me, rows_a, rows_b, *pieces, *tokens, *accs)
+    )(me, rows, *pieces, *tokens, *accs)
 
 
 def own_scores(me, order, rows, tokens, accs):
@@ -334,7 +331,7 @@
     y0, z1, y0r = over_y(half), over_z(half, 1), over_y(rest)
     z1, y0, y0r, rest, mate_acts = gate(z1, y0, y0r, rest, mate_acts)
     z2, y3, xa3 = over_z(z3, 1), over_y(z3), over_x(z3)
-    y1, y1r = over_y(z1), over_z(y0r, 1)
+    y1, y1r = over_z(y0, 1), over_z(y0r, 1)
     z2, y3, xa3, rest = gate(z2, y3, xa3, rest)
     y2, xa2, xb3 = over_y(z2), over_x(z2), over_x(y3)
     z1r = over_z(rest, 1)
@@ -342,13 +339,13 @@
         (half, y0, z3, z1, y1, z2, y3, rest, y0r, xa3), tuple(range(7)), (7, 8, 9),
         errors.shape[1] // SEGS,
     )
-    xb2 = over_xy(z2)
+    xb2 = over_x(y2)
 
     tokens = tuple(in_hbm(a) for a in (errors, activations, mate_errs, mate_acts))
-    *accs, late, e0, a0, e1, a1 = first_half(x, mine, (y2, z1r, y1r), (0,), (1, 2), tokens)
+    *accs, e0, a0, e1, a1 = first_half(x, mine, (y2,), (0,), tokens)
     order = (0, 2, 12, 4, 6, 8, 14, 10)
     mates, rows = mate_scores(
-        me, order, others, late, (xa2, xb3, xb2), (e1, a1), accs[2:]
+        me, order, others, (z1r, y1r, xa2, xb3, xb2), (e1, a1), accs[2:]
     )
     return mate(mates) + own_scores(me, order, rows, (e0, a0), accs[:2])
 

time: 50 us -> 48.1 us (0.962)
  starting transfers between devices: 23 us -> 20.4 us
  waiting for transfers between devices: 14.9 us -> 15.4 us
    ppermute x17, starting transfers between devices: 23 us -> 20.4 us  [permuted(): swap = lambda a, gx, bx: lax.ppermute(a, AXES, pairs(n_grp, n_blk, gx, bx))]
    ppermute x17, waiting for transfers between devices: 14.9 us -> 15.4 us  [permuted(): swap = lambda a, gx, bx: lax.ppermute(a, AXES, pairs(n_grp, n_blk, gx, bx))]
where the time goes in v5:
time: 48.1 us; the launch traced here: 47.9 us
  starting transfers between devices  20.4 us (42%)
  waiting for transfers between devices  15.4 us (32%)
  Pallas kernels  11.4 us (24%)
  other arithmetic  0.61 us (1%)
    ppermute x17, starting transfers between devices, permuted(): swap = lambda a, gx, bx: lax.ppermute(a, AXES, pairs(n_grp, n_blk, gx, bx))  20.4 us
    ppermute x17, waiting for transfers between devices, permuted(): swap = lambda a, gx, bx: lax.ppermute(a, AXES, pairs(n_grp, n_blk, gx, bx))  15.4 us
    pallas_call x1, Pallas kernels, first_half(): pl.pallas_call(functools.partial(first_kernel, now, len(pieces)), out_sha...  5.92 us
    pallas_call x1, Pallas kernels, mate_scores(): pl.pallas_call(functools.partial(mate_kernel, order, len(pieces)), out_sh...  1.55 us
    pallas_call x1, Pallas kernels, pack(): pl.pallas_call(pack_kernel, out_shape=(jax.ShapeDtypeStruct((n * RANK, wi...  1.39 us
    pallas_call x1, Pallas kernels, own_scores(): pl.pallas_call(functools.partial(own_kernel, order), out_shape=jax.ShapeD...  1.3 us
  transfers between devices with their start and end apart: 17, of which 6 were waited for; matrix products, arithmetic and copies ran while one was open for 0% of the time, Pallas kernels for 20%

profile of v5, /device:TPU:1, one launch (start us, length us, event | category | flops | bytes accessed | tf_op | source)
XLA Modules:
  0.0 47.9 jit_solution(13349690443135578649)
XLA Ops:
  0.0 0.1 collective-permute-start.3
  0.1 1.4 %pack.1 = (bf16[104,1152]{1,0:T(8,128)(2,1)S(1)}, bf16[2,128,1152]{2,1,0:T(8,128)(2,1)S(1)}) custom-call(s32[1]{0:T(128)} %bitcast.1.x_ref, bf16[1,13,4096]{2,1,0:T(8,128)(2,1)} %err_hbm.1, bf16[1,13,14336]{2,1,0:T(8,128)(2,1)} %act_hbm.1), custom_call_target="tpu_custom_call" | custom-call | tf_op jit(solution)/shard_map/pack/pallas_call | solution.py:68
  1.5 0.0 copy-start
  1.5 0.3 pack_again.1
  1.8 2.8 %collective-permute-start = (bf16[104,1152]{1,0:T(8,128)(2,1)S(1)}, bf16[104,1152]{1,0:T(8,128)(2,1)S(1)}, u32[]{:S(2)}, u32[]{:S(2)}) collective-permute-start(bf16[104,1152]{1,0:T(8,128)(2,1)S(1)} %get-tuple-element.31.refs_0_), channel_id=1, source_target_pairs={{0,4},{1,5},{2,6},{3,7},{4,0},{5,1},{6,2},{7,3},{8,12},{9,13},{10,... | collective-permute-start | bytes 718856 | tf_op jit(solution)/shard_map/ppermute | solution.py:318
  4.6 2.2 %collective-permute-start.4 = (bf16[104,1152]{1,0:T(8,128)(2,1)S(1)}, bf16[104,1152]{1,0:T(8,128)(2,1)S(1)}, u32[]{:S(2)}, u32[]{:S(2)}) collective-permute-start(bf16[104,1152]{1,0:T(8,128)(2,1)S(1)} %get-tuple-element.34), channel_id=1, source_target_pairs={{0,12},{1,13},{2,14},{3,15},{4,8},{5,9},{6,10},{7,11},{8,4},{9,5},... | collective-permute-start | bytes 718856 | tf_op jit(solution)/shard_map/ppermute | solution.py:318
  6.8 1.2 %collective-permute-start.1 = (bf16[104,1152]{1,0:T(8,128)(2,1)S(1)}, bf16[104,1152]{1,0:T(8,128)(2,1)S(1)}, u32[]{:S(2)}, u32[]{:S(2)}) collective-permute-start(bf16[104,1152]{1,0:T(8,128)(2,1)S(1)} %get-tuple-element.31.refs_0_), channel_id=1, source_target_pairs={{0,2},{1,3},{2,0},{3,1},{4,6},{5,7},{6,4},{7,5},{8,10},{9,11},{10,... | collective-permute-start | bytes 718856 | tf_op jit(solution)/shard_map/ppermute | solution.py:318
  8.0 0.2 collective-permute-start.2
  8.3 2.5 %collective-permute-done.refs_0_ = bf16[104,1152]{1,0:T(8,128)(2,1)S(1)} collective-permute-done((bf16[104,1152]{1,0:T(8,128)(2,1)S(1)}, bf16[104,1152]{1,0:T(8,128)(2,1)S(1)}, u32[]{:S(2)}, u32[]{:S(2)}) %collective-permute-start) | collective-permute-done | bytes 239648 | tf_op jit(solution)/shard_map/ppermute | solution.py:318
  10.8 0.0 copy-done
  10.8 0.6 %collective-permute-start.15 = (bf16[192,4096]{1,0:T(8,128)(2,1)S(1)}, bf16[192,4096]{1,0:T(8,128)(2,1)S(1)}, u32[]{:S(2)}, u32[]{:S(2)}) collective-permute-start(bf16[192,4096]{1,0:T(8,128)(2,1)S(1)} %copy-done), channel_id=1, source_target_pairs={{0,1},{1,0},{2,3},{3,2},{4,5},{5,4},{6,7},{7,6},{8,9},{9,8},{10,11... | collective-permute-start | bytes 4718600 | tf_op jit(solution)/shard_map/ppermute | solution.py:318
  11.4 6.6 %collective-permute-done.4.refs_2_ = bf16[104,1152]{1,0:T(8,128)(2,1)S(1)} collective-permute-done((bf16[104,1152]{1,0:T(8,128)(2,1)S(1)}, bf16[104,1152]{1,0:T(8,128)(2,1)S(1)}, u32[]{:S(2)}, u32[]{:S(2)}) %collective-permute-start.4) | collective-permute-done | bytes 239648 | tf_op jit(solution)/shard_map/ppermute | solution.py:318
  18.0 0.0 collective-permute-start.6
  18.0 0.0 collective-permute-done.1.refs_1_
  18.0 1.2 %collective-permute-start.7 = (bf16[104,1152]{1,0:T(8,128)(2,1)S(1)}, bf16[104,1152]{1,0:T(8,128)(2,1)S(1)}, u32[]{:S(2)}, u32[]{:S(2)}) collective-permute-start(bf16[104,1152]{1,0:T(8,128)(2,1)S(1)} %collective-permute-done.4.refs_2_), channel_id=1, source_target_pairs={{0,2},{1,3},{2,0},{3,1},{4,6},{5,7},{6,4},{7,5},{8,10},{9,11},{10,... | collective-permute-start | bytes 718856 | tf_op jit(solution)/shard_map/ppermute | solution.py:318
  19.2 0.0 collective-permute-done.2.refs_2_
  19.2 1.2 %collective-permute-start.8 = (bf16[104,1152]{1,0:T(8,128)(2,1)S(1)}, bf16[104,1152]{1,0:T(8,128)(2,1)S(1)}, u32[]{:S(2)}, u32[]{:S(2)}) collective-permute-start(bf16[104,1152]{1,0:T(8,128)(2,1)S(1)} %collective-permute-done.4.refs_2_), channel_id=1, source_target_pairs={{0,16},{1,17},{2,18},{3,19},{4,20},{5,21},{6,22},{7,23},{8,24},{9,... | collective-permute-start | bytes 718856 | tf_op jit(solution)/shard_map/ppermute | solution.py:318
  20.4 0.0 collective-permute-done.3.refs_4_
  20.4 1.5 %collective-permute-start.5 = (bf16[104,1152]{1,0:T(8,128)(2,1)S(1)}, bf16[104,1152]{1,0:T(8,128)(2,1)S(1)}, u32[]{:S(2)}, u32[]{:S(2)}) collective-permute-start(bf16[104,1152]{1,0:T(8,128)(2,1)S(1)} %get-tuple-element.33.refs_1_), channel_id=1, source_target_pairs={{0,4},{1,5},{2,6},{3,7},{4,0},{5,1},{6,2},{7,3},{8,12},{9,13},{10,... | collective-permute-start | bytes 718856 | tf_op jit(solution)/shard_map/ppermute | solution.py:318
  21.9 2.6 %collective-permute-done.6.refs_0_ = bf16[104,1152]{1,0:T(8,128)(2,1)S(1)} collective-permute-done((bf16[104,1152]{1,0:T(8,128)(2,1)S(1)}, bf16[104,1152]{1,0:T(8,128)(2,1)S(1)}, u32[]{:S(2)}, u32[]{:S(2)}) %collective-permute-start.6) | collective-permute-done | bytes 239648 | tf_op jit(solution)/shard_map/ppermute | solution.py:318
  24.5 0.0 collective-permute-done.7.refs_1_
  24.5 0.4 collective-permute-done.8.refs_2_
  24.8 1.0 %collective-permute-start.13 = (bf16[104,1152]{1,0:T(8,128)(2,1)S(1)}, bf16[104,1152]{1,0:T(8,128)(2,1)S(1)}, u32[]{:S(2)}, u32[]{:S(2)}) collective-permute-start(bf16[104,1152]{1,0:T(8,128)(2,1)S(1)} %get-tuple-element.37.refs_5_), channel_id=1, source_target_pairs={{0,2},{1,3},{2,0},{3,1},{4,6},{5,7},{6,4},{7,5},{8,10},{9,11},{10,... | collective-permute-start | bytes 718856 | tf_op jit(solution)/shard_map/ppermute | solution.py:318
  25.9 1.2 %collective-permute-start.11 = (bf16[104,1152]{1,0:T(8,128)(2,1)S(1)}, bf16[104,1152]{1,0:T(8,128)(2,1)S(1)}, u32[]{:S(2)}, u32[]{:S(2)}) collective-permute-start(bf16[104,1152]{1,0:T(8,128)(2,1)S(1)} %get-tuple-element.37.refs_5_), channel_id=1, source_target_pairs={{0,16},{1,17},{2,18},{3,19},{4,20},{5,21},{6,22},{7,23},{8,24},{9,... | collective-permute-start | bytes 718856 | tf_op jit(solution)/shard_map/ppermute | solution.py:318
  27.1 0.3 collective-permute-start.12
  27.3 2.3 %collective-permute-done.5.refs_4_ = bf16[104,1152]{1,0:T(8,128)(2,1)S(1)} collective-permute-done((bf16[104,1152]{1,0:T(8,128)(2,1)S(1)}, bf16[104,1152]{1,0:T(8,128)(2,1)S(1)}, u32[]{:S(2)}, u32[]{:S(2)}) %collective-permute-start.5) | collective-permute-done | bytes 239648 | tf_op jit(solution)/shard_map/ppermute | solution.py:318
  29.6 0.2 collective-permute-start.9
  29.8 0.9 %unpacked.1 = (bf16[112,9216]{1,0:T(8,128)(2,1)S(1)}, bf16[48,9216]{1,0:T(8,128)(2,1)S(1)}) custom-call(bf16[104,1152]{1,0:T(8,128)(2,1)S(1)} %get-tuple-element.31.refs_0_, bf16[104,1152]{1,0:T(8,128)(2,1)S(1)} %get-tuple-element.33.refs_1_, bf16[104,1152]{1,0:T(8,128)(2,1)S(1)} %collective-permute-done.4.refs_2_, ...), custom_call_target="tpu_custom_call" | custom-call | flops 8000000000 | bytes 24000000 | tf_op jit(solution)/shard_map/unpacked/pallas_call | solution.py:185
  30.7 0.0 collective-permute-done.15.refs_3_
  30.7 0.0 copy-start.1
  30.7 1.3 %collective-permute-start.10 = (bf16[104,1152]{1,0:T(8,128)(2,1)S(1)}, bf16[104,1152]{1,0:T(8,128)(2,1)S(1)}, u32[]{:S(2)}, u32[]{:S(2)}) collective-permute-start(bf16[104,1152]{1,0:T(8,128)(2,1)S(1)} %get-tuple-element.40.refs_8_), channel_id=1, source_target_pairs={{0,4},{1,5},{2,6},{3,7},{4,0},{5,1},{6,2},{7,3},{8,12},{9,13},{10,... | collective-permute-start | bytes 718856 | tf_op jit(solution)/shard_map/ppermute | solution.py:318
  32.1 0.0 collective-permute-done.13.refs_0_
  32.1 1.2 %collective-permute-start.14 = (bf16[104,1152]{1,0:T(8,128)(2,1)S(1)}, bf16[104,1152]{1,0:T(8,128)(2,1)S(1)}, u32[]{:S(2)}, u32[]{:S(2)}) collective-permute-start(bf16[104,1152]{1,0:T(8,128)(2,1)S(1)} %collective-permute-done.13.refs_0_), channel_id=1, source_target_pairs={{0,16},{1,17},{2,18},{3,19},{4,20},{5,21},{6,22},{7,23},{8,24},{9,... | collective-permute-start | bytes 718856 | tf_op jit(solution)/shard_map/ppermute | solution.py:318
  33.3 0.0 copy-done.1
  33.3 5.9 %first_half.1 = (f32[128,192]{1,0:T(8,128)S(1)}, f32[128,192]{1,0:T(8,128)S(1)}, f32[128,192]{1,0:T(8,128)S(1)}, f32[128,192]{1,0:T(8,128)S(1)}, bf16[192,2048]{...) custom-call(s32[1]{0:T(128)} %bitcast.1.x_ref, ...), custom_call_target="tpu_custom_call" | custom-call | flops 12000000000 | bytes 36000000 | tf_op jit(solution)/shard_map/first_half/pallas_call | solution.py:223
  39.2 0.0 collective-permute-done.11.refs_2_
  39.2 0.0 collective-permute-done.12.refs_3_
  39.2 0.0 collective-permute-done.9.refs_0_
  39.2 1.1 %collective-permute-done.10.refs_1_ = bf16[104,1152]{1,0:T(8,128)(2,1)S(1)} collective-permute-done((bf16[104,1152]{1,0:T(8,128)(2,1)S(1)}, bf16[104,1152]{1,0:T(8,128)(2,1)S(1)}, u32[]{:S(2)}, u32[]{:S(2)}) %collective-permute-start.10) | collective-permute-done | bytes 239648 | tf_op jit(solution)/shard_map/ppermute | solution.py:318
  40.3 0.0 collective-permute-done.14.refs_4_
  40.3 1.6 %mate_scores.1 = (f32[16,192]{1,0:T(8,128)S(1)}, bf16[128,9216]{1,0:T(8,128)(2,1)S(1)}) custom-call(s32[1]{0:T(128)} %bitcast.me_ref, bf16[48,9216]{1,0:T(8,128)(2,1)S(1)} %get-tuple-element.42.rows_ref, bf16[104,1152]{1,0:T(8,128)(2,1)S(1)} %collective-permute-done.9.refs_0_, bf16[104,1152]{1,0:T(8,128)(2,1)S(1)} %collective-permute-done.10.refs_1_, ...), custom_call_target="tpu_custom_call" | custom-call | flops 5000000000 | bytes 15000000 | tf_op jit(solution)/shard_map/mate_scores/pallas_call | solution.py:278
  41.9 4.1 %collective-permute-start.16 = (f32[16,192]{1,0:T(8,128)S(1)}, f32[16,192]{1,0:T(8,128)S(1)}, u32[]{:S(2)}, u32[]{:S(2)}) collective-permute-start(f32[16,192]{1,0:T(8,128)S(1)} %get-tuple-element.49), channel_id=1, source_target_pairs={{0,1},{1,0},{2,3},{3,2},{4,5},{5,4},{6,7},{7,6},{8,9},{9,8},{10,11... | collective-permute-start | bytes 36872 | tf_op jit(solution)/shard_map/ppermute | solution.py:318
  46.0 1.3 %own_scores.1 = f32[16,192]{1,0:T(8,128)S(1)} custom-call(s32[1]{0:T(128)} %bitcast.me_ref, bf16[128,9216]{1,0:T(8,128)(2,1)S(1)} %get-tuple-element.50.rows, bf16[192,2048]{1,0:T(8,128)(2,1)S(1)} %get-tuple-element.51.refs_0_, bf16[192,7168]{1,0:T(8,128)(2,1)S(1)} %get-tuple-element.52.refs_1_, f32[128,192]{1,0:T(8,128)S(1)} %get-tuple-element.53.refs_2_, ...), custom_call_target="tpu_custom_call" | custom-call | flops 30000001024 | bytes 90000000 | tf_op jit(solution)/shard_map/own_scores/pallas_call | solution.py:294
  47.3 0.0 collective-permute-done.16
  47.3 0.6 %add.3 = f32[16,192]{1,0:T(8,128)} add(f32[16,192]{1,0:T(8,128)S(1)} %collective-permute-done.16, f32[16,192]{1,0:T(8,128)S(1)} %own_scores.1) | non-fusion elementwise | flops 3072 | bytes 36864 | tf_op jit(solution)/shard_map/add | solution.py:350
  (2 shorter events, 0.0 us)
Async XLA Ops:
  0.0 20.4 %collective-permute-start.3 = (bf16[192,14336]{1,0:T(8,128)(2,1)}, bf16[192,14336]{1,0:T(8,128)(2,1)}, u32[]{:S(2)}, u32[]{:S(2)}) collective-permute-start(bf16[192,14336]{1,0:T(8,128)(2,1)} %refs_2_.1), channel_id=1, source_target_pairs={{0,1},{1,0},{2,3},{3,2},{4,5},{5,4},{6,7},{7,6},{8,9},{9,8},{10,11... | collective-permute-start | bytes 16515080 | tf_op jit(solution)/shard_map/ppermute | solution.py:318
  1.5 9.3 %copy-start = (bf16[192,4096]{1,0:T(8,128)(2,1)S(1)}, bf16[192,4096]{1,0:T(8,128)(2,1)}, u32[]{:S(2)}) copy-start(bf16[192,4096]{1,0:T(8,128)(2,1)} %refs_1_.1) | copy-start | bytes 4718596
  1.8 9.0 %collective-permute-start = (bf16[104,1152]{1,0:T(8,128)(2,1)S(1)}, bf16[104,1152]{1,0:T(8,128)(2,1)S(1)}, u32[]{:S(2)}, u32[]{:S(2)}) collective-permute-start(bf16[104,1152]{1,0:T(8,128)(2,1)S(1)} %get-tuple-element.31.refs_0_), channel_id=1, source_target_pairs={{0,4},{1,5},{2,6},{3,7},{4,0},{5,1},{6,2},{7,3},{8,12},{9,13},{10,... | collective-permute-start | bytes 718856 | tf_op jit(solution)/shard_map/ppermute | solution.py:318
  4.6 13.4 %collective-permute-start.4 = (bf16[104,1152]{1,0:T(8,128)(2,1)S(1)}, bf16[104,1152]{1,0:T(8,128)(2,1)S(1)}, u32[]{:S(2)}, u32[]{:S(2)}) collective-permute-start(bf16[104,1152]{1,0:T(8,128)(2,1)S(1)} %get-tuple-element.34), channel_id=1, source_target_pairs={{0,12},{1,13},{2,14},{3,15},{4,8},{5,9},{6,10},{7,11},{8,4},{9,5},... | collective-permute-start | bytes 718856 | tf_op jit(solution)/shard_map/ppermute | solution.py:318
  6.8 11.2 %collective-permute-start.1 = (bf16[104,1152]{1,0:T(8,128)(2,1)S(1)}, bf16[104,1152]{1,0:T(8,128)(2,1)S(1)}, u32[]{:S(2)}, u32[]{:S(2)}) collective-permute-start(bf16[104,1152]{1,0:T(8,128)(2,1)S(1)} %get-tuple-element.31.refs_0_), channel_id=1, source_target_pairs={{0,2},{1,3},{2,0},{3,1},{4,6},{5,7},{6,4},{7,5},{8,10},{9,11},{10,... | collective-permute-start | bytes 718856 | tf_op jit(solution)/shard_map/ppermute | solution.py:318
  8.0 11.2 %collective-permute-start.2 = (bf16[104,1152]{1,0:T(8,128)(2,1)S(1)}, bf16[104,1152]{1,0:T(8,128)(2,1)S(1)}, u32[]{:S(2)}, u32[]{:S(2)}) collective-permute-start(bf16[104,1152]{1,0:T(8,128)(2,1)S(1)} %get-tuple-element.32.refs_3_), channel_id=1, source_target_pairs={{0,2},{1,3},{2,0},{3,1},{4,6},{5,7},{6,4},{7,5},{8,10},{9,11},{10,... | collective-permute-start | bytes 718856 | tf_op jit(solution)/shard_map/ppermute | solution.py:318
  10.8 19.9 %collective-permute-start.15 = (bf16[192,4096]{1,0:T(8,128)(2,1)S(1)}, bf16[192,4096]{1,0:T(8,128)(2,1)S(1)}, u32[]{:S(2)}, u32[]{:S(2)}) collective-permute-start(bf16[192,4096]{1,0:T(8,128)(2,1)S(1)} %copy-done), channel_id=1, source_target_pairs={{0,1},{1,0},{2,3},{3,2},{4,5},{5,4},{6,7},{7,6},{8,9},{9,8},{10,11... | collective-permute-start | bytes 4718600 | tf_op jit(solution)/shard_map/ppermute | solution.py:318
  18.0 6.5 %collective-permute-start.6 = (bf16[104,1152]{1,0:T(8,128)(2,1)S(1)}, bf16[104,1152]{1,0:T(8,128)(2,1)S(1)}, u32[]{:S(2)}, u32[]{:S(2)}) collective-permute-start(bf16[104,1152]{1,0:T(8,128)(2,1)S(1)} %collective-permute-done.4.refs_2_), channel_id=1, source_target_pairs={{0,4},{1,5},{2,6},{3,7},{4,0},{5,1},{6,2},{7,3},{8,12},{9,13},{10,... | collective-permute-start | bytes 718856 | tf_op jit(solution)/shard_map/ppermute | solution.py:318
  18.0 6.5 %collective-permute-start.7 = (bf16[104,1152]{1,0:T(8,128)(2,1)S(1)}, bf16[104,1152]{1,0:T(8,128)(2,1)S(1)}, u32[]{:S(2)}, u32[]{:S(2)}) collective-permute-start(bf16[104,1152]{1,0:T(8,128)(2,1)S(1)} %collective-permute-done.4.refs_2_), channel_id=1, source_target_pairs={{0,2},{1,3},{2,0},{3,1},{4,6},{5,7},{6,4},{7,5},{8,10},{9,11},{10,... | collective-permute-start | bytes 718856 | tf_op jit(solution)/shard_map/ppermute | solution.py:318
  19.2 5.6 %collective-permute-start.8 = (bf16[104,1152]{1,0:T(8,128)(2,1)S(1)}, bf16[104,1152]{1,0:T(8,128)(2,1)S(1)}, u32[]{:S(2)}, u32[]{:S(2)}) collective-permute-start(bf16[104,1152]{1,0:T(8,128)(2,1)S(1)} %collective-permute-done.4.refs_2_), channel_id=1, source_target_pairs={{0,16},{1,17},{2,18},{3,19},{4,20},{5,21},{6,22},{7,23},{8,24},{9,... | collective-permute-start | bytes 718856 | tf_op jit(solution)/shard_map/ppermute | solution.py:318
  20.4 9.2 %collective-permute-start.5 = (bf16[104,1152]{1,0:T(8,128)(2,1)S(1)}, bf16[104,1152]{1,0:T(8,128)(2,1)S(1)}, u32[]{:S(2)}, u32[]{:S(2)}) collective-permute-start(bf16[104,1152]{1,0:T(8,128)(2,1)S(1)} %get-tuple-element.33.refs_1_), channel_id=1, source_target_pairs={{0,4},{1,5},{2,6},{3,7},{4,0},{5,1},{6,2},{7,3},{8,12},{9,13},{10,... | collective-permute-start | bytes 718856 | tf_op jit(solution)/shard_map/ppermute | solution.py:318
  24.8 7.2 %collective-permute-start.13 = (bf16[104,1152]{1,0:T(8,128)(2,1)S(1)}, bf16[104,1152]{1,0:T(8,128)(2,1)S(1)}, u32[]{:S(2)}, u32[]{:S(2)}) collective-permute-start(bf16[104,1152]{1,0:T(8,128)(2,1)S(1)} %get-tuple-element.37.refs_5_), channel_id=1, source_target_pairs={{0,2},{1,3},{2,0},{3,1},{4,6},{5,7},{6,4},{7,5},{8,10},{9,11},{10,... | collective-permute-start | bytes 718856 | tf_op jit(solution)/shard_map/ppermute | solution.py:318
  25.9 13.3 %collective-permute-start.11 = (bf16[104,1152]{1,0:T(8,128)(2,1)S(1)}, bf16[104,1152]{1,0:T(8,128)(2,1)S(1)}, u32[]{:S(2)}, u32[]{:S(2)}) collective-permute-start(bf16[104,1152]{1,0:T(8,128)(2,1)S(1)} %get-tuple-element.37.refs_5_), channel_id=1, source_target_pairs={{0,16},{1,17},{2,18},{3,19},{4,20},{5,21},{6,22},{7,23},{8,24},{9,... | collective-permute-start | bytes 718856 | tf_op jit(solution)/shard_map/ppermute | solution.py:318
  27.1 12.1 %collective-permute-start.12 = (bf16[104,1152]{1,0:T(8,128)(2,1)S(1)}, bf16[104,1152]{1,0:T(8,128)(2,1)S(1)}, u32[]{:S(2)}, u32[]{:S(2)}) collective-permute-start(bf16[104,1152]{1,0:T(8,128)(2,1)S(1)} %get-tuple-element.38.refs_6_), channel_id=1, source_target_pairs={{0,16},{1,17},{2,18},{3,19},{4,20},{5,21},{6,22},{7,23},{8,24},{9,... | collective-permute-start | bytes 718856 | tf_op jit(solution)/shard_map/ppermute | solution.py:318
  29.6 9.6 %collective-permute-start.9 = (bf16[104,1152]{1,0:T(8,128)(2,1)S(1)}, bf16[104,1152]{1,0:T(8,128)(2,1)S(1)}, u32[]{:S(2)}, u32[]{:S(2)}) collective-permute-start(bf16[104,1152]{1,0:T(8,128)(2,1)S(1)} %get-tuple-element.39.refs_7_), channel_id=1, source_target_pairs={{0,4},{1,5},{2,6},{3,7},{4,0},{5,1},{6,2},{7,3},{8,12},{9,13},{10,... | collective-permute-start | bytes 718856 | tf_op jit(solution)/shard_map/ppermute | solution.py:318
  30.7 2.6 %copy-start.1 = (bf16[192,4096]{1,0:T(8,128)(2,1)}, bf16[192,4096]{1,0:T(8,128)(2,1)S(1)}, u32[]{:S(2)}) copy-start(bf16[192,4096]{1,0:T(8,128)(2,1)S(1)} %collective-permute-done.15.refs_3_) | copy-start | bytes 4718596
  30.7 9.6 %collective-permute-start.10 = (bf16[104,1152]{1,0:T(8,128)(2,1)S(1)}, bf16[104,1152]{1,0:T(8,128)(2,1)S(1)}, u32[]{:S(2)}, u32[]{:S(2)}) collective-permute-start(bf16[104,1152]{1,0:T(8,128)(2,1)S(1)} %get-tuple-element.40.refs_8_), channel_id=1, source_target_pairs={{0,4},{1,5},{2,6},{3,7},{4,0},{5,1},{6,2},{7,3},{8,12},{9,13},{10,... | collective-permute-start | bytes 718856 | tf_op jit(solution)/shard_map/ppermute | solution.py:318
  32.1 8.2 %collective-permute-start.14 = (bf16[104,1152]{1,0:T(8,128)(2,1)S(1)}, bf16[104,1152]{1,0:T(8,128)(2,1)S(1)}, u32[]{:S(2)}, u32[]{:S(2)}) collective-permute-start(bf16[104,1152]{1,0:T(8,128)(2,1)S(1)} %collective-permute-done.13.refs_0_), channel_id=1, source_target_pairs={{0,16},{1,17},{2,18},{3,19},{4,20},{5,21},{6,22},{7,23},{8,24},{9,... | collective-permute-start | bytes 718856 | tf_op jit(solution)/shard_map/ppermute | solution.py:318
  41.9 5.4 %collective-permute-start.16 = (f32[16,192]{1,0:T(8,128)S(1)}, f32[16,192]{1,0:T(8,128)S(1)}, u32[]{:S(2)}, u32[]{:S(2)}) collective-permute-start(f32[16,192]{1,0:T(8,128)S(1)} %get-tuple-element.49), channel_id=1, source_target_pairs={{0,1},{1,0},{2,3},{3,2},{4,5},{5,4},{6,7},{7,6},{8,9},{9,8},{10,11... | collective-permute-start | bytes 36872 | tf_op jit(solution)/shard_map/ppermute | solution.py:318

commit v6 on v5

--- a/solution.py
+++ b/solution.py
@@ -329,11 +329,11 @@
     z3 = over_z(half, 3)
     half, rest = pack_again(x, runs)
     y0, z1, y0r = over_y(half), over_z(half, 1), over_y(rest)
-    z1, y0, y0r, rest, mate_acts = gate(z1, y0, y0r, rest, mate_acts)
+    y0, y0r, rest, mate_acts = gate(y0, y0r, rest, mate_acts)
     z2, y3, xa3 = over_z(z3, 1), over_y(z3), over_x(z3)
     y1, y1r = over_z(y0, 1), over_z(y0r, 1)
-    z2, y3, xa3, rest = gate(z2, y3, xa3, rest)
-    y2, xa2, xb3 = over_y(z2), over_x(z2), over_x(y3)
+    z2, y3, xa3, rest, z1 = gate(z2, y3, xa3, rest, z1)
+    y2, xa2, xb3 = over_y(z2), over_x(z2), over_y(xa3)
     z1r = over_z(rest, 1)
     mine, others = unpacked(
         (half, y0, z3, z1, y1, z2, y3, rest, y0r, xa3), tuple(range(7)), (7, 8, 9),

time: 48.1 us -> 46 us (0.956)
  waiting for transfers between devices: 15.4 us -> 11.7 us
  starting transfers between devices: 20.4 us -> 22 us
    ppermute x17, waiting for transfers between devices: 15.4 us -> 11.7 us  [permuted(): swap = lambda a, gx, bx: lax.ppermute(a, AXES, pairs(n_grp, n_blk, gx, bx))]
    ppermute x17, starting transfers between devices: 20.4 us -> 22 us  [permuted(): swap = lambda a, gx, bx: lax.ppermute(a, AXES, pairs(n_grp, n_blk, gx, bx))]
  transfers between devices with their start and end apart: 17 -> 17, of which waited for: 6 -> 6; matrix products, arithmetic and copies ran while one was open for 0% -> 0% of each run, Pallas kernels for 20% -> 21%
where the time goes in v6:
time: 46 us; the launch traced here: 45.9 us
  starting transfers between devices  22 us (48%)
  waiting for transfers between devices  11.7 us (25%)
  Pallas kernels  11.4 us (25%)
  other arithmetic  0.61 us (1%)
    ppermute x17, starting transfers between devices, permuted(): swap = lambda a, gx, bx: lax.ppermute(a, AXES, pairs(n_grp, n_blk, gx, bx))  22 us
    ppermute x17, waiting for transfers between devices, permuted(): swap = lambda a, gx, bx: lax.ppermute(a, AXES, pairs(n_grp, n_blk, gx, bx))  11.7 us
    pallas_call x1, Pallas kernels, first_half(): pl.pallas_call(functools.partial(first_kernel, now, len(pieces)), out_sha...  5.92 us
    pallas_call x1, Pallas kernels, mate_scores(): pl.pallas_call(functools.partial(mate_kernel, order, len(pieces)), out_sh...  1.57 us
    pallas_call x1, Pallas kernels, pack(): pl.pallas_call(pack_kernel, out_shape=(jax.ShapeDtypeStruct((n * RANK, wi...  1.39 us
    pallas_call x1, Pallas kernels, own_scores(): pl.pallas_call(functools.partial(own_kernel, order), out_shape=jax.ShapeD...  1.31 us
  transfers between devices with their start and end apart: 17, of which 6 were waited for; matrix products, arithmetic and copies ran while one was open for 0% of the time, Pallas kernels for 21%

profile of v6, /device:TPU:1, one launch (start us, length us, event | category | flops | bytes accessed | tf_op | source)
XLA Modules:
  0.0 45.9 jit_solution(9584222443153925441)
XLA Ops:
  0.0 0.1 collective-permute-start.2
  0.1 1.4 %pack.1 = (bf16[104,1152]{1,0:T(8,128)(2,1)S(1)}, bf16[2,128,1152]{2,1,0:T(8,128)(2,1)S(1)}) custom-call(s32[1]{0:T(128)} %bitcast.1.x_ref, bf16[1,13,4096]{2,1,0:T(8,128)(2,1)} %err_hbm.1, bf16[1,13,14336]{2,1,0:T(8,128)(2,1)} %act_hbm.1), custom_call_target="tpu_custom_call" | custom-call | tf_op jit(solution)/shard_map/pack/pallas_call | solution.py:68
  1.5 0.0 copy-start
  1.5 0.3 pack_again.1
  1.8 2.8 %collective-permute-start = (bf16[104,1152]{1,0:T(8,128)(2,1)S(1)}, bf16[104,1152]{1,0:T(8,128)(2,1)S(1)}, u32[]{:S(2)}, u32[]{:S(2)}) collective-permute-start(bf16[104,1152]{1,0:T(8,128)(2,1)S(1)} %get-tuple-element.31.refs_0_), channel_id=1, source_target_pairs={{0,2},{1,3},{2,0},{3,1},{4,6},{5,7},{6,4},{7,5},{8,10},{9,11},{10,... | collective-permute-start | bytes 718856 | tf_op jit(solution)/shard_map/ppermute | solution.py:318
  4.5 3.3 %collective-permute-start.3 = (bf16[104,1152]{1,0:T(8,128)(2,1)S(1)}, bf16[104,1152]{1,0:T(8,128)(2,1)S(1)}, u32[]{:S(2)}, u32[]{:S(2)}) collective-permute-start(bf16[104,1152]{1,0:T(8,128)(2,1)S(1)} %get-tuple-element.34), channel_id=1, source_target_pairs={{0,12},{1,13},{2,14},{3,15},{4,8},{5,9},{6,10},{7,11},{8,4},{9,5},... | collective-permute-start | bytes 718856 | tf_op jit(solution)/shard_map/ppermute | solution.py:318
  7.9 0.2 collective-permute-start.1
  8.1 0.0 collective-permute-start.7
  8.1 2.6 %collective-permute-done.refs_0_ = bf16[104,1152]{1,0:T(8,128)(2,1)S(1)} collective-permute-done((bf16[104,1152]{1,0:T(8,128)(2,1)S(1)}, bf16[104,1152]{1,0:T(8,128)(2,1)S(1)}, u32[]{:S(2)}, u32[]{:S(2)}) %collective-permute-start) | collective-permute-done | bytes 239648 | tf_op jit(solution)/shard_map/ppermute | solution.py:318
  10.7 0.0 copy-done
  10.7 0.8 %collective-permute-start.15 = (bf16[192,4096]{1,0:T(8,128)(2,1)S(1)}, bf16[192,4096]{1,0:T(8,128)(2,1)S(1)}, u32[]{:S(2)}, u32[]{:S(2)}) collective-permute-start(bf16[192,4096]{1,0:T(8,128)(2,1)S(1)} %copy-done), channel_id=1, source_target_pairs={{0,1},{1,0},{2,3},{3,2},{4,5},{5,4},{6,7},{7,6},{8,9},{9,8},{10,11... | collective-permute-start | bytes 4718600 | tf_op jit(solution)/shard_map/ppermute | solution.py:318
  11.5 2.2 %collective-permute-done.3.refs_2_ = bf16[104,1152]{1,0:T(8,128)(2,1)S(1)} collective-permute-done((bf16[104,1152]{1,0:T(8,128)(2,1)S(1)}, bf16[104,1152]{1,0:T(8,128)(2,1)S(1)}, u32[]{:S(2)}, u32[]{:S(2)}) %collective-permute-start.3) | collective-permute-done | bytes 239648 | tf_op jit(solution)/shard_map/ppermute | solution.py:318
  13.7 4.4 %collective-permute-start.4 = (bf16[104,1152]{1,0:T(8,128)(2,1)S(1)}, bf16[104,1152]{1,0:T(8,128)(2,1)S(1)}, u32[]{:S(2)}, u32[]{:S(2)}) collective-permute-start(bf16[104,1152]{1,0:T(8,128)(2,1)S(1)} %collective-permute-done.3.refs_2_), channel_id=1, source_target_pairs={{0,4},{1,5},{2,6},{3,7},{4,0},{5,1},{6,2},{7,3},{8,12},{9,13},{10,... | collective-permute-start | bytes 718856 | tf_op jit(solution)/shard_map/ppermute | solution.py:318
  18.1 0.0 collective-permute-done.1.refs_1_
  18.1 0.2 collective-permute-start.5
  18.3 0.0 collective-permute-done.2.refs_3_
  18.3 1.2 %collective-permute-start.6 = (bf16[104,1152]{1,0:T(8,128)(2,1)S(1)}, bf16[104,1152]{1,0:T(8,128)(2,1)S(1)}, u32[]{:S(2)}, u32[]{:S(2)}) collective-permute-start(bf16[104,1152]{1,0:T(8,128)(2,1)S(1)} %collective-permute-done.3.refs_2_), channel_id=1, source_target_pairs={{0,16},{1,17},{2,18},{3,19},{4,20},{5,21},{6,22},{7,23},{8,24},{9,... | collective-permute-start | bytes 718856 | tf_op jit(solution)/shard_map/ppermute | solution.py:318
  19.5 0.0 collective-permute-done.7.refs_4_
  19.5 0.6 %collective-permute-start.8 = (bf16[104,1152]{1,0:T(8,128)(2,1)S(1)}, bf16[104,1152]{1,0:T(8,128)(2,1)S(1)}, u32[]{:S(2)}, u32[]{:S(2)}) collective-permute-start(bf16[104,1152]{1,0:T(8,128)(2,1)S(1)} %get-tuple-element.33.refs_1_), channel_id=1, source_target_pairs={{0,4},{1,5},{2,6},{3,7},{4,0},{5,1},{6,2},{7,3},{8,12},{9,13},{10,... | collective-permute-start | bytes 718856 | tf_op jit(solution)/shard_map/ppermute | solution.py:318
  20.2 3.2 %collective-permute-done.4.refs_0_ = bf16[104,1152]{1,0:T(8,128)(2,1)S(1)} collective-permute-done((bf16[104,1152]{1,0:T(8,128)(2,1)S(1)}, bf16[104,1152]{1,0:T(8,128)(2,1)S(1)}, u32[]{:S(2)}, u32[]{:S(2)}) %collective-permute-start.4) | collective-permute-done | bytes 239648 | tf_op jit(solution)/shard_map/ppermute | solution.py:318
  23.4 0.7 %collective-permute-done.5.refs_1_ = bf16[104,1152]{1,0:T(8,128)(2,1)S(1)} collective-permute-done((bf16[104,1152]{1,0:T(8,128)(2,1)S(1)}, bf16[104,1152]{1,0:T(8,128)(2,1)S(1)}, u32[]{:S(2)}, u32[]{:S(2)}) %collective-permute-start.5) | collective-permute-done | bytes 239648 | tf_op jit(solution)/shard_map/ppermute | solution.py:318
  24.0 0.0 collective-permute-done.6.refs_2_
  24.0 1.2 %collective-permute-start.13 = (bf16[104,1152]{1,0:T(8,128)(2,1)S(1)}, bf16[104,1152]{1,0:T(8,128)(2,1)S(1)}, u32[]{:S(2)}, u32[]{:S(2)}) collective-permute-start(bf16[104,1152]{1,0:T(8,128)(2,1)S(1)} %get-tuple-element.37.refs_5_), channel_id=1, source_target_pairs={{0,2},{1,3},{2,0},{3,1},{4,6},{5,7},{6,4},{7,5},{8,10},{9,11},{10,... | collective-permute-start | bytes 718856 | tf_op jit(solution)/shard_map/ppermute | solution.py:318
  25.2 1.2 %collective-permute-start.11 = (bf16[104,1152]{1,0:T(8,128)(2,1)S(1)}, bf16[104,1152]{1,0:T(8,128)(2,1)S(1)}, u32[]{:S(2)}, u32[]{:S(2)}) collective-permute-start(bf16[104,1152]{1,0:T(8,128)(2,1)S(1)} %get-tuple-element.37.refs_5_), channel_id=1, source_target_pairs={{0,16},{1,17},{2,18},{3,19},{4,20},{5,21},{6,22},{7,23},{8,24},{9,... | collective-permute-start | bytes 718856 | tf_op jit(solution)/shard_map/ppermute | solution.py:318
  26.4 0.3 collective-permute-start.12
  26.7 1.8 %collective-permute-done.8.refs_4_ = bf16[104,1152]{1,0:T(8,128)(2,1)S(1)} collective-permute-done((bf16[104,1152]{1,0:T(8,128)(2,1)S(1)}, bf16[104,1152]{1,0:T(8,128)(2,1)S(1)}, u32[]{:S(2)}, u32[]{:S(2)}) %collective-permute-start.8) | collective-permute-done | bytes 239648 | tf_op jit(solution)/shard_map/ppermute | solution.py:318
  28.5 1.1 %collective-permute-start.9 = (bf16[104,1152]{1,0:T(8,128)(2,1)S(1)}, bf16[104,1152]{1,0:T(8,128)(2,1)S(1)}, u32[]{:S(2)}, u32[]{:S(2)}) collective-permute-start(bf16[104,1152]{1,0:T(8,128)(2,1)S(1)} %get-tuple-element.39.refs_7_), channel_id=1, source_target_pairs={{0,4},{1,5},{2,6},{3,7},{4,0},{5,1},{6,2},{7,3},{8,12},{9,13},{10,... | collective-permute-start | bytes 718856 | tf_op jit(solution)/shard_map/ppermute | solution.py:318
  29.6 0.9 %unpacked.1 = (bf16[112,9216]{1,0:T(8,128)(2,1)S(1)}, bf16[48,9216]{1,0:T(8,128)(2,1)S(1)}) custom-call(bf16[104,1152]{1,0:T(8,128)(2,1)S(1)} %get-tuple-element.31.refs_0_, bf16[104,1152]{1,0:T(8,128)(2,1)S(1)} %get-tuple-element.33.refs_1_, bf16[104,1152]{1,0:T(8,128)(2,1)S(1)} %collective-permute-done.3.refs_2_, ...), custom_call_target="tpu_custom_call" | custom-call | flops 8000000000 | bytes 24000000 | tf_op jit(solution)/shard_map/unpacked/pallas_call | solution.py:185
  30.5 0.0 collective-permute-done.15.refs_3_
  30.5 0.0 copy-start.1
  30.5 0.5 %collective-permute-start.10 = (bf16[104,1152]{1,0:T(8,128)(2,1)S(1)}, bf16[104,1152]{1,0:T(8,128)(2,1)S(1)}, u32[]{:S(2)}, u32[]{:S(2)}) collective-permute-start(bf16[104,1152]{1,0:T(8,128)(2,1)S(1)} %get-tuple-element.40.refs_8_), channel_id=1, source_target_pairs={{0,4},{1,5},{2,6},{3,7},{4,0},{5,1},{6,2},{7,3},{8,12},{9,13},{10,... | collective-permute-start | bytes 718856 | tf_op jit(solution)/shard_map/ppermute | solution.py:318
  31.0 0.0 collective-permute-done.13.refs_0_
  31.0 1.2 %collective-permute-start.14 = (bf16[104,1152]{1,0:T(8,128)(2,1)S(1)}, bf16[104,1152]{1,0:T(8,128)(2,1)S(1)}, u32[]{:S(2)}, u32[]{:S(2)}) collective-permute-start(bf16[104,1152]{1,0:T(8,128)(2,1)S(1)} %collective-permute-done.13.refs_0_), channel_id=1, source_target_pairs={{0,16},{1,17},{2,18},{3,19},{4,20},{5,21},{6,22},{7,23},{8,24},{9,... | collective-permute-start | bytes 718856 | tf_op jit(solution)/shard_map/ppermute | solution.py:318
  32.2 0.0 copy-done.1
  32.2 5.9 %first_half.1 = (f32[128,192]{1,0:T(8,128)S(1)}, f32[128,192]{1,0:T(8,128)S(1)}, f32[128,192]{1,0:T(8,128)S(1)}, f32[128,192]{1,0:T(8,128)S(1)}, bf16[192,2048]{...) custom-call(s32[1]{0:T(128)} %bitcast.1.x_ref, ...), custom_call_target="tpu_custom_call" | custom-call | flops 12000000000 | bytes 36000000 | tf_op jit(solution)/shard_map/first_half/pallas_call | solution.py:223
  38.1 0.0 collective-permute-done.11.refs_2_
  38.1 0.0 collective-permute-done.12.refs_3_
  38.2 0.0 collective-permute-done.9.refs_0_
  38.2 1.2 %collective-permute-done.10.refs_1_ = bf16[104,1152]{1,0:T(8,128)(2,1)S(1)} collective-permute-done((bf16[104,1152]{1,0:T(8,128)(2,1)S(1)}, bf16[104,1152]{1,0:T(8,128)(2,1)S(1)}, u32[]{:S(2)}, u32[]{:S(2)}) %collective-permute-start.10) | collective-permute-done | bytes 239648 | tf_op jit(solution)/shard_map/ppermute | solution.py:318
  39.4 0.0 collective-permute-done.14.refs_4_
  39.4 1.6 %mate_scores.1 = (f32[16,192]{1,0:T(8,128)S(1)}, bf16[128,9216]{1,0:T(8,128)(2,1)S(1)}) custom-call(s32[1]{0:T(128)} %bitcast.me_ref, bf16[48,9216]{1,0:T(8,128)(2,1)S(1)} %get-tuple-element.42.rows_ref, bf16[104,1152]{1,0:T(8,128)(2,1)S(1)} %collective-permute-done.9.refs_0_, bf16[104,1152]{1,0:T(8,128)(2,1)S(1)} %collective-permute-done.10.refs_1_, ...), custom_call_target="tpu_custom_call" | custom-call | flops 5000000000 | bytes 15000000 | tf_op jit(solution)/shard_map/mate_scores/pallas_call | solution.py:278
  40.9 3.0 %collective-permute-start.16 = (f32[16,192]{1,0:T(8,128)S(1)}, f32[16,192]{1,0:T(8,128)S(1)}, u32[]{:S(2)}, u32[]{:S(2)}) collective-permute-start(f32[16,192]{1,0:T(8,128)S(1)} %get-tuple-element.49), channel_id=1, source_target_pairs={{0,1},{1,0},{2,3},{3,2},{4,5},{5,4},{6,7},{7,6},{8,9},{9,8},{10,11... | collective-permute-start | bytes 36872 | tf_op jit(solution)/shard_map/ppermute | solution.py:318
  43.9 1.3 %own_scores.1 = f32[16,192]{1,0:T(8,128)S(1)} custom-call(s32[1]{0:T(128)} %bitcast.me_ref, bf16[128,9216]{1,0:T(8,128)(2,1)S(1)} %get-tuple-element.50.rows, bf16[192,2048]{1,0:T(8,128)(2,1)S(1)} %get-tuple-element.51.refs_0_, bf16[192,7168]{1,0:T(8,128)(2,1)S(1)} %get-tuple-element.52.refs_1_, f32[128,192]{1,0:T(8,128)S(1)} %get-tuple-element.53.refs_2_, ...), custom_call_target="tpu_custom_call" | custom-call | flops 30000001024 | bytes 90000000 | tf_op jit(solution)/shard_map/own_scores/pallas_call | solution.py:294
  45.3 0.0 collective-permute-done.16
  45.3 0.6 %add.3 = f32[16,192]{1,0:T(8,128)} add(f32[16,192]{1,0:T(8,128)S(1)} %collective-permute-done.16, f32[16,192]{1,0:T(8,128)S(1)} %own_scores.1) | non-fusion elementwise | flops 3072 | bytes 36864 | tf_op jit(solution)/shard_map/add | solution.py:350
  (2 shorter events, 0.0 us)
Async XLA Ops:
  0.0 18.3 %collective-permute-start.2 = (bf16[192,14336]{1,0:T(8,128)(2,1)}, bf16[192,14336]{1,0:T(8,128)(2,1)}, u32[]{:S(2)}, u32[]{:S(2)}) collective-permute-start(bf16[192,14336]{1,0:T(8,128)(2,1)} %refs_2_.1), channel_id=1, source_target_pairs={{0,1},{1,0},{2,3},{3,2},{4,5},{5,4},{6,7},{7,6},{8,9},{9,8},{10,11... | collective-permute-start | bytes 16515080 | tf_op jit(solution)/shard_map/ppermute | solution.py:318
  1.5 9.3 %copy-start = (bf16[192,4096]{1,0:T(8,128)(2,1)S(1)}, bf16[192,4096]{1,0:T(8,128)(2,1)}, u32[]{:S(2)}) copy-start(bf16[192,4096]{1,0:T(8,128)(2,1)} %refs_1_.1) | copy-start | bytes 4718596
  1.8 8.9 %collective-permute-start = (bf16[104,1152]{1,0:T(8,128)(2,1)S(1)}, bf16[104,1152]{1,0:T(8,128)(2,1)S(1)}, u32[]{:S(2)}, u32[]{:S(2)}) collective-permute-start(bf16[104,1152]{1,0:T(8,128)(2,1)S(1)} %get-tuple-element.31.refs_0_), channel_id=1, source_target_pairs={{0,2},{1,3},{2,0},{3,1},{4,6},{5,7},{6,4},{7,5},{8,10},{9,11},{10,... | collective-permute-start | bytes 718856 | tf_op jit(solution)/shard_map/ppermute | solution.py:318
  4.5 9.2 %collective-permute-start.3 = (bf16[104,1152]{1,0:T(8,128)(2,1)S(1)}, bf16[104,1152]{1,0:T(8,128)(2,1)S(1)}, u32[]{:S(2)}, u32[]{:S(2)}) collective-permute-start(bf16[104,1152]{1,0:T(8,128)(2,1)S(1)} %get-tuple-element.34), channel_id=1, source_target_pairs={{0,12},{1,13},{2,14},{3,15},{4,8},{5,9},{6,10},{7,11},{8,4},{9,5},... | collective-permute-start | bytes 718856 | tf_op jit(solution)/shard_map/ppermute | solution.py:318
  7.9 10.2 %collective-permute-start.1 = (bf16[104,1152]{1,0:T(8,128)(2,1)S(1)}, bf16[104,1152]{1,0:T(8,128)(2,1)S(1)}, u32[]{:S(2)}, u32[]{:S(2)}) collective-permute-start(bf16[104,1152]{1,0:T(8,128)(2,1)S(1)} %get-tuple-element.32.refs_2_), channel_id=1, source_target_pairs={{0,2},{1,3},{2,0},{3,1},{4,6},{5,7},{6,4},{7,5},{8,10},{9,11},{10,... | collective-permute-start | bytes 718856 | tf_op jit(solution)/shard_map/ppermute | solution.py:318
  8.1 11.5 %collective-permute-start.7 = (bf16[104,1152]{1,0:T(8,128)(2,1)S(1)}, bf16[104,1152]{1,0:T(8,128)(2,1)S(1)}, u32[]{:S(2)}, u32[]{:S(2)}) collective-permute-start(bf16[104,1152]{1,0:T(8,128)(2,1)S(1)} %get-tuple-element.31.refs_0_), channel_id=1, source_target_pairs={{0,4},{1,5},{2,6},{3,7},{4,0},{5,1},{6,2},{7,3},{8,12},{9,13},{10,... | collective-permute-start | bytes 718856 | tf_op jit(solution)/shard_map/ppermute | solution.py:318
  10.7 19.8 %collective-permute-start.15 = (bf16[192,4096]{1,0:T(8,128)(2,1)S(1)}, bf16[192,4096]{1,0:T(8,128)(2,1)S(1)}, u32[]{:S(2)}, u32[]{:S(2)}) collective-permute-start(bf16[192,4096]{1,0:T(8,128)(2,1)S(1)} %copy-done), channel_id=1, source_target_pairs={{0,1},{1,0},{2,3},{3,2},{4,5},{5,4},{6,7},{7,6},{8,9},{9,8},{10,11... | collective-permute-start | bytes 4718600 | tf_op jit(solution)/shard_map/ppermute | solution.py:318
  13.7 9.7 %collective-permute-start.4 = (bf16[104,1152]{1,0:T(8,128)(2,1)S(1)}, bf16[104,1152]{1,0:T(8,128)(2,1)S(1)}, u32[]{:S(2)}, u32[]{:S(2)}) collective-permute-start(bf16[104,1152]{1,0:T(8,128)(2,1)S(1)} %collective-permute-done.3.refs_2_), channel_id=1, source_target_pairs={{0,4},{1,5},{2,6},{3,7},{4,0},{5,1},{6,2},{7,3},{8,12},{9,13},{10,... | collective-permute-start | bytes 718856 | tf_op jit(solution)/shard_map/ppermute | solution.py:318
  18.1 5.9 %collective-permute-start.5 = (bf16[104,1152]{1,0:T(8,128)(2,1)S(1)}, bf16[104,1152]{1,0:T(8,128)(2,1)S(1)}, u32[]{:S(2)}, u32[]{:S(2)}) collective-permute-start(bf16[104,1152]{1,0:T(8,128)(2,1)S(1)} %collective-permute-done.3.refs_2_), channel_id=1, source_target_pairs={{0,2},{1,3},{2,0},{3,1},{4,6},{5,7},{6,4},{7,5},{8,10},{9,11},{10,... | collective-permute-start | bytes 718856 | tf_op jit(solution)/shard_map/ppermute | solution.py:318
  18.3 5.7 %collective-permute-start.6 = (bf16[104,1152]{1,0:T(8,128)(2,1)S(1)}, bf16[104,1152]{1,0:T(8,128)(2,1)S(1)}, u32[]{:S(2)}, u32[]{:S(2)}) collective-permute-start(bf16[104,1152]{1,0:T(8,128)(2,1)S(1)} %collective-permute-done.3.refs_2_), channel_id=1, source_target_pairs={{0,16},{1,17},{2,18},{3,19},{4,20},{5,21},{6,22},{7,23},{8,24},{9,... | collective-permute-start | bytes 718856 | tf_op jit(solution)/shard_map/ppermute | solution.py:318
  19.5 9.0 %collective-permute-start.8 = (bf16[104,1152]{1,0:T(8,128)(2,1)S(1)}, bf16[104,1152]{1,0:T(8,128)(2,1)S(1)}, u32[]{:S(2)}, u32[]{:S(2)}) collective-permute-start(bf16[104,1152]{1,0:T(8,128)(2,1)S(1)} %get-tuple-element.33.refs_1_), channel_id=1, source_target_pairs={{0,4},{1,5},{2,6},{3,7},{4,0},{5,1},{6,2},{7,3},{8,12},{9,13},{10,... | collective-permute-start | bytes 718856 | tf_op jit(solution)/shard_map/ppermute | solution.py:318
  24.0 7.0 %collective-permute-start.13 = (bf16[104,1152]{1,0:T(8,128)(2,1)S(1)}, bf16[104,1152]{1,0:T(8,128)(2,1)S(1)}, u32[]{:S(2)}, u32[]{:S(2)}) collective-permute-start(bf16[104,1152]{1,0:T(8,128)(2,1)S(1)} %get-tuple-element.37.refs_5_), channel_id=1, source_target_pairs={{0,2},{1,3},{2,0},{3,1},{4,6},{5,7},{6,4},{7,5},{8,10},{9,11},{10,... | collective-permute-start | bytes 718856 | tf_op jit(solution)/shard_map/ppermute | solution.py:318
  25.2 12.9 %collective-permute-start.11 = (bf16[104,1152]{1,0:T(8,128)(2,1)S(1)}, bf16[104,1152]{1,0:T(8,128)(2,1)S(1)}, u32[]{:S(2)}, u32[]{:S(2)}) collective-permute-start(bf16[104,1152]{1,0:T(8,128)(2,1)S(1)} %get-tuple-element.37.refs_5_), channel_id=1, source_target_pairs={{0,16},{1,17},{2,18},{3,19},{4,20},{5,21},{6,22},{7,23},{8,24},{9,... | collective-permute-start | bytes 718856 | tf_op jit(solution)/shard_map/ppermute | solution.py:318
  26.4 11.7 %collective-permute-start.12 = (bf16[104,1152]{1,0:T(8,128)(2,1)S(1)}, bf16[104,1152]{1,0:T(8,128)(2,1)S(1)}, u32[]{:S(2)}, u32[]{:S(2)}) collective-permute-start(bf16[104,1152]{1,0:T(8,128)(2,1)S(1)} %get-tuple-element.41.refs_9_), channel_id=1, source_target_pairs={{0,2},{1,3},{2,0},{3,1},{4,6},{5,7},{6,4},{7,5},{8,10},{9,11},{10,... | collective-permute-start | bytes 718856 | tf_op jit(solution)/shard_map/ppermute | solution.py:318
  28.5 9.6 %collective-permute-start.9 = (bf16[104,1152]{1,0:T(8,128)(2,1)S(1)}, bf16[104,1152]{1,0:T(8,128)(2,1)S(1)}, u32[]{:S(2)}, u32[]{:S(2)}) collective-permute-start(bf16[104,1152]{1,0:T(8,128)(2,1)S(1)} %get-tuple-element.39.refs_7_), channel_id=1, source_target_pairs={{0,4},{1,5},{2,6},{3,7},{4,0},{5,1},{6,2},{7,3},{8,12},{9,13},{10,... | collective-permute-start | bytes 718856 | tf_op jit(solution)/shard_map/ppermute | solution.py:318
  30.5 1.7 %copy-start.1 = (bf16[192,4096]{1,0:T(8,128)(2,1)}, bf16[192,4096]{1,0:T(8,128)(2,1)S(1)}, u32[]{:S(2)}) copy-start(bf16[192,4096]{1,0:T(8,128)(2,1)S(1)} %collective-permute-done.15.refs_3_) | copy-start | bytes 4718596
  30.5 8.8 %collective-permute-start.10 = (bf16[104,1152]{1,0:T(8,128)(2,1)S(1)}, bf16[104,1152]{1,0:T(8,128)(2,1)S(1)}, u32[]{:S(2)}, u32[]{:S(2)}) collective-permute-start(bf16[104,1152]{1,0:T(8,128)(2,1)S(1)} %get-tuple-element.40.refs_8_), channel_id=1, source_target_pairs={{0,4},{1,5},{2,6},{3,7},{4,0},{5,1},{6,2},{7,3},{8,12},{9,13},{10,... | collective-permute-start | bytes 718856 | tf_op jit(solution)/shard_map/ppermute | solution.py:318
  31.0 8.4 %collective-permute-start.14 = (bf16[104,1152]{1,0:T(8,128)(2,1)S(1)}, bf16[104,1152]{1,0:T(8,128)(2,1)S(1)}, u32[]{:S(2)}, u32[]{:S(2)}) collective-permute-start(bf16[104,1152]{1,0:T(8,128)(2,1)S(1)} %collective-permute-done.13.refs_0_), channel_id=1, source_target_pairs={{0,16},{1,17},{2,18},{3,19},{4,20},{5,21},{6,22},{7,23},{8,24},{9,... | collective-permute-start | bytes 718856 | tf_op jit(solution)/shard_map/ppermute | solution.py:318
  40.9 4.3 %collective-permute-start.16 = (f32[16,192]{1,0:T(8,128)S(1)}, f32[16,192]{1,0:T(8,128)S(1)}, u32[]{:S(2)}, u32[]{:S(2)}) collective-permute-start(f32[16,192]{1,0:T(8,128)S(1)} %get-tuple-element.49), channel_id=1, source_target_pairs={{0,1},{1,0},{2,3},{3,2},{4,5},{5,4},{6,7},{7,6},{8,9},{9,8},{10,11... | collective-permute-start | bytes 36872 | tf_op jit(solution)/shard_map/ppermute | solution.py:318

commit v7 on v6

--- a/solution.py
+++ b/solution.py
@@ -14,7 +14,7 @@
 ROWS = 16
 CUTS = (1, 4)
 LIMIT = 16 << 20
-TICK = 8
+TICK = 3
 PACK = 30
 
 

time: 46 us -> 45.6 us (level)
  waiting for transfers between devices: 11.7 us -> 11.2 us
    ppermute x17, waiting for transfers between devices: 11.7 us -> 11.2 us  [permuted(): swap = lambda a, gx, bx: lax.ppermute(a, AXES, pairs(n_grp, n_blk, gx, bx))]
  transfers between devices with their start and end apart: 17 -> 17, of which waited for: 6 -> 6; matrix products, arithmetic and copies ran while one was open for 0% -> 0% of each run, Pallas kernels for 21% -> 22%
where the time goes in v7:
time: 45.6 us; the launch traced here: 45.5 us
  starting transfers between devices  22.1 us (48%)
  Pallas kernels  11.5 us (25%)
  waiting for transfers between devices  11.2 us (25%)
  other arithmetic  0.61 us (1%)
    ppermute x17, starting transfers between devices, permuted(): swap = lambda a, gx, bx: lax.ppermute(a, AXES, pairs(n_grp, n_blk, gx, bx))  22.1 us
    ppermute x17, waiting for transfers between devices, permuted(): swap = lambda a, gx, bx: lax.ppermute(a, AXES, pairs(n_grp, n_blk, gx, bx))  11.2 us
    pallas_call x1, Pallas kernels, first_half(): pl.pallas_call(functools.partial(first_kernel, now, len(pieces)), out_sha...  5.92 us
    pallas_call x1, Pallas kernels, mate_scores(): pl.pallas_call(functools.partial(mate_kernel, order, len(pieces)), out_sh...  1.59 us
    pallas_call x1, Pallas kernels, pack(): pl.pallas_call(pack_kernel, out_shape=(jax.ShapeDtypeStruct((n * RANK, wi...  1.39 us
    pallas_call x1, Pallas kernels, own_scores(): pl.pallas_call(functools.partial(own_kernel, order), out_shape=jax.ShapeD...  1.34 us
    pallas_call x1, Pallas kernels, unpacked(): pl.pallas_call(functools.partial(unpack_kernel, now, later, ew), out_shap...  0.92 us
  transfers between devices with their start and end apart: 17, of which 6 were waited for; matrix products, arithmetic and copies ran while one was open for 0% of the time, Pallas kernels for 22%

profile of v7, /device:TPU:1, one launch (start us, length us, event | category | flops | bytes accessed | tf_op | source)
XLA Modules:
  0.0 45.5 jit_solution(15587864772623535080)
XLA Ops:
  0.0 0.1 collective-permute-start.2
  0.1 0.5 collective-permute-start.15
  0.5 1.4 %pack.1 = (bf16[104,1152]{1,0:T(8,128)(2,1)S(1)}, bf16[2,128,1152]{2,1,0:T(8,128)(2,1)S(1)}) custom-call(s32[1]{0:T(128)} %bitcast.1.x_ref, bf16[1,13,4096]{2,1,0:T(8,128)(2,1)} %err_hbm.1, bf16[1,13,14336]{2,1,0:T(8,128)(2,1)} %act_hbm.1), custom_call_target="tpu_custom_call" | custom-call | tf_op jit(solution)/shard_map/pack/pallas_call | solution.py:68
  1.9 0.3 pack_again.1
  2.2 2.3 %collective-permute-start = (bf16[104,1152]{1,0:T(8,128)(2,1)S(1)}, bf16[104,1152]{1,0:T(8,128)(2,1)S(1)}, u32[]{:S(2)}, u32[]{:S(2)}) collective-permute-start(bf16[104,1152]{1,0:T(8,128)(2,1)S(1)} %get-tuple-element.31.refs_0_), channel_id=1, source_target_pairs={{0,2},{1,3},{2,0},{3,1},{4,6},{5,7},{6,4},{7,5},{8,10},{9,11},{10,... | collective-permute-start | bytes 718856 | tf_op jit(solution)/shard_map/ppermute | solution.py:318
  4.5 3.3 %collective-permute-start.3 = (bf16[104,1152]{1,0:T(8,128)(2,1)S(1)}, bf16[104,1152]{1,0:T(8,128)(2,1)S(1)}, u32[]{:S(2)}, u32[]{:S(2)}) collective-permute-start(bf16[104,1152]{1,0:T(8,128)(2,1)S(1)} %get-tuple-element.34), channel_id=1, source_target_pairs={{0,12},{1,13},{2,14},{3,15},{4,8},{5,9},{6,10},{7,11},{8,4},{9,5},... | collective-permute-start | bytes 718856 | tf_op jit(solution)/shard_map/ppermute | solution.py:318
  7.8 0.2 collective-permute-start.1
  8.1 2.2 %collective-permute-done.refs_0_ = bf16[104,1152]{1,0:T(8,128)(2,1)S(1)} collective-permute-done((bf16[104,1152]{1,0:T(8,128)(2,1)S(1)}, bf16[104,1152]{1,0:T(8,128)(2,1)S(1)}, u32[]{:S(2)}, u32[]{:S(2)}) %collective-permute-start) | collective-permute-done | bytes 239648 | tf_op jit(solution)/shard_map/ppermute | solution.py:318
  10.3 1.2 %collective-permute-start.7 = (bf16[104,1152]{1,0:T(8,128)(2,1)S(1)}, bf16[104,1152]{1,0:T(8,128)(2,1)S(1)}, u32[]{:S(2)}, u32[]{:S(2)}) collective-permute-start(bf16[104,1152]{1,0:T(8,128)(2,1)S(1)} %get-tuple-element.31.refs_0_), channel_id=1, source_target_pairs={{0,4},{1,5},{2,6},{3,7},{4,0},{5,1},{6,2},{7,3},{8,12},{9,13},{10,... | collective-permute-start | bytes 718856 | tf_op jit(solution)/shard_map/ppermute | solution.py:318
  11.5 1.6 %collective-permute-done.3.refs_2_ = bf16[104,1152]{1,0:T(8,128)(2,1)S(1)} collective-permute-done((bf16[104,1152]{1,0:T(8,128)(2,1)S(1)}, bf16[104,1152]{1,0:T(8,128)(2,1)S(1)}, u32[]{:S(2)}, u32[]{:S(2)}) %collective-permute-start.3) | collective-permute-done | bytes 239648 | tf_op jit(solution)/shard_map/ppermute | solution.py:318
  13.1 4.7 %collective-permute-start.4 = (bf16[104,1152]{1,0:T(8,128)(2,1)S(1)}, bf16[104,1152]{1,0:T(8,128)(2,1)S(1)}, u32[]{:S(2)}, u32[]{:S(2)}) collective-permute-start(bf16[104,1152]{1,0:T(8,128)(2,1)S(1)} %collective-permute-done.3.refs_2_), channel_id=1, source_target_pairs={{0,4},{1,5},{2,6},{3,7},{4,0},{5,1},{6,2},{7,3},{8,12},{9,13},{10,... | collective-permute-start | bytes 718856 | tf_op jit(solution)/shard_map/ppermute | solution.py:318
  17.8 0.0 collective-permute-done.1.refs_1_
  17.8 0.2 collective-permute-start.5
  18.0 0.0 collective-permute-done.2.refs_3_
  18.0 1.2 %collective-permute-start.6 = (bf16[104,1152]{1,0:T(8,128)(2,1)S(1)}, bf16[104,1152]{1,0:T(8,128)(2,1)S(1)}, u32[]{:S(2)}, u32[]{:S(2)}) collective-permute-start(bf16[104,1152]{1,0:T(8,128)(2,1)S(1)} %collective-permute-done.3.refs_2_), channel_id=1, source_target_pairs={{0,16},{1,17},{2,18},{3,19},{4,20},{5,21},{6,22},{7,23},{8,24},{9,... | collective-permute-start | bytes 718856 | tf_op jit(solution)/shard_map/ppermute | solution.py:318
  19.3 0.0 collective-permute-done.7.refs_4_
  19.3 0.4 collective-permute-start.8
  19.6 3.7 %collective-permute-done.4.refs_0_ = bf16[104,1152]{1,0:T(8,128)(2,1)S(1)} collective-permute-done((bf16[104,1152]{1,0:T(8,128)(2,1)S(1)}, bf16[104,1152]{1,0:T(8,128)(2,1)S(1)}, u32[]{:S(2)}, u32[]{:S(2)}) %collective-permute-start.4) | collective-permute-done | bytes 239648 | tf_op jit(solution)/shard_map/ppermute | solution.py:318
  23.4 0.1 collective-permute-done.5.refs_1_
  23.5 0.0 collective-permute-done.6.refs_2_
  23.5 1.2 %collective-permute-start.13 = (bf16[104,1152]{1,0:T(8,128)(2,1)S(1)}, bf16[104,1152]{1,0:T(8,128)(2,1)S(1)}, u32[]{:S(2)}, u32[]{:S(2)}) collective-permute-start(bf16[104,1152]{1,0:T(8,128)(2,1)S(1)} %get-tuple-element.37.refs_5_), channel_id=1, source_target_pairs={{0,2},{1,3},{2,0},{3,1},{4,6},{5,7},{6,4},{7,5},{8,10},{9,11},{10,... | collective-permute-start | bytes 718856 | tf_op jit(solution)/shard_map/ppermute | solution.py:318
  24.7 1.2 %collective-permute-start.11 = (bf16[104,1152]{1,0:T(8,128)(2,1)S(1)}, bf16[104,1152]{1,0:T(8,128)(2,1)S(1)}, u32[]{:S(2)}, u32[]{:S(2)}) collective-permute-start(bf16[104,1152]{1,0:T(8,128)(2,1)S(1)} %get-tuple-element.37.refs_5_), channel_id=1, source_target_pairs={{0,16},{1,17},{2,18},{3,19},{4,20},{5,21},{6,22},{7,23},{8,24},{9,... | collective-permute-start | bytes 718856 | tf_op jit(solution)/shard_map/ppermute | solution.py:318
  25.9 0.3 collective-permute-start.12
  26.2 2.3 %collective-permute-done.8.refs_4_ = bf16[104,1152]{1,0:T(8,128)(2,1)S(1)} collective-permute-done((bf16[104,1152]{1,0:T(8,128)(2,1)S(1)}, bf16[104,1152]{1,0:T(8,128)(2,1)S(1)}, u32[]{:S(2)}, u32[]{:S(2)}) %collective-permute-start.8) | collective-permute-done | bytes 239648 | tf_op jit(solution)/shard_map/ppermute | solution.py:318
  28.5 1.1 %collective-permute-start.9 = (bf16[104,1152]{1,0:T(8,128)(2,1)S(1)}, bf16[104,1152]{1,0:T(8,128)(2,1)S(1)}, u32[]{:S(2)}, u32[]{:S(2)}) collective-permute-start(bf16[104,1152]{1,0:T(8,128)(2,1)S(1)} %get-tuple-element.39.refs_7_), channel_id=1, source_target_pairs={{0,4},{1,5},{2,6},{3,7},{4,0},{5,1},{6,2},{7,3},{8,12},{9,13},{10,... | collective-permute-start | bytes 718856 | tf_op jit(solution)/shard_map/ppermute | solution.py:318
  29.6 0.9 %unpacked.1 = (bf16[112,9216]{1,0:T(8,128)(2,1)S(1)}, bf16[48,9216]{1,0:T(8,128)(2,1)S(1)}) custom-call(bf16[104,1152]{1,0:T(8,128)(2,1)S(1)} %get-tuple-element.31.refs_0_, bf16[104,1152]{1,0:T(8,128)(2,1)S(1)} %get-tuple-element.33.refs_1_, bf16[104,1152]{1,0:T(8,128)(2,1)S(1)} %collective-permute-done.3.refs_2_, ...), custom_call_target="tpu_custom_call" | custom-call | flops 3000000000 | bytes 9000000 | tf_op jit(solution)/shard_map/unpacked/pallas_call | solution.py:185
  30.5 0.0 collective-permute-done.15.refs_3_
  30.5 0.0 copy-start
  30.5 0.5 collective-permute-start.10
  31.0 0.0 collective-permute-done.13.refs_0_
  31.0 1.2 %collective-permute-start.14 = (bf16[104,1152]{1,0:T(8,128)(2,1)S(1)}, bf16[104,1152]{1,0:T(8,128)(2,1)S(1)}, u32[]{:S(2)}, u32[]{:S(2)}) collective-permute-start(bf16[104,1152]{1,0:T(8,128)(2,1)S(1)} %collective-permute-done.13.refs_0_), channel_id=1, source_target_pairs={{0,16},{1,17},{2,18},{3,19},{4,20},{5,21},{6,22},{7,23},{8,24},{9,... | collective-permute-start | bytes 718856 | tf_op jit(solution)/shard_map/ppermute | solution.py:318
  32.2 0.0 copy-done
  32.2 5.9 %first_half.1 = (f32[128,192]{1,0:T(8,128)S(1)}, f32[128,192]{1,0:T(8,128)S(1)}, f32[128,192]{1,0:T(8,128)S(1)}, f32[128,192]{1,0:T(8,128)S(1)}, bf16[192,2048]{...) custom-call(s32[1]{0:T(128)} %bitcast.1.x_ref, ...), custom_call_target="tpu_custom_call" | custom-call | flops 12000000000 | bytes 36000000 | tf_op jit(solution)/shard_map/first_half/pallas_call | solution.py:223
  38.1 0.0 collective-permute-done.11.refs_2_
  38.1 0.0 collective-permute-done.12.refs_3_
  38.1 0.0 collective-permute-done.9.refs_0_
  38.1 1.2 %collective-permute-done.10.refs_1_ = bf16[104,1152]{1,0:T(8,128)(2,1)S(1)} collective-permute-done((bf16[104,1152]{1,0:T(8,128)(2,1)S(1)}, bf16[104,1152]{1,0:T(8,128)(2,1)S(1)}, u32[]{:S(2)}, u32[]{:S(2)}) %collective-permute-start.10) | collective-permute-done | bytes 239648 | tf_op jit(solution)/shard_map/ppermute | solution.py:318
  39.3 0.0 collective-permute-done.14.refs_4_
  39.3 1.6 %mate_scores.1 = (f32[16,192]{1,0:T(8,128)S(1)}, bf16[128,9216]{1,0:T(8,128)(2,1)S(1)}) custom-call(s32[1]{0:T(128)} %bitcast.me_ref, bf16[48,9216]{1,0:T(8,128)(2,1)S(1)} %get-tuple-element.42.rows_ref, bf16[104,1152]{1,0:T(8,128)(2,1)S(1)} %collective-permute-done.9.refs_0_, bf16[104,1152]{1,0:T(8,128)(2,1)S(1)} %collective-permute-done.10.refs_1_, ...), custom_call_target="tpu_custom_call" | custom-call | flops 5000000000 | bytes 15000000 | tf_op jit(solution)/shard_map/mate_scores/pallas_call | solution.py:278
  40.9 2.6 %collective-permute-start.16 = (f32[16,192]{1,0:T(8,128)S(1)}, f32[16,192]{1,0:T(8,128)S(1)}, u32[]{:S(2)}, u32[]{:S(2)}) collective-permute-start(f32[16,192]{1,0:T(8,128)S(1)} %get-tuple-element.49), channel_id=1, source_target_pairs={{0,1},{1,0},{2,3},{3,2},{4,5},{5,4},{6,7},{7,6},{8,9},{9,8},{10,11... | collective-permute-start | bytes 36872 | tf_op jit(solution)/shard_map/ppermute | solution.py:318
  43.5 1.3 %own_scores.1 = f32[16,192]{1,0:T(8,128)S(1)} custom-call(s32[1]{0:T(128)} %bitcast.me_ref, bf16[128,9216]{1,0:T(8,128)(2,1)S(1)} %get-tuple-element.50.rows, bf16[192,2048]{1,0:T(8,128)(2,1)S(1)} %get-tuple-element.51.refs_0_, bf16[192,7168]{1,0:T(8,128)(2,1)S(1)} %get-tuple-element.52.refs_1_, f32[128,192]{1,0:T(8,128)S(1)} %get-tuple-element.53.refs_2_, ...), custom_call_target="tpu_custom_call" | custom-call | flops 30000001024 | bytes 90000000 | tf_op jit(solution)/shard_map/own_scores/pallas_call | solution.py:294
  44.9 0.0 collective-permute-done.16
  44.9 0.6 %add.3 = f32[16,192]{1,0:T(8,128)} add(f32[16,192]{1,0:T(8,128)S(1)} %collective-permute-done.16, f32[16,192]{1,0:T(8,128)S(1)} %own_scores.1) | non-fusion elementwise | flops 3072 | bytes 36864 | tf_op jit(solution)/shard_map/add | solution.py:350
  (2 shorter events, 0.0 us)
Async XLA Ops:
  0.0 18.0 %collective-permute-start.2 = (bf16[192,14336]{1,0:T(8,128)(2,1)}, bf16[192,14336]{1,0:T(8,128)(2,1)}, u32[]{:S(2)}, u32[]{:S(2)}) collective-permute-start(bf16[192,14336]{1,0:T(8,128)(2,1)} %refs_2_.1), channel_id=1, source_target_pairs={{0,1},{1,0},{2,3},{3,2},{4,5},{5,4},{6,7},{7,6},{8,9},{9,8},{10,11... | collective-permute-start | bytes 16515080 | tf_op jit(solution)/shard_map/ppermute | solution.py:318
  0.1 30.5 %collective-permute-start.15 = (bf16[192,4096]{1,0:T(8,128)(2,1)}, bf16[192,4096]{1,0:T(8,128)(2,1)S(1)}, u32[]{:S(2)}, u32[]{:S(2)}) collective-permute-start(bf16[192,4096]{1,0:T(8,128)(2,1)} %refs_1_.1), channel_id=1, source_target_pairs={{0,1},{1,0},{2,3},{3,2},{4,5},{5,4},{6,7},{7,6},{8,9},{9,8},{10,11... | collective-permute-start | bytes 4718600 | tf_op jit(solution)/shard_map/ppermute | solution.py:318
  2.2 8.1 %collective-permute-start = (bf16[104,1152]{1,0:T(8,128)(2,1)S(1)}, bf16[104,1152]{1,0:T(8,128)(2,1)S(1)}, u32[]{:S(2)}, u32[]{:S(2)}) collective-permute-start(bf16[104,1152]{1,0:T(8,128)(2,1)S(1)} %get-tuple-element.31.refs_0_), channel_id=1, source_target_pairs={{0,2},{1,3},{2,0},{3,1},{4,6},{5,7},{6,4},{7,5},{8,10},{9,11},{10,... | collective-permute-start | bytes 718856 | tf_op jit(solution)/shard_map/ppermute | solution.py:318
  4.5 8.6 %collective-permute-start.3 = (bf16[104,1152]{1,0:T(8,128)(2,1)S(1)}, bf16[104,1152]{1,0:T(8,128)(2,1)S(1)}, u32[]{:S(2)}, u32[]{:S(2)}) collective-permute-start(bf16[104,1152]{1,0:T(8,128)(2,1)S(1)} %get-tuple-element.34), channel_id=1, source_target_pairs={{0,12},{1,13},{2,14},{3,15},{4,8},{5,9},{6,10},{7,11},{8,4},{9,5},... | collective-permute-start | bytes 718856 | tf_op jit(solution)/shard_map/ppermute | solution.py:318
  7.8 10.0 %collective-permute-start.1 = (bf16[104,1152]{1,0:T(8,128)(2,1)S(1)}, bf16[104,1152]{1,0:T(8,128)(2,1)S(1)}, u32[]{:S(2)}, u32[]{:S(2)}) collective-permute-start(bf16[104,1152]{1,0:T(8,128)(2,1)S(1)} %get-tuple-element.32.refs_2_), channel_id=1, source_target_pairs={{0,2},{1,3},{2,0},{3,1},{4,6},{5,7},{6,4},{7,5},{8,10},{9,11},{10,... | collective-permute-start | bytes 718856 | tf_op jit(solution)/shard_map/ppermute | solution.py:318
  10.3 9.0 %collective-permute-start.7 = (bf16[104,1152]{1,0:T(8,128)(2,1)S(1)}, bf16[104,1152]{1,0:T(8,128)(2,1)S(1)}, u32[]{:S(2)}, u32[]{:S(2)}) collective-permute-start(bf16[104,1152]{1,0:T(8,128)(2,1)S(1)} %get-tuple-element.31.refs_0_), channel_id=1, source_target_pairs={{0,4},{1,5},{2,6},{3,7},{4,0},{5,1},{6,2},{7,3},{8,12},{9,13},{10,... | collective-permute-start | bytes 718856 | tf_op jit(solution)/shard_map/ppermute | solution.py:318
  13.1 10.3 %collective-permute-start.4 = (bf16[104,1152]{1,0:T(8,128)(2,1)S(1)}, bf16[104,1152]{1,0:T(8,128)(2,1)S(1)}, u32[]{:S(2)}, u32[]{:S(2)}) collective-permute-start(bf16[104,1152]{1,0:T(8,128)(2,1)S(1)} %collective-permute-done.3.refs_2_), channel_id=1, source_target_pairs={{0,4},{1,5},{2,6},{3,7},{4,0},{5,1},{6,2},{7,3},{8,12},{9,13},{10,... | collective-permute-start | bytes 718856 | tf_op jit(solution)/shard_map/ppermute | solution.py:318
  17.8 5.7 %collective-permute-start.5 = (bf16[104,1152]{1,0:T(8,128)(2,1)S(1)}, bf16[104,1152]{1,0:T(8,128)(2,1)S(1)}, u32[]{:S(2)}, u32[]{:S(2)}) collective-permute-start(bf16[104,1152]{1,0:T(8,128)(2,1)S(1)} %collective-permute-done.3.refs_2_), channel_id=1, source_target_pairs={{0,2},{1,3},{2,0},{3,1},{4,6},{5,7},{6,4},{7,5},{8,10},{9,11},{10,... | collective-permute-start | bytes 718856 | tf_op jit(solution)/shard_map/ppermute | solution.py:318
  18.0 5.4 %collective-permute-start.6 = (bf16[104,1152]{1,0:T(8,128)(2,1)S(1)}, bf16[104,1152]{1,0:T(8,128)(2,1)S(1)}, u32[]{:S(2)}, u32[]{:S(2)}) collective-permute-start(bf16[104,1152]{1,0:T(8,128)(2,1)S(1)} %collective-permute-done.3.refs_2_), channel_id=1, source_target_pairs={{0,16},{1,17},{2,18},{3,19},{4,20},{5,21},{6,22},{7,23},{8,24},{9,... | collective-permute-start | bytes 718856 | tf_op jit(solution)/shard_map/ppermute | solution.py:318
  19.3 9.2 %collective-permute-start.8 = (bf16[104,1152]{1,0:T(8,128)(2,1)S(1)}, bf16[104,1152]{1,0:T(8,128)(2,1)S(1)}, u32[]{:S(2)}, u32[]{:S(2)}) collective-permute-start(bf16[104,1152]{1,0:T(8,128)(2,1)S(1)} %get-tuple-element.33.refs_1_), channel_id=1, source_target_pairs={{0,4},{1,5},{2,6},{3,7},{4,0},{5,1},{6,2},{7,3},{8,12},{9,13},{10,... | collective-permute-start | bytes 718856 | tf_op jit(solution)/shard_map/ppermute | solution.py:318
  23.5 7.5 %collective-permute-start.13 = (bf16[104,1152]{1,0:T(8,128)(2,1)S(1)}, bf16[104,1152]{1,0:T(8,128)(2,1)S(1)}, u32[]{:S(2)}, u32[]{:S(2)}) collective-permute-start(bf16[104,1152]{1,0:T(8,128)(2,1)S(1)} %get-tuple-element.37.refs_5_), channel_id=1, source_target_pairs={{0,2},{1,3},{2,0},{3,1},{4,6},{5,7},{6,4},{7,5},{8,10},{9,11},{10,... | collective-permute-start | bytes 718856 | tf_op jit(solution)/shard_map/ppermute | solution.py:318
  24.7 13.4 %collective-permute-start.11 = (bf16[104,1152]{1,0:T(8,128)(2,1)S(1)}, bf16[104,1152]{1,0:T(8,128)(2,1)S(1)}, u32[]{:S(2)}, u32[]{:S(2)}) collective-permute-start(bf16[104,1152]{1,0:T(8,128)(2,1)S(1)} %get-tuple-element.37.refs_5_), channel_id=1, source_target_pairs={{0,16},{1,17},{2,18},{3,19},{4,20},{5,21},{6,22},{7,23},{8,24},{9,... | collective-permute-start | bytes 718856 | tf_op jit(solution)/shard_map/ppermute | solution.py:318
  25.9 12.2 %collective-permute-start.12 = (bf16[104,1152]{1,0:T(8,128)(2,1)S(1)}, bf16[104,1152]{1,0:T(8,128)(2,1)S(1)}, u32[]{:S(2)}, u32[]{:S(2)}) collective-permute-start(bf16[104,1152]{1,0:T(8,128)(2,1)S(1)} %get-tuple-element.41.refs_9_), channel_id=1, source_target_pairs={{0,2},{1,3},{2,0},{3,1},{4,6},{5,7},{6,4},{7,5},{8,10},{9,11},{10,... | collective-permute-start | bytes 718856 | tf_op jit(solution)/shard_map/ppermute | solution.py:318
  28.5 9.6 %collective-permute-start.9 = (bf16[104,1152]{1,0:T(8,128)(2,1)S(1)}, bf16[104,1152]{1,0:T(8,128)(2,1)S(1)}, u32[]{:S(2)}, u32[]{:S(2)}) collective-permute-start(bf16[104,1152]{1,0:T(8,128)(2,1)S(1)} %get-tuple-element.39.refs_7_), channel_id=1, source_target_pairs={{0,4},{1,5},{2,6},{3,7},{4,0},{5,1},{6,2},{7,3},{8,12},{9,13},{10,... | collective-permute-start | bytes 718856 | tf_op jit(solution)/shard_map/ppermute | solution.py:318
  30.5 1.7 %copy-start = (bf16[192,4096]{1,0:T(8,128)(2,1)}, bf16[192,4096]{1,0:T(8,128)(2,1)S(1)}, u32[]{:S(2)}) copy-start(bf16[192,4096]{1,0:T(8,128)(2,1)S(1)} %collective-permute-done.15.refs_3_) | copy-start | bytes 4718596
  30.5 8.8 %collective-permute-start.10 = (bf16[104,1152]{1,0:T(8,128)(2,1)S(1)}, bf16[104,1152]{1,0:T(8,128)(2,1)S(1)}, u32[]{:S(2)}, u32[]{:S(2)}) collective-permute-start(bf16[104,1152]{1,0:T(8,128)(2,1)S(1)} %get-tuple-element.40.refs_8_), channel_id=1, source_target_pairs={{0,4},{1,5},{2,6},{3,7},{4,0},{5,1},{6,2},{7,3},{8,12},{9,13},{10,... | collective-permute-start | bytes 718856 | tf_op jit(solution)/shard_map/ppermute | solution.py:318
  31.0 8.4 %collective-permute-start.14 = (bf16[104,1152]{1,0:T(8,128)(2,1)S(1)}, bf16[104,1152]{1,0:T(8,128)(2,1)S(1)}, u32[]{:S(2)}, u32[]{:S(2)}) collective-permute-start(bf16[104,1152]{1,0:T(8,128)(2,1)S(1)} %collective-permute-done.13.refs_0_), channel_id=1, source_target_pairs={{0,16},{1,17},{2,18},{3,19},{4,20},{5,21},{6,22},{7,23},{8,24},{9,... | collective-permute-start | bytes 718856 | tf_op jit(solution)/shard_map/ppermute | solution.py:318
  40.9 3.9 %collective-permute-start.16 = (f32[16,192]{1,0:T(8,128)S(1)}, f32[16,192]{1,0:T(8,128)S(1)}, u32[]{:S(2)}, u32[]{:S(2)}) collective-permute-start(f32[16,192]{1,0:T(8,128)S(1)} %get-tuple-element.49), channel_id=1, source_target_pairs={{0,1},{1,0},{2,3},{3,2},{4,5},{5,4},{6,7},{7,6},{8,9},{9,8},{10,11... | collective-permute-start | bytes 36872 | tf_op jit(solution)/shard_map/ppermute | solution.py:318
